TPU v7x, 32 devices: a whole 2x2x4 slice. The times are simulated.
32 devices in a mesh: ray: 8 (over z, y), pix: 4 (over x, core).
Axes of the slice: x: 2, y: 2, z: 4, core: 2. Of those that a mesh axis runs over, the one named last changes fastest.
Arguments:
- positions: float32 [2, 8192], P(None, 'ray'), may hold values from -2 to 2
- directions: float32 [2, 8192], P(None, 'ray'), may hold values from -0.35 to 0.35
- path: float32 [8192], P('ray'), may hold values from -9 to 9
- amplitude: float32 [8192], P('ray'), may hold values from 0.3 to 3
- psf_grad: float32 [3, 1024, 1024], P(None, 'pix', 'ray'), may hold values from -0.3 to 0.3
Outputs:
- psf: float32 [3, 1024, 1024], P(None, 'pix', 'ray')
- ray_grad: float32 [6, 8192], P(None, 'ray')
All inputs are finite; a program needn't handle non-finite values.
Results may differ from a plain program's by a relative error of at most 0.0054.
Values may be sent and summed in bfloat16 or wider, within the bound.
No kernel may reach another device: no remote copies, remote signals or barrier semaphores. Data moves between devices by JAX's collectives and lax.ppermute only.
A program may use at most 192 MiB of HBM per device.

v0:
```python
import math

import jax
import jax.numpy as jnp
from jax import lax
from jax.sharding import PartitionSpec as P

NPIX = 1024


wave_scales = (1.2088, 1.0, 0.8953)
two_pi = 2.0 * math.pi


def centred(start, count):
    return (start + jnp.arange(count)).astype(jnp.float32) - 0.5 * NPIX + 0.5


def build_tables(rays, rows_x, cols_y, norm):
    row_list = []
    col_list = []
    weight = (rays[5] * norm)[:, None]
    for wave in range(3):
        scale = wave_scales[wave]
        angle = scale * (
            rays[4][:, None]
            + two_pi
            * (
                rays[2][:, None] * (rows_x[None, :] - rays[0][:, None])
                - rays[3][:, None] * rays[1][:, None]
            )
        )
        row_list.append(jnp.stack([weight * jnp.cos(angle), weight * jnp.sin(angle)]))
        beta = scale * two_pi * cols_y[:, None] * rays[3][None, :]
        col_list.append(jnp.stack([jnp.cos(beta), jnp.sin(beta)]))
    return (jnp.stack(row_list), jnp.stack(col_list))


def mixing(a_re, a_im):
    upper = jnp.concatenate([a_re, a_im], axis=1)
    lower = jnp.concatenate([-a_im, a_re], axis=1)
    return jnp.concatenate([upper, lower], axis=0).astype(jnp.bfloat16)


def product(left, right, dims):
    return lax.dot_general(left, right, dims, preferred_element_type=jnp.float32)


def block_count(count):
    return max(1, min(16, count // 256))


def field_terms(row_tab, col_tab):
    count = row_tab.shape[2]
    nblk = block_count(count)
    blk = count // nblk

    def step(index, total):
        a_blk = lax.dynamic_slice_in_dim(row_tab, index * blk, blk, 2)
        b_blk = lax.dynamic_slice_in_dim(col_tab, index * blk, blk, 3)
        parts = []
        for wave in range(3):
            left = jnp.concatenate([b_blk[wave, 0], b_blk[wave, 1]], axis=1).astype(jnp.bfloat16)
            parts.append(
                product(left, mixing(a_blk[wave, 0], a_blk[wave, 1]), (((1,), (0,)), ((), ())))
            )
        return total + jnp.concatenate(parts, axis=1)

    init = jnp.zeros((col_tab.shape[2], 6 * row_tab.shape[3]), jnp.float32)
    return lax.fori_loop(0, nblk, step, init)


def ray_partials(row_tab, col_tab, rows_x, cols_y, cotangent):
    count = row_tab.shape[2]
    nblk = block_count(count)
    blk = count // nblk
    plen = rows_x.shape[0]

    def one_block(index):
        a_blk = lax.dynamic_slice_in_dim(row_tab, index * blk, blk, 2)
        b_blk = lax.dynamic_slice_in_dim(col_tab, index * blk, blk, 3)
        first = jnp.zeros((blk,), jnp.float32)
        second = jnp.zeros((blk,), jnp.float32)
        third = jnp.zeros((blk,), jnp.float32)
        fourth = jnp.zeros((blk,), jnp.float32)
        for wave in range(3):
            scale = wave_scales[wave]
            a_re = a_blk[wave, 0]
            a_im = a_blk[wave, 1]
            b_re = b_blk[wave, 0]
            b_im = b_blk[wave, 1]
            left = jnp.concatenate([b_re, b_im], axis=1).astype(jnp.bfloat16)
            mix = mixing(a_re, a_im)
            grad_u = cotangent[:, 2 * plen * wave : 2 * plen * (wave + 1)]
            proj = product(left, grad_u, (((0,), (0,)), ((), ())))
            d_are = proj[:blk, :plen] + proj[blk:, plen:]
            d_aim = proj[:blk, plen:] - proj[blk:, :plen]
            d_b = product(grad_u, mix, (((1,), (1,)), ((), ())))
            d_beta = d_b[:, blk:] * b_re - d_b[:, :blk] * b_im
            d_alpha = d_aim * a_re - d_are * a_im
            first = first + scale * jnp.sum(d_alpha, axis=1)
            second = second + scale * two_pi * jnp.sum(d_alpha * rows_x[None, :], axis=1)
            third = third + scale * two_pi * jnp.sum(d_beta * cols_y[:, None], axis=0)
            fourth = fourth + jnp.sum(d_are * a_re + d_aim * a_im, axis=1)
        return jnp.stack([first, second, third, fourth])

    out = lax.map(one_block, jnp.arange(nblk))
    return jnp.transpose(out, (1, 0, 2)).reshape(4, count)


def finish(sums, rays):
    return jnp.stack(
        [
            sums[0],
            -two_pi * rays[2] * sums[0],
            -two_pi * rays[3] * sums[0],
            (sums[1] - two_pi * rays[0] * sums[0]) / NPIX,
            (sums[2] - two_pi * rays[1] * sums[0]) / NPIX,
            sums[3] / rays[5],
        ]
    )


def intensity(field, psf_grad, clen, plen):
    shaped = field.reshape(clen, 3, 2, plen)
    psf = jnp.transpose(shaped[:, :, 0] ** 2 + shaped[:, :, 1] ** 2, (1, 2, 0))
    weight = jnp.transpose(psf_grad, (2, 0, 1))
    grad_u = (2.0 * weight[:, :, None, :] * shaped).reshape(clen, 6 * plen).astype(jnp.bfloat16)
    return (psf, grad_u)


def on_device(positions, directions, path, amplitude, psf_grad):
    rays = jnp.concatenate([positions, directions, path[None], amplitude[None]], axis=0)
    local = rays.shape[1]
    plen = NPIX // lax.axis_size("pix")
    clen = NPIX // lax.axis_size("ray")
    norm = 1.0 / math.sqrt(local * lax.axis_size("ray"))
    rows_x = centred(lax.axis_index("pix") * plen, plen)
    all_cols = centred(0, NPIX)
    row_tab, col_tab = build_tables(rays, rows_x, all_cols, norm)
    field = lax.psum_scatter(field_terms(row_tab, col_tab), "ray", scatter_dimension=0, tiled=True)
    psf, grad_u = intensity(field, psf_grad, clen, plen)
    gathered = lax.all_gather(grad_u, "ray", axis=0, tiled=True)
    partial_value = ray_partials(row_tab, col_tab, rows_x, all_cols, gathered)
    sums = lax.psum(partial_value, "pix")
    return (psf, finish(sums, rays))


def solution(mesh):
    in_specs = (P(None, "ray"), P(None, "ray"), P("ray"), P("ray"), P(None, "pix", "ray"))
    out_specs = (P(None, "pix", "ray"), P(None, "ray"))
    return jax.shard_map(
        on_device, mesh=mesh, in_specs=in_specs, out_specs=out_specs, check_vma=False
    )
```

profile of v0, /device:TPU:0, one launch (start us, length us, event | category | flops | bytes accessed | tf_op | source)
XLA Modules:
  0.0 587.4 jit_solution(12088630044009121379)
XLA Ops:
  9.5 14.5 %cosine_multiply_fusion.2 = (f32[1,1024,256]{2,1,0:T(8,128)S(1)}, f32[1,1024,256]{2,1,0:T(8,128)S(1)}, f32[1,1024,256]{2,1,0:T(8,128)}, f32[1,1024,256]{2,1,0:T(...) fusion(f32[1024]{0:T(1024)S(1)} %mul.582, f32[1024]{0:T(1024)S(1)} %bitcast.218, ...), kind=kLoop, calls=%fused_computation.214 | loop fusion | flops 3407872 | bytes 6312960 | tf_op jit(solution)/shard_map/mul | solution.py:33
  25.5 46.3 %multiply_cosine_fusion.2 = (f32[1,1024,1024]{2,1,0:T(8,128)S(1)}, f32[1,1024,1024]{2,1,0:T(8,128)}, f32[1,1024,1024]{2,1,0:T(8,128)}, f32[1,1024,1024]{2,1,0:T(...) fusion(f32[1024]{0:T(1024)S(1)} %bitcast.216, f32[1024]{0:T(1024)S(1)} %fusion.125, ...), kind=kLoop, calls=%fused_computation.205 | loop fusion | flops 3145728 | bytes 25182208 | tf_op jit(solution)/shard_map/cos | solution.py:35
  73.5 2.3 maximum_bitcast_fusion.4
  76.0 3.0 pad_maximum_fusion.1
  79.0 7.7 %maximum_bitcast_fusion.1 = (f32[1,2,1024,1024]{3,2,1,0:T(8,128)S(1)}, f32[1,2,1024,1024]{3,2,1,0:T(8,128)}) fusion(f32[1,1024,1024]{2,1,0:T(8,128)} %get-tuple-element.304, f32[1,1024,1024]{2,1,0:T(8,128)S(1)} %get-tuple-element.303, f32[1,1024,1024]{2,1,0:T(8,128)} %get-tuple-element.309, f32[1,1024,1024]{2,1,0:T(8,128)} %get-tuple-element.310), kind=kLoop, calls=%fused_computation.196 | loop fusion | flops 4194304 | bytes 33554432 | tf_op jit(solution)/shard_map/stack | solution.py:36
  86.7 15.7 %fusion.129 = (bf16[3,2,1024,1024]{3,2,1,0:T(8,128)(2,1)}, f32[3,2,1024,1024]{3,2,1,0:T(8,128)}) fusion(f32[1,2,1024,1024]{3,2,1,0:T(8,128)S(1)} %maximum_bitcast_fusion.3, f32[1,2,1024,1024]{3,2,1,0:T(8,128)} %get-tuple-element.314, f32[1,2,1024,1024]{3,2,1,0:T(8,128)S(1)} %get-tuple-element.313), kind=kLoop, calls=%fused_computation.240 | loop fusion | flops 18874368 | bytes 62914560
  102.4 64.4 %while.27 = (s32[]{:T(128)}, f32[1024,1536]{0,1:T(8,128)}, bf16[3,2,1024,1024]{3,2,1,0:T(8,128)(2,1)}, f32[3,2,1024,256]{3,2,1,0:T(8,128)}, s32[]{:T(128)}, /*index=5*/s32[]{:T(128)}, s32[]{:T(128)}, s32[]{:T(128)}, s32[]{}, s32[]{}) while((s32[]{:T(128)}, f32[1024,1536]{0,1:T(8,128)}, bf16[3,2,1024,1024]{3,2,1,0:T(8,128)(2,1)}, ...), condition=%wide.region_1.0_spmd.clone, body=%wide.region_0.0_spmd.clone.sunk | while | flops 1629880320 | bytes 44826832 | solution.py:70
  112.3 5.0 maximum_add_fusion.2
  127.2 6.6 %maximum_add_fusion.2 = f32[1024,1536]{0,1:T(8,128)} fusion(f32[1024,512]{0,1:T(8,128)} %fusion.193, f32[1024,512]{0,1:T(8,128)} %fusion.194, f32[1024,512]{0,1:T(8,128)S(1)} %fusion.195, f32[1024,1536]{0,1:T(8,128)} %get-tuple-element.510, pred[]{:T(512)S(6)} %compare.3), kind=kLoop, calls=%fused_computation.133.clone.1 | loop fusion | flops 6291456 | bytes 18874368 | tf_op jit(solution)/shard_map/while/body/eval_jaxpr/add | solution.py:67
  143.7 6.6 %maximum_add_fusion.2 = f32[1024,1536]{0,1:T(8,128)} fusion(f32[1024,512]{0,1:T(8,128)} %fusion.193, f32[1024,512]{0,1:T(8,128)} %fusion.194, f32[1024,512]{0,1:T(8,128)S(1)} %fusion.195, f32[1024,1536]{0,1:T(8,128)} %get-tuple-element.510, pred[]{:T(512)S(6)} %compare.3), kind=kLoop, calls=%fused_computation.133.clone.1 | loop fusion | flops 6291456 | bytes 18874368 | tf_op jit(solution)/shard_map/while/body/eval_jaxpr/add | solution.py:67
  160.2 6.6 %maximum_add_fusion.2 = f32[1024,1536]{0,1:T(8,128)} fusion(f32[1024,512]{0,1:T(8,128)} %fusion.193, f32[1024,512]{0,1:T(8,128)} %fusion.194, f32[1024,512]{0,1:T(8,128)S(1)} %fusion.195, f32[1024,1536]{0,1:T(8,128)} %get-tuple-element.510, pred[]{:T(512)S(6)} %compare.3), kind=kLoop, calls=%fused_computation.133.clone.1 | loop fusion | flops 6291456 | bytes 18874368 | tf_op jit(solution)/shard_map/while/body/eval_jaxpr/add | solution.py:67
  167.8 120.2 %reduce-scatter.2.cloned.1.call-done = f32[128,1536]{0,1:T(8,128)} async-done(((f32[1024,1536]{0,1:T(8,128)}), f32[128,1536]{0,1:T(8,128)}) %reduce-scatter.2.cloned.1.call-update) | async-done | bytes 786448 | tf_op jit(solution)/shard_map/reduce_scatter | solution.py:141
  291.9 60.4 %all-gather.2.cloned.1.call-done = bf16[1024,1536]{0,1:T(8,128)(2,1)} async-done(((bf16[128,1536]{0,1:T(8,128)(2,1)}), bf16[1024,1536]{0,1:T(8,128)(2,1)}) %all-gather.2.cloned.1.call-update) | async-done | bytes 3145744 | tf_op jit(solution)/shard_map/all_gather | solution.py:143
  352.4 4.7 copy.11
  357.6 209.6 %while.26 = (s32[]{:T(128)}, f32[4,4,256]{2,1,0:T(4,128)}, s32[4]{0:T(128)}, f32[3,2,1024,1024]{3,2,1,0:T(8,128)}, bf16[1024,1536]{1,0:T(8,128)(2,1)}, /*index=5...) while((s32[]{:T(128)}, f32[4,4,256]{2,1,0:T(4,128)}, ...), condition=%wide.region_16.17_spmd.clone.clone, body=%wide.region_3.16_spmd.clone.clone.sunk | while | flops 3242466048 | bytes 113556512 | solution.py:107
  359.7 5.1 constant_dynamic-slice_fusion.15
  365.6 3.0 fusion.180
  368.6 2.4 constant_dynamic-slice_fusion.14
  374.9 2.5 copy.46
  378.8 3.0 fusion.178
  387.5 2.6 copy.41
  390.1 2.5 copy.42
  394.3 3.0 fusion.176
  412.1 5.1 constant_dynamic-slice_fusion.15
  418.0 3.0 fusion.180
  421.0 2.4 constant_dynamic-slice_fusion.14
  427.3 2.5 copy.46
  431.2 3.0 fusion.178
  439.9 2.6 copy.41
  442.5 2.5 copy.42
  446.7 3.0 fusion.176
  464.5 5.1 constant_dynamic-slice_fusion.15
  470.4 3.0 fusion.180
  473.4 2.4 constant_dynamic-slice_fusion.14
  479.7 2.5 copy.46
  483.6 3.0 fusion.178
  492.3 2.6 copy.41
  494.9 2.5 copy.42
  499.1 3.0 fusion.176
  516.9 5.1 constant_dynamic-slice_fusion.15
  522.8 3.0 fusion.180
  525.8 2.4 constant_dynamic-slice_fusion.14
  532.1 2.5 copy.46
  536.0 3.0 fusion.178
  544.7 2.6 copy.41
  547.3 2.5 copy.42
  551.5 3.0 fusion.176
  567.3 11.1 %psum.7 = f32[4,1024]{1,0:T(4,128)S(1)} all-reduce(f32[4,1024]{1,0:T(4,128)} %bitcast.221), channel_id=1, replica_groups=mesh['ray'=8,'pix'=4] {'pix'}, use_global_device_ids=true, to_apply=%region_17.18 | all-reduce | flops 4096 | bytes 32768 | tf_op jit(solution)/shard_map/psum | solution.py:145
  (261 shorter events, 162.2 us)
Async XLA Ops:
  7.2 280.9 %reduce-scatter.2.cloned.1.call-start = ((), (), s32[]{:S(2)}) async-start(), calls=%async_computation.1 | async-start | bytes 7077888 | tf_op jit(solution)/shard_map/reduce_scatter | solution.py:141
  73.5 2.5 copy-start.8
  166.8 1.0 copy-start.11
  166.8 185.6 %all-gather.2.cloned.1.call-start = ((), (), s32[]{:S(2)}) async-start(), calls=%async_computation.2 | async-start | bytes 3538944 | tf_op jit(solution)/shard_map/all_gather | solution.py:143
  357.6 220.8 %copy-start.12 = (f32[2,1024]{1,0:T(2,128)S(1)}, f32[2,1024]{1,0:T(2,128)}, u32[]{:S(2)}) copy-start(f32[2,1024]{1,0:T(2,128)} %param.10) | copy-start | bytes 24580
  371.2 2.1 copy-start.3
  400.9 5.9 %copy-start.4 = (f32[1,1,256,256]{2,3,1,0:T(8,128)S(1)}, f32[1,1,256,256]{2,3,1,0:T(8,128)}, u32[]{:S(2)}) copy-start(f32[1,1,256,256]{2,3,1,0:T(8,128)} %copy.43) | copy-start | bytes 786436 | tf_op jit(solution)/shard_map/while
  400.9 5.9 %copy-start.5 = (f32[1,1,256,256]{2,3,1,0:T(8,128)S(1)}, f32[1,1,256,256]{2,3,1,0:T(8,128)}, u32[]{:S(2)}) copy-start(f32[1,1,256,256]{2,3,1,0:T(8,128)} %copy.44) | copy-start | bytes 786436 | tf_op jit(solution)/shard_map/while
  400.9 5.9 %copy-start.9 = (bf16[256,256]{0,1:T(8,128)(2,1)S(1)}, bf16[256,256]{0,1:T(8,128)(2,1)}, u32[]{:S(2)}) copy-start(bf16[256,256]{0,1:T(8,128)(2,1)} %get-tuple-element.460) | copy-start | bytes 393220 | tf_op jit(solution)/shard_map/while
  400.9 5.9 %copy-start.10 = (bf16[1024,1536]{1,0:T(8,128)(2,1)S(1)}, bf16[1024,1536]{1,0:T(8,128)(2,1)}, u32[]{:S(2)}) copy-start(bf16[1024,1536]{1,0:T(8,128)(2,1)} %get-tuple-element.559) | copy-start | bytes 9437188 | tf_op jit(solution)/shard_map/while
  404.7 2.9 copy-start.6
  404.7 2.9 copy-start.7
  406.9 1.6 copy-start
  406.9 1.6 copy-start.1
  406.9 1.8 copy-start.2
  423.6 2.1 copy-start.3
  453.3 5.9 %copy-start.4 = (f32[1,1,256,256]{2,3,1,0:T(8,128)S(1)}, f32[1,1,256,256]{2,3,1,0:T(8,128)}, u32[]{:S(2)}) copy-start(f32[1,1,256,256]{2,3,1,0:T(8,128)} %copy.43) | copy-start | bytes 786436 | tf_op jit(solution)/shard_map/while
  453.3 5.9 %copy-start.5 = (f32[1,1,256,256]{2,3,1,0:T(8,128)S(1)}, f32[1,1,256,256]{2,3,1,0:T(8,128)}, u32[]{:S(2)}) copy-start(f32[1,1,256,256]{2,3,1,0:T(8,128)} %copy.44) | copy-start | bytes 786436 | tf_op jit(solution)/shard_map/while
  453.3 5.9 %copy-start.9 = (bf16[256,256]{0,1:T(8,128)(2,1)S(1)}, bf16[256,256]{0,1:T(8,128)(2,1)}, u32[]{:S(2)}) copy-start(bf16[256,256]{0,1:T(8,128)(2,1)} %get-tuple-element.460) | copy-start | bytes 393220 | tf_op jit(solution)/shard_map/while
  453.3 5.9 %copy-start.10 = (bf16[1024,1536]{1,0:T(8,128)(2,1)S(1)}, bf16[1024,1536]{1,0:T(8,128)(2,1)}, u32[]{:S(2)}) copy-start(bf16[1024,1536]{1,0:T(8,128)(2,1)} %get-tuple-element.559) | copy-start | bytes 9437188 | tf_op jit(solution)/shard_map/while
  457.1 2.9 copy-start.6
  457.1 2.9 copy-start.7
  459.3 1.6 copy-start
  459.3 1.6 copy-start.1
  459.3 1.8 copy-start.2
  476.0 2.1 copy-start.3
  505.7 5.9 %copy-start.4 = (f32[1,1,256,256]{2,3,1,0:T(8,128)S(1)}, f32[1,1,256,256]{2,3,1,0:T(8,128)}, u32[]{:S(2)}) copy-start(f32[1,1,256,256]{2,3,1,0:T(8,128)} %copy.43) | copy-start | bytes 786436 | tf_op jit(solution)/shard_map/while
  505.7 5.9 %copy-start.5 = (f32[1,1,256,256]{2,3,1,0:T(8,128)S(1)}, f32[1,1,256,256]{2,3,1,0:T(8,128)}, u32[]{:S(2)}) copy-start(f32[1,1,256,256]{2,3,1,0:T(8,128)} %copy.44) | copy-start | bytes 786436 | tf_op jit(solution)/shard_map/while
  505.7 5.9 %copy-start.9 = (bf16[256,256]{0,1:T(8,128)(2,1)S(1)}, bf16[256,256]{0,1:T(8,128)(2,1)}, u32[]{:S(2)}) copy-start(bf16[256,256]{0,1:T(8,128)(2,1)} %get-tuple-element.460) | copy-start | bytes 393220 | tf_op jit(solution)/shard_map/while
  505.7 5.9 %copy-start.10 = (bf16[1024,1536]{1,0:T(8,128)(2,1)S(1)}, bf16[1024,1536]{1,0:T(8,128)(2,1)}, u32[]{:S(2)}) copy-start(bf16[1024,1536]{1,0:T(8,128)(2,1)} %get-tuple-element.559) | copy-start | bytes 9437188 | tf_op jit(solution)/shard_map/while
  509.5 2.9 copy-start.6
  509.5 2.9 copy-start.7
  511.7 1.6 copy-start
  511.7 1.6 copy-start.1
  511.7 1.8 copy-start.2
  528.4 2.1 copy-start.3
  558.1 5.9 %copy-start.4 = (f32[1,1,256,256]{2,3,1,0:T(8,128)S(1)}, f32[1,1,256,256]{2,3,1,0:T(8,128)}, u32[]{:S(2)}) copy-start(f32[1,1,256,256]{2,3,1,0:T(8,128)} %copy.43) | copy-start | bytes 786436 | tf_op jit(solution)/shard_map/while
  558.1 5.9 %copy-start.5 = (f32[1,1,256,256]{2,3,1,0:T(8,128)S(1)}, f32[1,1,256,256]{2,3,1,0:T(8,128)}, u32[]{:S(2)}) copy-start(f32[1,1,256,256]{2,3,1,0:T(8,128)} %copy.44) | copy-start | bytes 786436 | tf_op jit(solution)/shard_map/while
  558.1 5.9 %copy-start.9 = (bf16[256,256]{0,1:T(8,128)(2,1)S(1)}, bf16[256,256]{0,1:T(8,128)(2,1)}, u32[]{:S(2)}) copy-start(bf16[256,256]{0,1:T(8,128)(2,1)} %get-tuple-element.460) | copy-start | bytes 393220 | tf_op jit(solution)/shard_map/while
  558.1 5.9 %copy-start.10 = (bf16[1024,1536]{1,0:T(8,128)(2,1)S(1)}, bf16[1024,1536]{1,0:T(8,128)(2,1)}, u32[]{:S(2)}) copy-start(bf16[1024,1536]{1,0:T(8,128)(2,1)} %get-tuple-element.559) | copy-start | bytes 9437188 | tf_op jit(solution)/shard_map/while
  561.9 2.9 copy-start.6
  561.9 2.9 copy-start.7
  564.1 1.6 copy-start
  564.1 1.6 copy-start.1
  564.1 1.8 copy-start.2
Sparse Core Ops, SparseCore 0:
  166.9 121.0 reduce-scatter.1
  290.1 62.1 all-gather.1
where the time goes:
time: 591 us; the launch traced here: 587 us
  waiting for transfers between devices  181 us (31%)
  other arithmetic  179 us (30%)
  local copies, waits for them, and re-layouts  128 us (22%)
  matrix products  70 us (12%)
  between operations  14.1 us (2%)
  blocking collectives  11.1 us (2%)
    reduce_scatter x1, waiting for transfers between devices, on_device(): lax.psum_scatter(field_terms(row_tab, col_tab), 'ray', scatter_dimension=...  120 us
    dot_general x36, matrix products, product(): lax.dot_general(left, right, dims, preferred_element_type=jnp.float32)  70 us
    while x128, local copies, waits for them, and re-layouts  70 us
    all_gather x1, waiting for transfers between devices, on_device(): gathered = lax.all_gather(grad_u, 'ray', axis=0, tiled=True)  60.4 us
    cos x1, other arithmetic, build_tables(): col_list.append(jnp.stack([jnp.cos(beta), jnp.sin(beta)]))  46.3 us
    add x4, other arithmetic, step(): return total + jnp.concatenate(parts, axis=1)  24.9 us
    sub x12, other arithmetic, one_block(): d_alpha = d_aim * a_re - d_are * a_im  23.5 us
    another operation x28, other arithmetic  21.7 us
  transfers between devices with their start and end apart: 2, of which 2 were waited for; matrix products, arithmetic and copies ran while one was open for 0% of the time, Pallas kernels for 0%

commit v1 on v0

v1 whole, which is shorter than its diff:
```python
import functools
import math

import jax
import jax.numpy as jnp
from jax import lax
from jax.experimental import pallas as pl
from jax.experimental.pallas import tpu as pltpu
from jax.sharding import PartitionSpec as P

NPIX = 1024
LANES = 128
CHUNK = 256
TILES = CHUNK // LANES

wave_scales = (1.2088, 1.0, 0.8953)
two_pi = 2.0 * math.pi
sin_terms = [(-1.0) ** n / math.factorial(2 * n + 1) * (0.5 * math.pi) ** (2 * n + 1) for n in range(5)]
cos_terms = [(-1.0) ** n / math.factorial(2 * n) * (0.5 * math.pi) ** (2 * n) for n in range(6)]


def horner(square, terms):
    value = terms[-1]
    for term in terms[-2::-1]:
        value = value * square + term
    return value


def circle(turns):
    rest = turns - jnp.floor(turns + 0.5)
    square = rest * rest
    sin = rest * horner(square, sin_terms)
    cos = horner(square, cos_terms)
    sin, cos = 2.0 * sin * cos, 1.0 - 2.0 * sin * sin
    return 1.0 - 2.0 * sin * sin, 2.0 * sin * cos


def times(left, right):
    return (left[0] * right[0] - left[1] * right[1], left[0] * right[1] + left[1] * right[0])


def ladder(first, second, twice, count):
    out = [first, second]
    while len(out) < count:
        out.append(twice * out[-1] - out[-2])
    return out[:count]


def psf_kernel(sizes, own_ref, near_ref, far_ref, extra_ref, grad_ref, psf_ref, own_out, near_out, far_out, extra_out,
               rays_s, row_base, col_base, steps, row_tab, col_tab, col_half, field, cot, sums):
    shards, local, plen, clen, half, pairs, norm = sizes
    x_mid = (lax.axis_index("pix") * plen).astype(jnp.float32) + (0.5 * plen - 0.5 * NPIX)
    y_low = (lax.axis_index("ray") * clen).astype(jnp.float32) + (0.5 - 0.5 * NPIX)

    split = local // CHUNK

    def place(slot, block):
        for item in range(6):
            rays_s[item, slot : slot + 1, :] = block[item : item + 1, :]

    place(0, own_ref[...])
    for index in range(pairs):
        place(1 + index, near_ref[index])
        place(1 + pairs + index, far_ref[index])
    place(1 + 2 * pairs, extra_ref[...])

    def spread(base, wave, part, sub, piece, value):
        for tile in range(TILES):
            base[wave, part, piece * TILES + tile, pl.ds(sub, shards, stride=8), :] = value[:, tile * LANES : (tile + 1) * LANES]

    def gather(base, wave, part, shard, chunk):
        rows8 = pl.ds(pl.multiple_of(shard * 8, 8), 8)
        first = lax.rem(chunk, split) * TILES
        return jnp.concatenate([base[wave, part, first + tile, rows8, :] for tile in range(TILES)], axis=1)

    @pl.loop(0, local // CHUNK)
    def _(piece):
        lanes = pl.ds(pl.multiple_of(piece * CHUNK, CHUNK), CHUNK)
        x, y, dir_l, dir_m, path, amp = [rays_s[item, :, lanes] for item in range(6)]
        phase = path * (1.0 / two_pi) + (dir_l * (x_mid - x) + dir_m * (y_low - y))
        amp = amp * norm
        for wave in range(3):
            scale = wave_scales[wave]
            value = circle((0.5 * scale) * dir_l)
            one = times(value, value)
            for sub in range(8):
                spread(row_base, wave, 0, sub, piece, value[0])
                spread(row_base, wave, 1, sub, piece, value[1])
                value = times(value, one)
            two = times(one, one)
            four = times(two, two)
            eight = times(four, four)
            steps[wave, 0, :, lanes] = eight[0]
            steps[wave, 1, :, lanes] = eight[1]
            cos, sin = circle(scale * phase)
            value = (amp * cos, amp * sin)
            one = circle(scale * dir_m)
            for sub in range(8):
                spread(col_base, wave, 0, sub, piece, value[0])
                spread(col_base, wave, 1, sub, piece, value[1])
                value = times(value, one)
            two = times(one, one)
            four = times(two, two)
            eight = times(four, four)
            steps[wave, 2, :, lanes] = eight[0]
            steps[wave, 3, :, lanes] = eight[1]

    field[...] = jnp.zeros_like(field)

    def where(chunk):
        return chunk // split, pl.ds(pl.multiple_of(lax.rem(chunk, split) * CHUNK, CHUNK), CHUNK)

    @pl.loop(0, shards * split)
    def _(chunk):
        shard, lanes = where(chunk)
        for wave in range(3):
            for base, step, tall, is_row in ((row_base, 0, half, True), (col_base, 2, clen, False)):
                c8 = jnp.broadcast_to(steps[wave, step, pl.ds(shard, 1), lanes], (8, CHUNK))
                s8 = jnp.broadcast_to(steps[wave, step + 1, pl.ds(shard, 1), lanes], (8, CHUNK))
                first = (gather(base, wave, 0, shard, chunk), gather(base, wave, 1, shard, chunk))
                second = times(first, (c8, s8))
                twice = 2.0 * c8
                for part in range(2):
                    run = ladder(first[part], second[part], twice, tall // 8)
                    for pair in range(tall // 16):
                        both = jnp.concatenate(run[2 * pair : 2 * pair + 2], axis=0)
                        place16 = pl.ds(part * tall + 16 * pair, 16)
                        if is_row:
                            row_tab[wave, chunk, place16, :] = both.astype(jnp.bfloat16)
                        else:
                            col_tab[wave, chunk, place16, :] = both
                            col_half[wave, place16, :] = both.astype(jnp.bfloat16)
            field[wave] += lax.dot_general(
                col_half[wave], row_tab[wave, chunk], (((1,), (1,)), ((), ())), preferred_element_type=jnp.float32
            )

    offset = lax.broadcasted_iota(jnp.int32, (8, half), 1).astype(jnp.float32) + 0.5
    for wave in range(3):
        for group in range(clen // 8):
            rows = slice(8 * group, 8 * group + 8)
            low = slice(clen + 8 * group, clen + 8 * group + 8)
            even_r, odd_r = field[wave, rows, :half], field[wave, rows, half:]
            even_i, odd_i = field[wave, low, :half], field[wave, low, half:]
            up_r, up_i = even_r - odd_i, even_i + odd_r
            dn_r, dn_i = even_r + odd_i, even_i - odd_r
            psf_ref[wave, 0, rows, :] = dn_r * dn_r + dn_i * dn_i
            psf_ref[wave, 1, rows, :] = up_r * up_r + up_i * up_i
            g_dn = 2.0 * grad_ref[wave, 0, rows, :]
            g_up = 2.0 * grad_ref[wave, 1, rows, :]
            dn_r, dn_i, up_r, up_i = g_dn * dn_r, g_dn * dn_i, g_up * up_r, g_up * up_i
            p_r, p_i, m_r, m_i = up_r + dn_r, up_i + dn_i, up_r - dn_r, up_i - dn_i
            plain = jnp.concatenate(
                [jnp.concatenate([p_r, m_i], axis=1), jnp.concatenate([p_i, -m_r], axis=1)], axis=0
            )
            heavy = jnp.concatenate(
                [
                    jnp.concatenate([offset * m_r, offset * p_i], axis=1),
                    jnp.concatenate([offset * m_i, -(offset * p_r)], axis=1),
                ],
                axis=0,
            )
            cot[wave, 32 * group : 32 * group + 16, :] = plain.astype(jnp.bfloat16)
            cot[wave, 32 * group + 16 : 32 * group + 32, :] = heavy.astype(jnp.bfloat16)

    sub = lax.broadcasted_iota(jnp.int32, (8, CHUNK), 0).astype(jnp.float32)
    y_sub = sub + (y_low + clen)

    @pl.loop(0, shards * split)
    def _(chunk):
        shard, lanes = where(chunk)
        total = [jnp.zeros((8, CHUNK), jnp.float32) for _ in range(4)]
        for wave in range(3):
            scale = wave_scales[wave]
            back = jnp.dot(cot[wave], row_tab[wave, chunk], preferred_element_type=jnp.float32)
            im_sum = jnp.zeros((8, CHUNK), jnp.float32)
            up_sum = jnp.zeros((8, CHUNK), jnp.float32)
            re_sum = jnp.zeros((8, CHUNK), jnp.float32)
            x_sum = jnp.zeros((8, CHUNK), jnp.float32)
            for group in range(clen // 8):
                e_r, e_i, f_r, f_i = [back[32 * group + 8 * n : 32 * group + 8 * n + 8] for n in range(4)]
                b_r = col_tab[wave, chunk, 8 * group : 8 * group + 8, :]
                b_i = col_tab[wave, chunk, clen + 8 * group : clen + 8 * group + 8, :]
                im_sum = im_sum + (b_r * e_i - b_i * e_r)
                re_sum = re_sum + (b_r * e_r + b_i * e_i)
                x_sum = x_sum + (b_r * f_i - b_i * f_r)
                up_sum = up_sum + im_sum
            total[0] = total[0] + scale * im_sum
            total[1] = total[1] + (scale * two_pi) * (x_mid * im_sum + x_sum)
            total[2] = total[2] + (scale * two_pi) * (y_sub * im_sum - 8.0 * up_sum)
            total[3] = total[3] + re_sum
        rows = [jnp.sum(value, axis=0, keepdims=True) for value in total]
        sums[shard, :, lanes] = jnp.concatenate(rows, axis=0)

    own_out[...] = sums[0]
    for index in range(pairs):
        near_out[index] = sums[1 + index]
        far_out[index] = sums[1 + pairs + index]
    extra_out[...] = sums[1 + 2 * pairs]


def split_pairs(shards):
    if shards == 8:
        return ((3, 7), (1, 6), (2, 4)), 5
    pairs = (shards - 2) // 2
    return tuple((1 + n, 1 + pairs + n) for n in range(pairs)), shards - 1


def on_device(positions, directions, path, amplitude, psf_grad):
    rays = jnp.concatenate([positions, directions, path[None], amplitude[None]], axis=0)
    local = rays.shape[1]
    shards = lax.axis_size("ray")
    rows = lax.axis_size("pix")
    plen = NPIX // rows
    clen = NPIX // shards
    half = max(plen // 2, LANES)
    norm = 1.0 / math.sqrt(local * shards)
    pairs, last = split_pairs(shards)
    count = len(pairs)

    def swap(value, ray_even, ray_odd, pix=0):
        moves = []
        for r in range(shards):
            for p in range(rows):
                moves.append((r * rows + p, (r ^ (ray_odd if p % 2 else ray_even)) * rows + (p ^ pix)))
        return lax.ppermute(value, ("ray", "pix"), moves)

    near = jnp.stack([swap(rays, even, odd) for even, odd in pairs])
    extra = swap(rays, last, last)
    far = swap(near, 0, 0, 1)

    weight = psf_grad.reshape(3, 2, plen // 2, clen)
    weight = jnp.stack([weight[:, 0, ::-1], weight[:, 1]], axis=1).transpose(0, 1, 3, 2)
    if half != plen // 2:
        weight = jnp.pad(weight, ((0, 0), (0, 0), (0, 0), (0, half - plen // 2)))

    chunks = shards * (local // CHUNK)
    sizes = (shards, local, plen, clen, half, count, norm)
    f32, bf16 = jnp.float32, jnp.bfloat16
    vmem = pl.BlockSpec(memory_space=pltpu.VMEM)
    psf, own_sum, near_sum, far_sum, extra_sum = pl.pallas_call(
        functools.partial(psf_kernel, sizes),
        out_shape=[
            jax.ShapeDtypeStruct((3, 2, clen, half), f32),
            jax.ShapeDtypeStruct((4, local), f32),
            jax.ShapeDtypeStruct((count, 4, local), f32),
            jax.ShapeDtypeStruct((count, 4, local), f32),
            jax.ShapeDtypeStruct((4, local), f32),
        ],
        in_specs=[vmem] * 5,
        out_specs=[vmem] * 5,
        scratch_shapes=[
            pltpu.VMEM((6, shards, local), f32),
            pltpu.VMEM((3, 2, local // LANES, 8 * shards, LANES), f32),
            pltpu.VMEM((3, 2, local // LANES, 8 * shards, LANES), f32),
            pltpu.VMEM((3, 4, shards, local), f32),
            pltpu.VMEM((3, chunks, 2 * half, CHUNK), bf16),
            pltpu.VMEM((3, chunks, 2 * clen, CHUNK), f32),
            pltpu.VMEM((3, 2 * clen, CHUNK), bf16),
            pltpu.VMEM((3, 2 * clen, 2 * half), f32),
            pltpu.VMEM((3, 4 * clen, 2 * half), bf16),
            pltpu.VMEM((shards, 4, local), f32),
        ],
        compiler_params=pltpu.CompilerParams(vmem_limit_bytes=62 * 1024 * 1024),
    )(rays, near, far, extra, weight)

    psf = psf[..., : plen // 2].transpose(0, 1, 3, 2)
    psf = jnp.concatenate([psf[:, 0, ::-1], psf[:, 1]], axis=1)

    near_sum = near_sum + swap(far_sum, 0, 0, 1)
    total = own_sum + swap(extra_sum, last, last)
    for index, (even, odd) in enumerate(pairs):
        total = total + swap(near_sum[index], even, odd)
    bit = 1
    parts = total
    while bit < rows:
        parts = parts + swap(parts, 0, 0, bit)
        bit *= 2
    sums = parts
    grads = jnp.stack(
        [
            sums[0],
            -two_pi * rays[2] * sums[0],
            -two_pi * rays[3] * sums[0],
            (sums[1] - two_pi * rays[0] * sums[0]) / NPIX,
            (sums[2] - two_pi * rays[1] * sums[0]) / NPIX,
            sums[3] / rays[5],
        ]
    )
    return (psf, grads)


def solution(mesh):
    in_specs = (P(None, "ray"), P(None, "ray"), P("ray"), P("ray"), P(None, "pix", "ray"))
    out_specs = (P(None, "pix", "ray"), P(None, "ray"))
    return jax.shard_map(on_device, mesh=mesh, in_specs=in_specs, out_specs=out_specs, check_vma=False)
```

time: 591 us -> 58.6 us (0.10)
  other arithmetic: 179 us -> 2.46 us
  waiting for transfers between devices: 181 us -> 6.76 us
  local copies, waits for them, and re-layouts: 128 us -> 6.25 us
  matrix products: 70 us -> 0 us
  Pallas kernels: 0 us -> 26.3 us
  starting transfers between devices: 0.26 us -> 15.8 us
  between operations: 14.1 us -> 0.76 us
  blocking collectives: 11.1 us -> 0 us
    reduce_scatter x1 -> x0, waiting for transfers between devices: 120 us -> none  [on_device(): lax.psum_scatter(field_terms(row_tab, col_tab), 'ray', scatter_dimension=...]
    dot_general x36 -> x0, matrix products: 70 us -> none  [product(): lax.dot_general(left, right, dims, preferred_element_type=jnp.float32)]
    while x128 -> x0, local copies, waits for them, and re-layouts: 70 us -> none
    all_gather x1 -> x0, waiting for transfers between devices: 60.4 us -> none  [on_device(): gathered = lax.all_gather(grad_u, 'ray', axis=0, tiled=True)]
    cos x1 -> x0, other arithmetic: 46.3 us -> none  [build_tables(): col_list.append(jnp.stack([jnp.cos(beta), jnp.sin(beta)]))]
    another operation x33 -> x1, other arithmetic: 37.8 us -> 0.01 us  [on_device(): near = jnp.stack([swap(rays, even, odd) for even, odd in pairs])]
    slice x10 -> x1, local copies, waits for them, and re-layouts: 31.4 us -> 1.05 us  [on_device(): weight[:, 0, ::-1]]
    pallas_call x0 -> x1, Pallas kernels: none -> 26.3 us  [on_device(): pl.pallas_call(functools.partial(psf_kernel, sizes), out_shape=[jax.Shape...]
  transfers between devices with their start and end apart: 2 -> 12, of which waited for: 2 -> 7; matrix products, arithmetic and copies ran while one was open for 0% -> 9% of each run, Pallas kernels for 0% -> 0%
where the time goes in v1:
time: 58.6 us; the launch traced here: 58.3 us
  Pallas kernels  26.3 us (45%)
  starting transfers between devices  15.8 us (27%)
  waiting for transfers between devices  6.76 us (12%)
  local copies, waits for them, and re-layouts  6.25 us (11%)
  other arithmetic  2.46 us (4%)
  between operations  0.76 us (1%)
    pallas_call x1, Pallas kernels, on_device(): pl.pallas_call(functools.partial(psf_kernel, sizes), out_shape=[jax.Shape...  26.3 us
    ppermute x12, starting transfers between devices, swap(): return lax.ppermute(value, ('ray', 'pix'), moves)  15.8 us
    ppermute x12, waiting for transfers between devices, swap(): return lax.ppermute(value, ('ray', 'pix'), moves)  6.76 us
    unnamed x20, local copies, waits for them, and re-layouts  3.99 us
  transfers between devices with their start and end apart: 12, of which 7 were waited for; matrix products, arithmetic and copies ran while one was open for 9% of the time, Pallas kernels for 0%

profile of v1, /device:TPU:0, one launch (start us, length us, event | category | flops | bytes accessed | tf_op | source)
XLA Modules:
  0.0 58.3 jit_solution(5205245336008644741)
XLA Ops:
  0.6 0.8 %pad_maximum_fusion.2.own_ref = f32[6,1024]{1,0:T(8,128)S(1)} fusion(f32[1,1024]{1,0:T(1,128)} %bitcast.28, f32[1,1024]{1,0:T(1,128)} %bitcast.31, f32[2,1024]{1,0:T(2,128)} %param.6, f32[2,1024]{1,0:T(2,128)} %param.5), kind=kLoop, calls=%fused_computation.5 | loop fusion | flops 18432 | bytes 49152 | tf_op jit(solution)/shard_map/concatenate | solution.py:209
  1.4 0.0 copy-start.1
  1.4 5.1 %collective-permute-start.4 = (f32[6,1024]{1,0:T(8,128)S(1)}, f32[6,1024]{1,0:T(8,128)S(1)}, u32[]{:S(2)}, u32[]{:S(2)}) collective-permute-start(f32[6,1024]{1,0:T(8,128)S(1)} %pad_maximum_fusion.2.own_ref), channel_id=1, source_target_pairs={{0,20},{1,21},{2,22},{3,23},{4,16},{5,17},{6,18},{7,19},{8,28},{9,... | collective-permute-start | bytes 73736 | tf_op jit(solution)/shard_map/ppermute | solution.py:225
  6.5 1.6 %collective-permute-start.2 = (f32[6,1024]{1,0:T(8,128)S(1)}, f32[6,1024]{1,0:T(8,128)S(1)}, u32[]{:S(2)}, u32[]{:S(2)}) collective-permute-start(f32[6,1024]{1,0:T(8,128)S(1)} %pad_maximum_fusion.2.own_ref), channel_id=1, source_target_pairs={{0,8},{1,17},{2,10},{3,19},{4,12},{5,21},{6,14},{7,23},{8,0},{9,25... | collective-permute-start | bytes 73736 | tf_op jit(solution)/shard_map/ppermute | solution.py:225
  8.0 0.5 collective-permute-start.1
  8.6 1.4 %collective-permute-start = (f32[6,1024]{1,0:T(8,128)S(1)}, f32[6,1024]{1,0:T(8,128)S(1)}, u32[]{:S(2)}, u32[]{:S(2)}) collective-permute-start(f32[6,1024]{1,0:T(8,128)S(1)} %pad_maximum_fusion.2.own_ref), channel_id=1, source_target_pairs={{0,12},{1,29},{2,14},{3,31},{4,8},{5,25},{6,10},{7,27},{8,4},{9,21... | collective-permute-start | bytes 73736 | tf_op jit(solution)/shard_map/ppermute | solution.py:225
  10.0 1.0 %fusion.2 = (f32[3,1,128,128]{3,2,1,0:T(8,128)S(1)}, f32[3,1,128,128]{3,2,1,0:T(8,128)S(1)}) fusion(f32[3,2,128,128]{3,2,1,0:T(8,128)} %bitcast.23), kind=kLoop, calls=%fused_computation.16 | loop fusion | bytes 786432 | tf_op jit(solution)/shard_map/slice | solution.py:232
  11.0 0.0 copy-done.1
  11.0 0.1 copy.13
  11.2 0.3 rev.6
  11.4 0.1 copy.14
  11.6 0.0 collective-permute-done.2
  11.6 0.4 collective-permute-done.1
  12.0 1.4 %collective-permute-done = f32[6,1024]{1,0:T(8,128)S(1)} collective-permute-done((f32[6,1024]{1,0:T(8,128)S(1)}, f32[6,1024]{1,0:T(8,128)S(1)}, u32[]{:S(2)}, u32[]{:S(2)}) %collective-permute-start) | collective-permute-done | bytes 24608 | tf_op jit(solution)/shard_map/ppermute | solution.py:225
  13.4 0.0 copy-start
  13.4 1.6 %collective-permute-start.3 = (f32[3,6,1024]{2,1,0:T(8,128)S(1)}, f32[3,6,1024]{2,1,0:T(8,128)S(1)}, u32[]{:S(2)}, u32[]{:S(2)}) collective-permute-start(f32[3,6,1024]{2,1,0:T(8,128)S(1)} %pad_maximum_fusion.1.near_ref), channel_id=1, source_target_pairs={{0,1},{1,0},{2,3},{3,2},{4,5},{5,4},{6,7},{7,6},{8,9},{9,8},{10,11... | collective-permute-start | bytes 221192 | tf_op jit(solution)/shard_map/ppermute | solution.py:225
  15.0 0.8 %maximum_bitcast_fusion.grad_ref = f32[3,2,128,128]{3,2,1,0:T(8,128)} fusion(f32[3,1,128,128]{2,3,1,0:T(8,128)S(1)} %copy.14, f32[3,1,128,128]{2,3,1,0:T(8,128)S(1)} %rev.6), kind=kLoop, calls=%fused_computation | loop fusion | flops 98304 | bytes 786432 | tf_op jit(solution)/shard_map/transpose | solution.py:232
  15.7 0.0 copy-done
  15.7 0.0 collective-permute-done.4.extra_ref
  15.7 0.2 collective-permute-done.3.far_ref
  15.9 0.5 copy-done.3
  16.4 0.6 %copy-done.2 = f32[3,6,1024]{2,1,0:T(8,128)} copy-done((f32[3,6,1024]{2,1,0:T(8,128)}, f32[3,6,1024]{2,1,0:T(8,128)S(1)}, u32[]{:S(2)}) %copy-start.2) | copy-done | bytes 73752
  17.0 26.3 %shard_map.68 = (f32[3,2,128,128]{3,2,1,0:T(8,128)}, f32[4,1024]{1,0:T(4,128)}, f32[3,4,1024]{2,1,0:T(4,128)}, f32[3,4,1024]{2,1,0:T(4,128)}, f32[4,1024]{1,0:T(4,128)}) custom-call(f32[6,1024]{1,0:T(8,128)} %copy-done.1, f32[3,6,1024]{2,1,0:T(8,128)} %copy-done, f32[3,6,1024]{2,1,0:T(8,128)} %copy-done.2, f32[6,1024]{1,0:T(8,128)} %copy-done.3, ...), custom_call_target="tpu_custom_call" | custom-call | tf_op jit(solution)/shard_map/pallas_call | solution.py:240
  43.3 0.0 collective-permute-start.6
  43.3 0.3 collective-permute-start.5
  43.6 1.1 %collective-permute-done.6 = f32[3,4,1024]{2,1,0:T(4,128)S(1)} collective-permute-done((f32[3,4,1024]{2,1,0:T(4,128)}, f32[3,4,1024]{2,1,0:T(4,128)S(1)}, u32[]{:S(2)}, u32[]{:S(2)}) %collective-permute-start.6) | collective-permute-done | bytes 49184 | tf_op jit(solution)/shard_map/ppermute | solution.py:225
  44.7 0.8 %add.22 = f32[3,4,1024]{2,1,0:T(4,128)S(1)} add(f32[3,4,1024]{2,1,0:T(4,128)} %get-tuple-element.10, f32[3,4,1024]{2,1,0:T(4,128)S(1)} %collective-permute-done.6) | non-fusion elementwise | flops 12288 | bytes 147456 | tf_op jit(solution)/shard_map/add | solution.py:269
  45.6 0.0 copy-start.7
  45.6 0.4 collective-permute-start.7
  46.0 1.6 %collective-permute-start.9 = (f32[4,1024]{1,0:T(4,128)S(1)}, f32[4,1024]{1,0:T(4,128)S(1)}, u32[]{:S(2)}, u32[]{:S(2)}) collective-permute-start(f32[4,1024]{1,0:T(4,128)S(1)} %get-tuple-element.21), channel_id=1, source_target_pairs={{0,8},{1,17},{2,10},{3,19},{4,12},{5,21},{6,14},{7,23},{8,0},{9,25... | collective-permute-start | bytes 49160 | tf_op jit(solution)/shard_map/ppermute | solution.py:225
  47.6 1.5 %collective-permute-start.8 = (f32[4,1024]{1,0:T(4,128)S(1)}, f32[4,1024]{1,0:T(4,128)S(1)}, u32[]{:S(2)}, u32[]{:S(2)}) collective-permute-start(f32[4,1024]{1,0:T(4,128)S(1)} %get-tuple-element.22), channel_id=1, source_target_pairs={{0,4},{1,25},{2,6},{3,27},{4,0},{5,29},{6,2},{7,31},{8,12},{9,17},... | collective-permute-start | bytes 49160 | tf_op jit(solution)/shard_map/ppermute | solution.py:225
  49.1 0.0 collective-permute-done.5
  49.1 1.1 %collective-permute-done.7 = f32[4,1024]{1,0:T(4,128)S(1)} collective-permute-done((f32[4,1024]{1,0:T(4,128)S(1)}, f32[4,1024]{1,0:T(4,128)S(1)}, u32[]{:S(2)}, u32[]{:S(2)}) %collective-permute-start.7) | collective-permute-done | bytes 16416 | tf_op jit(solution)/shard_map/ppermute | solution.py:225
  50.3 0.0 collective-permute-done.9
  50.3 1.2 %collective-permute-done.8 = f32[4,1024]{1,0:T(4,128)S(1)} collective-permute-done((f32[4,1024]{1,0:T(4,128)S(1)}, f32[4,1024]{1,0:T(4,128)S(1)}, u32[]{:S(2)}, u32[]{:S(2)}) %collective-permute-start.8) | collective-permute-done | bytes 16416 | tf_op jit(solution)/shard_map/ppermute | solution.py:225
  51.5 0.0 copy-done.7
  51.5 0.2 collective-permute-start.10
  51.7 1.0 %slice_bitcast_fusion.1 = (f32[3,1,128,128]{2,3,0,1:T(8,128)S(1)}, f32[3,128,128]{1,2,0:T(8,128)S(1)}) fusion(f32[3,2,128,128]{2,3,1,0:T(8,128)} %bitcast.24), kind=kLoop, calls=%fused_computation.3 | loop fusion | bytes 786432
  52.8 0.3 rev.7
  53.1 0.0 collective-permute-done.10
  53.1 1.5 %collective-permute-start.11 = (f32[4,1024]{1,0:T(4,128)S(1)}, f32[4,1024]{1,0:T(4,128)S(1)}, u32[]{:S(2)}, u32[]{:S(2)}) collective-permute-start(f32[4,1024]{1,0:T(4,128)S(1)} %add.26), channel_id=1, source_target_pairs={{0,2},{1,3},{2,0},{3,1},{4,6},{5,7},{6,4},{7,5},{8,10},{9,11},{10,... | collective-permute-start | bytes 49160 | tf_op jit(solution)/shard_map/ppermute | solution.py:225
  54.7 0.9 %copy.12 = f32[3,256,128]{2,1,0:T(8,128)} copy(f32[3,256,128]{1,2,0:T(8,128)S(1)} %pad_maximum_fusion) | data formatting | bytes 786432
  55.6 1.3 %collective-permute-done.11 = f32[4,1024]{1,0:T(4,128)S(1)} collective-permute-done((f32[4,1024]{1,0:T(4,128)S(1)}, f32[4,1024]{1,0:T(4,128)S(1)}, u32[]{:S(2)}, u32[]{:S(2)}) %collective-permute-start.11) | collective-permute-done | bytes 16416 | tf_op jit(solution)/shard_map/ppermute | solution.py:225
  56.9 0.0 copy-done.4
  56.9 0.0 copy-done.5
  56.9 0.0 copy-start.6
  57.0 0.6 %copy-done.6 = f32[1024]{0:T(1024)S(1)} copy-done((f32[1024]{0:T(1024)S(1)}, f32[1024]{0:T(1024)}, u32[]{:S(2)}) %copy-start.6) | copy-done | bytes 4120
  57.6 0.7 %stack.31 = f32[6,1024]{1,0:T(8,128)} concatenate(f32[1,1024]{1,0:T(1,128)S(1)} %get-tuple-element.31, f32[1,1024]{1,0:T(1,128)S(1)} %get-tuple-element.29, f32[1,1024]{1,0:T(1,128)S(1)} %get-tuple-element.30, f32[1,1024]{1,0:T(1,128)S(1)} %get-tuple-element.24, f32[1,1024]{1,0:T(1,128)S(1)} %get-tuple-element.23, f32[1,1024]{1,0:T(1,128)S(1)} %bitcast.30), dimensions={0} | concatenate | bytes 49152 | tf_op jit(solution)/shard_map/stack | solution.py:279
  (12 shorter events, 0.1 us)
Async XLA Ops:
  1.4 9.6 %copy-start.1 = (f32[6,1024]{1,0:T(8,128)}, f32[6,1024]{1,0:T(8,128)S(1)}, u32[]{:S(2)}) copy-start(f32[6,1024]{1,0:T(8,128)S(1)} %pad_maximum_fusion.2.own_ref) | copy-start | bytes 73732
  1.4 14.3 %collective-permute-start.4 = (f32[6,1024]{1,0:T(8,128)S(1)}, f32[6,1024]{1,0:T(8,128)S(1)}, u32[]{:S(2)}, u32[]{:S(2)}) collective-permute-start(f32[6,1024]{1,0:T(8,128)S(1)} %pad_maximum_fusion.2.own_ref), channel_id=1, source_target_pairs={{0,20},{1,21},{2,22},{3,23},{4,16},{5,17},{6,18},{7,19},{8,28},{9,... | collective-permute-start | bytes 73736 | tf_op jit(solution)/shard_map/ppermute | solution.py:225
  6.5 5.1 %collective-permute-start.2 = (f32[6,1024]{1,0:T(8,128)S(1)}, f32[6,1024]{1,0:T(8,128)S(1)}, u32[]{:S(2)}, u32[]{:S(2)}) collective-permute-start(f32[6,1024]{1,0:T(8,128)S(1)} %pad_maximum_fusion.2.own_ref), channel_id=1, source_target_pairs={{0,8},{1,17},{2,10},{3,19},{4,12},{5,21},{6,14},{7,23},{8,0},{9,25... | collective-permute-start | bytes 73736 | tf_op jit(solution)/shard_map/ppermute | solution.py:225
  8.0 3.9 %collective-permute-start.1 = (f32[6,1024]{1,0:T(8,128)S(1)}, f32[6,1024]{1,0:T(8,128)S(1)}, u32[]{:S(2)}, u32[]{:S(2)}) collective-permute-start(f32[6,1024]{1,0:T(8,128)S(1)} %pad_maximum_fusion.2.own_ref), channel_id=1, source_target_pairs={{0,4},{1,25},{2,6},{3,27},{4,0},{5,29},{6,2},{7,31},{8,12},{9,17},... | collective-permute-start | bytes 73736 | tf_op jit(solution)/shard_map/ppermute | solution.py:225
  8.6 4.8 %collective-permute-start = (f32[6,1024]{1,0:T(8,128)S(1)}, f32[6,1024]{1,0:T(8,128)S(1)}, u32[]{:S(2)}, u32[]{:S(2)}) collective-permute-start(f32[6,1024]{1,0:T(8,128)S(1)} %pad_maximum_fusion.2.own_ref), channel_id=1, source_target_pairs={{0,12},{1,29},{2,14},{3,31},{4,8},{5,25},{6,10},{7,27},{8,4},{9,21... | collective-permute-start | bytes 73736 | tf_op jit(solution)/shard_map/ppermute | solution.py:225
  13.4 2.3 %copy-start = (f32[3,6,1024]{2,1,0:T(8,128)}, f32[3,6,1024]{2,1,0:T(8,128)S(1)}, u32[]{:S(2)}) copy-start(f32[3,6,1024]{2,1,0:T(8,128)S(1)} %pad_maximum_fusion.1.near_ref) | copy-start | bytes 221188
  13.4 2.5 %collective-permute-start.3 = (f32[3,6,1024]{2,1,0:T(8,128)S(1)}, f32[3,6,1024]{2,1,0:T(8,128)S(1)}, u32[]{:S(2)}, u32[]{:S(2)}) collective-permute-start(f32[3,6,1024]{2,1,0:T(8,128)S(1)} %pad_maximum_fusion.1.near_ref), channel_id=1, source_target_pairs={{0,1},{1,0},{2,3},{3,2},{4,5},{5,4},{6,7},{7,6},{8,9},{9,8},{10,11... | collective-permute-start | bytes 221192 | tf_op jit(solution)/shard_map/ppermute | solution.py:225
  15.7 0.6 %copy-start.3 = (f32[6,1024]{1,0:T(8,128)}, f32[6,1024]{1,0:T(8,128)S(1)}, u32[]{:S(2)}) copy-start(f32[6,1024]{1,0:T(8,128)S(1)} %collective-permute-done.4.extra_ref) | copy-start | bytes 73732
  16.4 0.6 %copy-start.2 = (f32[3,6,1024]{2,1,0:T(8,128)}, f32[3,6,1024]{2,1,0:T(8,128)S(1)}, u32[]{:S(2)}) copy-start(f32[3,6,1024]{2,1,0:T(8,128)S(1)} %collective-permute-done.3.far_ref) | copy-start | bytes 221188
  43.3 1.4 %collective-permute-start.6 = (f32[3,4,1024]{2,1,0:T(4,128)}, f32[3,4,1024]{2,1,0:T(4,128)S(1)}, u32[]{:S(2)}, u32[]{:S(2)}) collective-permute-start(f32[3,4,1024]{2,1,0:T(4,128)} %get-tuple-element.11), channel_id=1, source_target_pairs={{0,1},{1,0},{2,3},{3,2},{4,5},{5,4},{6,7},{7,6},{8,9},{9,8},{10,11... | collective-permute-start | bytes 147464 | tf_op jit(solution)/shard_map/ppermute | solution.py:225
  43.3 5.8 %collective-permute-start.5 = (f32[4,1024]{1,0:T(4,128)}, f32[4,1024]{1,0:T(4,128)S(1)}, u32[]{:S(2)}, u32[]{:S(2)}) collective-permute-start(f32[4,1024]{1,0:T(4,128)} %get-tuple-element.9), channel_id=1, source_target_pairs={{0,20},{1,21},{2,22},{3,23},{4,16},{5,17},{6,18},{7,19},{8,28},{9,... | collective-permute-start | bytes 49160 | tf_op jit(solution)/shard_map/ppermute | solution.py:225
  45.6 5.9 %copy-start.7 = (f32[4,1024]{1,0:T(4,128)S(1)}, f32[4,1024]{1,0:T(4,128)}, u32[]{:S(2)}) copy-start(f32[4,1024]{1,0:T(4,128)} %get-tuple-element.8) | copy-start | bytes 49156
  45.6 4.7 %collective-permute-start.7 = (f32[4,1024]{1,0:T(4,128)S(1)}, f32[4,1024]{1,0:T(4,128)S(1)}, u32[]{:S(2)}, u32[]{:S(2)}) collective-permute-start(f32[4,1024]{1,0:T(4,128)S(1)} %get-tuple-element.20), channel_id=1, source_target_pairs={{0,12},{1,29},{2,14},{3,31},{4,8},{5,25},{6,10},{7,27},{8,4},{9,21... | collective-permute-start | bytes 49160 | tf_op jit(solution)/shard_map/ppermute | solution.py:225
  46.0 4.3 %collective-permute-start.9 = (f32[4,1024]{1,0:T(4,128)S(1)}, f32[4,1024]{1,0:T(4,128)S(1)}, u32[]{:S(2)}, u32[]{:S(2)}) collective-permute-start(f32[4,1024]{1,0:T(4,128)S(1)} %get-tuple-element.21), channel_id=1, source_target_pairs={{0,8},{1,17},{2,10},{3,19},{4,12},{5,21},{6,14},{7,23},{8,0},{9,25... | collective-permute-start | bytes 49160 | tf_op jit(solution)/shard_map/ppermute | solution.py:225
  47.6 3.9 %collective-permute-start.8 = (f32[4,1024]{1,0:T(4,128)S(1)}, f32[4,1024]{1,0:T(4,128)S(1)}, u32[]{:S(2)}, u32[]{:S(2)}) collective-permute-start(f32[4,1024]{1,0:T(4,128)S(1)} %get-tuple-element.22), channel_id=1, source_target_pairs={{0,4},{1,25},{2,6},{3,27},{4,0},{5,29},{6,2},{7,31},{8,12},{9,17},... | collective-permute-start | bytes 49160 | tf_op jit(solution)/shard_map/ppermute | solution.py:225
  51.5 1.6 %collective-permute-start.10 = (f32[4,1024]{1,0:T(4,128)S(1)}, f32[4,1024]{1,0:T(4,128)S(1)}, u32[]{:S(2)}, u32[]{:S(2)}) collective-permute-start(f32[4,1024]{1,0:T(4,128)S(1)} %add_add_fusion), channel_id=1, source_target_pairs={{0,1},{1,0},{2,3},{3,2},{4,5},{5,4},{6,7},{7,6},{8,9},{9,8},{10,11... | collective-permute-start | bytes 49160 | tf_op jit(solution)/shard_map/ppermute | solution.py:225
  53.1 3.8 %collective-permute-start.11 = (f32[4,1024]{1,0:T(4,128)S(1)}, f32[4,1024]{1,0:T(4,128)S(1)}, u32[]{:S(2)}, u32[]{:S(2)}) collective-permute-start(f32[4,1024]{1,0:T(4,128)S(1)} %add.26), channel_id=1, source_target_pairs={{0,2},{1,3},{2,0},{3,1},{4,6},{5,7},{6,4},{7,5},{8,10},{9,11},{10,... | collective-permute-start | bytes 49160 | tf_op jit(solution)/shard_map/ppermute | solution.py:225
  55.6 1.3 %copy-start.4 = (f32[2,1024]{1,0:T(2,128)S(1)}, f32[2,1024]{1,0:T(2,128)}, u32[]{:S(2)}) copy-start(f32[2,1024]{1,0:T(2,128)} %param.6) | copy-start | bytes 24580
  55.6 1.3 %copy-start.5 = (f32[2,1024]{1,0:T(2,128)S(1)}, f32[2,1024]{1,0:T(2,128)}, u32[]{:S(2)}) copy-start(f32[2,1024]{1,0:T(2,128)} %param.5) | copy-start | bytes 24580
  56.9 0.7 %copy-start.6 = (f32[1024]{0:T(1024)S(1)}, f32[1024]{0:T(1024)}, u32[]{:S(2)}) copy-start(f32[1024]{0:T(1024)} %param.8) | copy-start | bytes 12292

commit v2 on v1

--- a/solution.py
+++ b/solution.py
@@ -10,7 +10,7 @@
 
 NPIX = 1024
 LANES = 128
-CHUNK = 256
+CHUNK = 1024
 TILES = CHUNK // LANES
 
 wave_scales = (1.2088, 1.0, 0.8953)
@@ -47,8 +47,9 @@
 
 
 def psf_kernel(sizes, own_ref, near_ref, far_ref, extra_ref, grad_ref, psf_ref, own_out, near_out, far_out, extra_out,
-               rays_s, row_base, col_base, steps, row_tab, col_tab, col_half, field, cot, sums):
+               rays_s, row_base, col_base, steps, sums, *tables):
     shards, local, plen, clen, half, pairs, norm = sizes
+    row_tab, col_tab, col_half, field, cot = [tables[3 * n : 3 * n + 3] for n in range(5)]
     x_mid = (lax.axis_index("pix") * plen).astype(jnp.float32) + (0.5 * plen - 0.5 * NPIX)
     y_low = (lax.axis_index("ray") * clen).astype(jnp.float32) + (0.5 - 0.5 * NPIX)
 
@@ -105,7 +106,8 @@
             steps[wave, 2, :, lanes] = eight[0]
             steps[wave, 3, :, lanes] = eight[1]
 
-    field[...] = jnp.zeros_like(field)
+    for wave in range(3):
+        field[wave][...] = jnp.zeros_like(field[wave])
 
     def where(chunk):
         return chunk // split, pl.ds(pl.multiple_of(lax.rem(chunk, split) * CHUNK, CHUNK), CHUNK)
@@ -126,12 +128,12 @@
                         both = jnp.concatenate(run[2 * pair : 2 * pair + 2], axis=0)
                         place16 = pl.ds(part * tall + 16 * pair, 16)
                         if is_row:
-                            row_tab[wave, chunk, place16, :] = both.astype(jnp.bfloat16)
+                            row_tab[wave][chunk, place16, :] = both.astype(jnp.bfloat16)
                         else:
-                            col_tab[wave, chunk, place16, :] = both
-                            col_half[wave, place16, :] = both.astype(jnp.bfloat16)
-            field[wave] += lax.dot_general(
-                col_half[wave], row_tab[wave, chunk], (((1,), (1,)), ((), ())), preferred_element_type=jnp.float32
+                            col_tab[wave][chunk, place16, :] = both
+                            col_half[wave][place16, :] = both.astype(jnp.bfloat16)
+            field[wave][...] += lax.dot_general(
+                col_half[wave][...], row_tab[wave][chunk], (((1,), (1,)), ((), ())), preferred_element_type=jnp.float32
             )
 
     offset = lax.broadcasted_iota(jnp.int32, (8, half), 1).astype(jnp.float32) + 0.5
@@ -139,8 +141,8 @@
         for group in range(clen // 8):
             rows = slice(8 * group, 8 * group + 8)
             low = slice(clen + 8 * group, clen + 8 * group + 8)
-            even_r, odd_r = field[wave, rows, :half], field[wave, rows, half:]
-            even_i, odd_i = field[wave, low, :half], field[wave, low, half:]
+            even_r, odd_r = field[wave][rows, :half], field[wave][rows, half:]
+            even_i, odd_i = field[wave][low, :half], field[wave][low, half:]
             up_r, up_i = even_r - odd_i, even_i + odd_r
             dn_r, dn_i = even_r + odd_i, even_i - odd_r
             psf_ref[wave, 0, rows, :] = dn_r * dn_r + dn_i * dn_i
@@ -159,8 +161,8 @@
                 ],
                 axis=0,
             )
-            cot[wave, 32 * group : 32 * group + 16, :] = plain.astype(jnp.bfloat16)
-            cot[wave, 32 * group + 16 : 32 * group + 32, :] = heavy.astype(jnp.bfloat16)
+            cot[wave][32 * group : 32 * group + 16, :] = plain.astype(jnp.bfloat16)
+            cot[wave][32 * group + 16 : 32 * group + 32, :] = heavy.astype(jnp.bfloat16)
 
     sub = lax.broadcasted_iota(jnp.int32, (8, CHUNK), 0).astype(jnp.float32)
     y_sub = sub + (y_low + clen)
@@ -171,15 +173,15 @@
         total = [jnp.zeros((8, CHUNK), jnp.float32) for _ in range(4)]
         for wave in range(3):
             scale = wave_scales[wave]
-            back = jnp.dot(cot[wave], row_tab[wave, chunk], preferred_element_type=jnp.float32)
+            back = jnp.dot(cot[wave][...], row_tab[wave][chunk], preferred_element_type=jnp.float32)
             im_sum = jnp.zeros((8, CHUNK), jnp.float32)
             up_sum = jnp.zeros((8, CHUNK), jnp.float32)
             re_sum = jnp.zeros((8, CHUNK), jnp.float32)
             x_sum = jnp.zeros((8, CHUNK), jnp.float32)
             for group in range(clen // 8):
                 e_r, e_i, f_r, f_i = [back[32 * group + 8 * n : 32 * group + 8 * n + 8] for n in range(4)]
-                b_r = col_tab[wave, chunk, 8 * group : 8 * group + 8, :]
-                b_i = col_tab[wave, chunk, clen + 8 * group : clen + 8 * group + 8, :]
+                b_r = col_tab[wave][chunk, 8 * group : 8 * group + 8, :]
+                b_i = col_tab[wave][chunk, clen + 8 * group : clen + 8 * group + 8, :]
                 im_sum = im_sum + (b_r * e_i - b_i * e_r)
                 re_sum = re_sum + (b_r * e_r + b_i * e_i)
                 x_sum = x_sum + (b_r * f_i - b_i * f_r)
@@ -253,12 +255,12 @@
             pltpu.VMEM((3, 2, local // LANES, 8 * shards, LANES), f32),
             pltpu.VMEM((3, 2, local // LANES, 8 * shards, LANES), f32),
             pltpu.VMEM((3, 4, shards, local), f32),
-            pltpu.VMEM((3, chunks, 2 * half, CHUNK), bf16),
-            pltpu.VMEM((3, chunks, 2 * clen, CHUNK), f32),
-            pltpu.VMEM((3, 2 * clen, CHUNK), bf16),
-            pltpu.VMEM((3, 2 * clen, 2 * half), f32),
-            pltpu.VMEM((3, 4 * clen, 2 * half), bf16),
             pltpu.VMEM((shards, 4, local), f32),
+            *[pltpu.VMEM((chunks, 2 * half, CHUNK), bf16)] * 3,
+            *[pltpu.VMEM((chunks, 2 * clen, CHUNK), f32)] * 3,
+            *[pltpu.VMEM((2 * clen, CHUNK), bf16)] * 3,
+            *[pltpu.VMEM((2 * clen, 2 * half), f32)] * 3,
+            *[pltpu.VMEM((4 * clen, 2 * half), bf16)] * 3,
         ],
         compiler_params=pltpu.CompilerParams(vmem_limit_bytes=62 * 1024 * 1024),
     )(rays, near, far, extra, weight)

time: 58.6 us -> 50.7 us (0.87)
  Pallas kernels: 26.3 us -> 18.4 us
    pallas_call x1, Pallas kernels: 26.3 us -> 18.4 us  [on_device(): pl.pallas_call(functools.partial(psf_kernel, sizes), out_shape=[jax.Shape...]
  transfers between devices with their start and end apart: 12 -> 12, of which waited for: 7 -> 7; matrix products, arithmetic and copies ran while one was open for 9% -> 11% of each run, Pallas kernels for 0% -> 0%
where the time goes in v2:
time: 50.7 us; the launch traced here: 50.4 us
  Pallas kernels  18.4 us (36%)
  starting transfers between devices  15.8 us (31%)
  waiting for transfers between devices  6.75 us (13%)
  local copies, waits for them, and re-layouts  6.25 us (12%)
  other arithmetic  2.46 us (5%)
  between operations  0.76 us (1%)
    pallas_call x1, Pallas kernels, on_device(): pl.pallas_call(functools.partial(psf_kernel, sizes), out_shape=[jax.Shape...  18.4 us
    ppermute x12, starting transfers between devices, swap(): return lax.ppermute(value, ('ray', 'pix'), moves)  15.8 us
    ppermute x12, waiting for transfers between devices, swap(): return lax.ppermute(value, ('ray', 'pix'), moves)  6.75 us
    unnamed x20, local copies, waits for them, and re-layouts  3.99 us
    slice x1, local copies, waits for them, and re-layouts, on_device(): weight[:, 0, ::-1]  1.05 us
  transfers between devices with their start and end apart: 12, of which 7 were waited for; matrix products, arithmetic and copies ran while one was open for 11% of the time, Pallas kernels for 0%

profile of v2, /device:TPU:0, one launch (start us, length us, event | category | flops | bytes accessed | tf_op | source)
XLA Modules:
  0.0 50.4 jit_solution(3402299175154531503)
XLA Ops:
  0.6 0.8 %pad_maximum_fusion.2.own_ref = f32[6,1024]{1,0:T(8,128)S(1)} fusion(f32[1,1024]{1,0:T(1,128)} %bitcast.28, f32[1,1024]{1,0:T(1,128)} %bitcast.31, f32[2,1024]{1,0:T(2,128)} %param.6, f32[2,1024]{1,0:T(2,128)} %param.5), kind=kLoop, calls=%fused_computation.5 | loop fusion | flops 18432 | bytes 49152 | tf_op jit(solution)/shard_map/concatenate | solution.py:211
  1.4 0.0 copy-start.1
  1.4 5.1 %collective-permute-start.4 = (f32[6,1024]{1,0:T(8,128)S(1)}, f32[6,1024]{1,0:T(8,128)S(1)}, u32[]{:S(2)}, u32[]{:S(2)}) collective-permute-start(f32[6,1024]{1,0:T(8,128)S(1)} %pad_maximum_fusion.2.own_ref), channel_id=1, source_target_pairs={{0,20},{1,21},{2,22},{3,23},{4,16},{5,17},{6,18},{7,19},{8,28},{9,... | collective-permute-start | bytes 73736 | tf_op jit(solution)/shard_map/ppermute | solution.py:227
  6.5 1.6 %collective-permute-start.2 = (f32[6,1024]{1,0:T(8,128)S(1)}, f32[6,1024]{1,0:T(8,128)S(1)}, u32[]{:S(2)}, u32[]{:S(2)}) collective-permute-start(f32[6,1024]{1,0:T(8,128)S(1)} %pad_maximum_fusion.2.own_ref), channel_id=1, source_target_pairs={{0,8},{1,17},{2,10},{3,19},{4,12},{5,21},{6,14},{7,23},{8,0},{9,25... | collective-permute-start | bytes 73736 | tf_op jit(solution)/shard_map/ppermute | solution.py:227
  8.0 0.5 %collective-permute-start.1 = (f32[6,1024]{1,0:T(8,128)S(1)}, f32[6,1024]{1,0:T(8,128)S(1)}, u32[]{:S(2)}, u32[]{:S(2)}) collective-permute-start(f32[6,1024]{1,0:T(8,128)S(1)} %pad_maximum_fusion.2.own_ref), channel_id=1, source_target_pairs={{0,4},{1,25},{2,6},{3,27},{4,0},{5,29},{6,2},{7,31},{8,12},{9,17},... | collective-permute-start | bytes 73736 | tf_op jit(solution)/shard_map/ppermute | solution.py:227
  8.6 1.4 %collective-permute-start = (f32[6,1024]{1,0:T(8,128)S(1)}, f32[6,1024]{1,0:T(8,128)S(1)}, u32[]{:S(2)}, u32[]{:S(2)}) collective-permute-start(f32[6,1024]{1,0:T(8,128)S(1)} %pad_maximum_fusion.2.own_ref), channel_id=1, source_target_pairs={{0,12},{1,29},{2,14},{3,31},{4,8},{5,25},{6,10},{7,27},{8,4},{9,21... | collective-permute-start | bytes 73736 | tf_op jit(solution)/shard_map/ppermute | solution.py:227
  10.0 1.0 %fusion.2 = (f32[3,1,128,128]{3,2,1,0:T(8,128)S(1)}, f32[3,1,128,128]{3,2,1,0:T(8,128)S(1)}) fusion(f32[3,2,128,128]{3,2,1,0:T(8,128)} %bitcast.23), kind=kLoop, calls=%fused_computation.16 | loop fusion | bytes 786432 | tf_op jit(solution)/shard_map/slice | solution.py:234
  11.0 0.0 copy-done.1
  11.0 0.1 copy.13
  11.2 0.3 rev.6
  11.4 0.1 copy.14
  11.6 0.0 collective-permute-done.2
  11.6 0.4 collective-permute-done.1
  12.0 1.4 %collective-permute-done = f32[6,1024]{1,0:T(8,128)S(1)} collective-permute-done((f32[6,1024]{1,0:T(8,128)S(1)}, f32[6,1024]{1,0:T(8,128)S(1)}, u32[]{:S(2)}, u32[]{:S(2)}) %collective-permute-start) | collective-permute-done | bytes 24608 | tf_op jit(solution)/shard_map/ppermute | solution.py:227
  13.4 0.0 copy-start
  13.4 1.6 %collective-permute-start.3 = (f32[3,6,1024]{2,1,0:T(8,128)S(1)}, f32[3,6,1024]{2,1,0:T(8,128)S(1)}, u32[]{:S(2)}, u32[]{:S(2)}) collective-permute-start(f32[3,6,1024]{2,1,0:T(8,128)S(1)} %pad_maximum_fusion.1.near_ref), channel_id=1, source_target_pairs={{0,1},{1,0},{2,3},{3,2},{4,5},{5,4},{6,7},{7,6},{8,9},{9,8},{10,11... | collective-permute-start | bytes 221192 | tf_op jit(solution)/shard_map/ppermute | solution.py:227
  15.0 0.8 %maximum_bitcast_fusion.grad_ref = f32[3,2,128,128]{3,2,1,0:T(8,128)} fusion(f32[3,1,128,128]{2,3,1,0:T(8,128)S(1)} %copy.14, f32[3,1,128,128]{2,3,1,0:T(8,128)S(1)} %rev.6), kind=kLoop, calls=%fused_computation | loop fusion | flops 98304 | bytes 786432 | tf_op jit(solution)/shard_map/transpose | solution.py:234
  15.7 0.0 copy-done
  15.7 0.0 collective-permute-done.4.extra_ref
  15.7 0.2 collective-permute-done.3.far_ref
  15.9 0.5 copy-done.3
  16.4 0.6 %copy-done.2 = f32[3,6,1024]{2,1,0:T(8,128)} copy-done((f32[3,6,1024]{2,1,0:T(8,128)}, f32[3,6,1024]{2,1,0:T(8,128)S(1)}, u32[]{:S(2)}) %copy-start.2) | copy-done | bytes 73752
  17.0 18.4 %shard_map.68 = (f32[3,2,128,128]{3,2,1,0:T(8,128)}, f32[4,1024]{1,0:T(4,128)}, f32[3,4,1024]{2,1,0:T(4,128)}, f32[3,4,1024]{2,1,0:T(4,128)}, f32[4,1024]{1,0:T(4,128)}) custom-call(f32[6,1024]{1,0:T(8,128)} %copy-done.1, f32[3,6,1024]{2,1,0:T(8,128)} %copy-done, f32[3,6,1024]{2,1,0:T(8,128)} %copy-done.2, f32[6,1024]{1,0:T(8,128)} %copy-done.3, ...), custom_call_target="tpu_custom_call" | custom-call | tf_op jit(solution)/shard_map/pallas_call | solution.py:242
  35.4 0.0 collective-permute-start.6
  35.4 0.3 collective-permute-start.5
  35.7 1.1 %collective-permute-done.6 = f32[3,4,1024]{2,1,0:T(4,128)S(1)} collective-permute-done((f32[3,4,1024]{2,1,0:T(4,128)}, f32[3,4,1024]{2,1,0:T(4,128)S(1)}, u32[]{:S(2)}, u32[]{:S(2)}) %collective-permute-start.6) | collective-permute-done | bytes 49184 | tf_op jit(solution)/shard_map/ppermute | solution.py:227
  36.8 0.8 %add.22 = f32[3,4,1024]{2,1,0:T(4,128)S(1)} add(f32[3,4,1024]{2,1,0:T(4,128)} %get-tuple-element.10, f32[3,4,1024]{2,1,0:T(4,128)S(1)} %collective-permute-done.6) | non-fusion elementwise | flops 12288 | bytes 147456 | tf_op jit(solution)/shard_map/add | solution.py:271
  37.6 0.0 copy-start.7
  37.7 0.4 collective-permute-start.7
  38.1 1.6 %collective-permute-start.9 = (f32[4,1024]{1,0:T(4,128)S(1)}, f32[4,1024]{1,0:T(4,128)S(1)}, u32[]{:S(2)}, u32[]{:S(2)}) collective-permute-start(f32[4,1024]{1,0:T(4,128)S(1)} %get-tuple-element.21), channel_id=1, source_target_pairs={{0,8},{1,17},{2,10},{3,19},{4,12},{5,21},{6,14},{7,23},{8,0},{9,25... | collective-permute-start | bytes 49160 | tf_op jit(solution)/shard_map/ppermute | solution.py:227
  39.7 1.5 %collective-permute-start.8 = (f32[4,1024]{1,0:T(4,128)S(1)}, f32[4,1024]{1,0:T(4,128)S(1)}, u32[]{:S(2)}, u32[]{:S(2)}) collective-permute-start(f32[4,1024]{1,0:T(4,128)S(1)} %get-tuple-element.22), channel_id=1, source_target_pairs={{0,4},{1,25},{2,6},{3,27},{4,0},{5,29},{6,2},{7,31},{8,12},{9,17},... | collective-permute-start | bytes 49160 | tf_op jit(solution)/shard_map/ppermute | solution.py:227
  41.2 0.0 collective-permute-done.5
  41.2 1.1 %collective-permute-done.7 = f32[4,1024]{1,0:T(4,128)S(1)} collective-permute-done((f32[4,1024]{1,0:T(4,128)S(1)}, f32[4,1024]{1,0:T(4,128)S(1)}, u32[]{:S(2)}, u32[]{:S(2)}) %collective-permute-start.7) | collective-permute-done | bytes 16416 | tf_op jit(solution)/shard_map/ppermute | solution.py:227
  42.4 0.0 collective-permute-done.9
  42.4 1.2 %collective-permute-done.8 = f32[4,1024]{1,0:T(4,128)S(1)} collective-permute-done((f32[4,1024]{1,0:T(4,128)S(1)}, f32[4,1024]{1,0:T(4,128)S(1)}, u32[]{:S(2)}, u32[]{:S(2)}) %collective-permute-start.8) | collective-permute-done | bytes 16416 | tf_op jit(solution)/shard_map/ppermute | solution.py:227
  43.6 0.0 copy-done.7
  43.6 0.2 collective-permute-start.10
  43.8 1.0 %slice_bitcast_fusion.1 = (f32[3,1,128,128]{2,3,0,1:T(8,128)S(1)}, f32[3,128,128]{1,2,0:T(8,128)S(1)}) fusion(f32[3,2,128,128]{2,3,1,0:T(8,128)} %bitcast.24), kind=kLoop, calls=%fused_computation.3 | loop fusion | bytes 786432
  44.9 0.3 rev.7
  45.2 0.0 collective-permute-done.10
  45.2 1.6 %collective-permute-start.11 = (f32[4,1024]{1,0:T(4,128)S(1)}, f32[4,1024]{1,0:T(4,128)S(1)}, u32[]{:S(2)}, u32[]{:S(2)}) collective-permute-start(f32[4,1024]{1,0:T(4,128)S(1)} %add.26), channel_id=1, source_target_pairs={{0,2},{1,3},{2,0},{3,1},{4,6},{5,7},{6,4},{7,5},{8,10},{9,11},{10,... | collective-permute-start | bytes 49160 | tf_op jit(solution)/shard_map/ppermute | solution.py:227
  46.8 0.9 %copy.12 = f32[3,256,128]{2,1,0:T(8,128)} copy(f32[3,256,128]{1,2,0:T(8,128)S(1)} %pad_maximum_fusion) | data formatting | bytes 786432
  47.7 1.3 %collective-permute-done.11 = f32[4,1024]{1,0:T(4,128)S(1)} collective-permute-done((f32[4,1024]{1,0:T(4,128)S(1)}, f32[4,1024]{1,0:T(4,128)S(1)}, u32[]{:S(2)}, u32[]{:S(2)}) %collective-permute-start.11) | collective-permute-done | bytes 16416 | tf_op jit(solution)/shard_map/ppermute | solution.py:227
  49.0 0.0 copy-done.4
  49.0 0.0 copy-done.5
  49.0 0.0 copy-start.6
  49.1 0.6 %copy-done.6 = f32[1024]{0:T(1024)S(1)} copy-done((f32[1024]{0:T(1024)S(1)}, f32[1024]{0:T(1024)}, u32[]{:S(2)}) %copy-start.6) | copy-done | bytes 4120
  49.7 0.7 %stack.31 = f32[6,1024]{1,0:T(8,128)} concatenate(f32[1,1024]{1,0:T(1,128)S(1)} %get-tuple-element.31, f32[1,1024]{1,0:T(1,128)S(1)} %get-tuple-element.29, f32[1,1024]{1,0:T(1,128)S(1)} %get-tuple-element.30, f32[1,1024]{1,0:T(1,128)S(1)} %get-tuple-element.24, f32[1,1024]{1,0:T(1,128)S(1)} %get-tuple-element.23, f32[1,1024]{1,0:T(1,128)S(1)} %bitcast.30), dimensions={0} | concatenate | bytes 49152 | tf_op jit(solution)/shard_map/stack | solution.py:281
  (12 shorter events, 0.1 us)
Async XLA Ops:
  1.4 9.6 %copy-start.1 = (f32[6,1024]{1,0:T(8,128)}, f32[6,1024]{1,0:T(8,128)S(1)}, u32[]{:S(2)}) copy-start(f32[6,1024]{1,0:T(8,128)S(1)} %pad_maximum_fusion.2.own_ref) | copy-start | bytes 73732
  1.4 14.3 %collective-permute-start.4 = (f32[6,1024]{1,0:T(8,128)S(1)}, f32[6,1024]{1,0:T(8,128)S(1)}, u32[]{:S(2)}, u32[]{:S(2)}) collective-permute-start(f32[6,1024]{1,0:T(8,128)S(1)} %pad_maximum_fusion.2.own_ref), channel_id=1, source_target_pairs={{0,20},{1,21},{2,22},{3,23},{4,16},{5,17},{6,18},{7,19},{8,28},{9,... | collective-permute-start | bytes 73736 | tf_op jit(solution)/shard_map/ppermute | solution.py:227
  6.5 5.1 %collective-permute-start.2 = (f32[6,1024]{1,0:T(8,128)S(1)}, f32[6,1024]{1,0:T(8,128)S(1)}, u32[]{:S(2)}, u32[]{:S(2)}) collective-permute-start(f32[6,1024]{1,0:T(8,128)S(1)} %pad_maximum_fusion.2.own_ref), channel_id=1, source_target_pairs={{0,8},{1,17},{2,10},{3,19},{4,12},{5,21},{6,14},{7,23},{8,0},{9,25... | collective-permute-start | bytes 73736 | tf_op jit(solution)/shard_map/ppermute | solution.py:227
  8.0 3.9 %collective-permute-start.1 = (f32[6,1024]{1,0:T(8,128)S(1)}, f32[6,1024]{1,0:T(8,128)S(1)}, u32[]{:S(2)}, u32[]{:S(2)}) collective-permute-start(f32[6,1024]{1,0:T(8,128)S(1)} %pad_maximum_fusion.2.own_ref), channel_id=1, source_target_pairs={{0,4},{1,25},{2,6},{3,27},{4,0},{5,29},{6,2},{7,31},{8,12},{9,17},... | collective-permute-start | bytes 73736 | tf_op jit(solution)/shard_map/ppermute | solution.py:227
  8.6 4.8 %collective-permute-start = (f32[6,1024]{1,0:T(8,128)S(1)}, f32[6,1024]{1,0:T(8,128)S(1)}, u32[]{:S(2)}, u32[]{:S(2)}) collective-permute-start(f32[6,1024]{1,0:T(8,128)S(1)} %pad_maximum_fusion.2.own_ref), channel_id=1, source_target_pairs={{0,12},{1,29},{2,14},{3,31},{4,8},{5,25},{6,10},{7,27},{8,4},{9,21... | collective-permute-start | bytes 73736 | tf_op jit(solution)/shard_map/ppermute | solution.py:227
  13.4 2.3 %copy-start = (f32[3,6,1024]{2,1,0:T(8,128)}, f32[3,6,1024]{2,1,0:T(8,128)S(1)}, u32[]{:S(2)}) copy-start(f32[3,6,1024]{2,1,0:T(8,128)S(1)} %pad_maximum_fusion.1.near_ref) | copy-start | bytes 221188
  13.4 2.5 %collective-permute-start.3 = (f32[3,6,1024]{2,1,0:T(8,128)S(1)}, f32[3,6,1024]{2,1,0:T(8,128)S(1)}, u32[]{:S(2)}, u32[]{:S(2)}) collective-permute-start(f32[3,6,1024]{2,1,0:T(8,128)S(1)} %pad_maximum_fusion.1.near_ref), channel_id=1, source_target_pairs={{0,1},{1,0},{2,3},{3,2},{4,5},{5,4},{6,7},{7,6},{8,9},{9,8},{10,11... | collective-permute-start | bytes 221192 | tf_op jit(solution)/shard_map/ppermute | solution.py:227
  15.7 0.6 %copy-start.3 = (f32[6,1024]{1,0:T(8,128)}, f32[6,1024]{1,0:T(8,128)S(1)}, u32[]{:S(2)}) copy-start(f32[6,1024]{1,0:T(8,128)S(1)} %collective-permute-done.4.extra_ref) | copy-start | bytes 73732
  16.4 0.6 %copy-start.2 = (f32[3,6,1024]{2,1,0:T(8,128)}, f32[3,6,1024]{2,1,0:T(8,128)S(1)}, u32[]{:S(2)}) copy-start(f32[3,6,1024]{2,1,0:T(8,128)S(1)} %collective-permute-done.3.far_ref) | copy-start | bytes 221188
  35.4 1.4 %collective-permute-start.6 = (f32[3,4,1024]{2,1,0:T(4,128)}, f32[3,4,1024]{2,1,0:T(4,128)S(1)}, u32[]{:S(2)}, u32[]{:S(2)}) collective-permute-start(f32[3,4,1024]{2,1,0:T(4,128)} %get-tuple-element.11), channel_id=1, source_target_pairs={{0,1},{1,0},{2,3},{3,2},{4,5},{5,4},{6,7},{7,6},{8,9},{9,8},{10,11... | collective-permute-start | bytes 147464 | tf_op jit(solution)/shard_map/ppermute | solution.py:227
  35.4 5.8 %collective-permute-start.5 = (f32[4,1024]{1,0:T(4,128)}, f32[4,1024]{1,0:T(4,128)S(1)}, u32[]{:S(2)}, u32[]{:S(2)}) collective-permute-start(f32[4,1024]{1,0:T(4,128)} %get-tuple-element.9), channel_id=1, source_target_pairs={{0,20},{1,21},{2,22},{3,23},{4,16},{5,17},{6,18},{7,19},{8,28},{9,... | collective-permute-start | bytes 49160 | tf_op jit(solution)/shard_map/ppermute | solution.py:227
  37.6 5.9 %copy-start.7 = (f32[4,1024]{1,0:T(4,128)S(1)}, f32[4,1024]{1,0:T(4,128)}, u32[]{:S(2)}) copy-start(f32[4,1024]{1,0:T(4,128)} %get-tuple-element.8) | copy-start | bytes 49156
  37.7 4.7 %collective-permute-start.7 = (f32[4,1024]{1,0:T(4,128)S(1)}, f32[4,1024]{1,0:T(4,128)S(1)}, u32[]{:S(2)}, u32[]{:S(2)}) collective-permute-start(f32[4,1024]{1,0:T(4,128)S(1)} %get-tuple-element.20), channel_id=1, source_target_pairs={{0,12},{1,29},{2,14},{3,31},{4,8},{5,25},{6,10},{7,27},{8,4},{9,21... | collective-permute-start | bytes 49160 | tf_op jit(solution)/shard_map/ppermute | solution.py:227
  38.1 4.3 %collective-permute-start.9 = (f32[4,1024]{1,0:T(4,128)S(1)}, f32[4,1024]{1,0:T(4,128)S(1)}, u32[]{:S(2)}, u32[]{:S(2)}) collective-permute-start(f32[4,1024]{1,0:T(4,128)S(1)} %get-tuple-element.21), channel_id=1, source_target_pairs={{0,8},{1,17},{2,10},{3,19},{4,12},{5,21},{6,14},{7,23},{8,0},{9,25... | collective-permute-start | bytes 49160 | tf_op jit(solution)/shard_map/ppermute | solution.py:227
  39.7 3.9 %collective-permute-start.8 = (f32[4,1024]{1,0:T(4,128)S(1)}, f32[4,1024]{1,0:T(4,128)S(1)}, u32[]{:S(2)}, u32[]{:S(2)}) collective-permute-start(f32[4,1024]{1,0:T(4,128)S(1)} %get-tuple-element.22), channel_id=1, source_target_pairs={{0,4},{1,25},{2,6},{3,27},{4,0},{5,29},{6,2},{7,31},{8,12},{9,17},... | collective-permute-start | bytes 49160 | tf_op jit(solution)/shard_map/ppermute | solution.py:227
  43.6 1.6 %collective-permute-start.10 = (f32[4,1024]{1,0:T(4,128)S(1)}, f32[4,1024]{1,0:T(4,128)S(1)}, u32[]{:S(2)}, u32[]{:S(2)}) collective-permute-start(f32[4,1024]{1,0:T(4,128)S(1)} %add_add_fusion), channel_id=1, source_target_pairs={{0,1},{1,0},{2,3},{3,2},{4,5},{5,4},{6,7},{7,6},{8,9},{9,8},{10,11... | collective-permute-start | bytes 49160 | tf_op jit(solution)/shard_map/ppermute | solution.py:227
  45.2 3.8 %collective-permute-start.11 = (f32[4,1024]{1,0:T(4,128)S(1)}, f32[4,1024]{1,0:T(4,128)S(1)}, u32[]{:S(2)}, u32[]{:S(2)}) collective-permute-start(f32[4,1024]{1,0:T(4,128)S(1)} %add.26), channel_id=1, source_target_pairs={{0,2},{1,3},{2,0},{3,1},{4,6},{5,7},{6,4},{7,5},{8,10},{9,11},{10,... | collective-permute-start | bytes 49160 | tf_op jit(solution)/shard_map/ppermute | solution.py:227
  47.7 1.3 %copy-start.4 = (f32[2,1024]{1,0:T(2,128)S(1)}, f32[2,1024]{1,0:T(2,128)}, u32[]{:S(2)}) copy-start(f32[2,1024]{1,0:T(2,128)} %param.6) | copy-start | bytes 24580
  47.7 1.3 %copy-start.5 = (f32[2,1024]{1,0:T(2,128)S(1)}, f32[2,1024]{1,0:T(2,128)}, u32[]{:S(2)}) copy-start(f32[2,1024]{1,0:T(2,128)} %param.5) | copy-start | bytes 24580
  49.0 0.7 %copy-start.6 = (f32[1024]{0:T(1024)S(1)}, f32[1024]{0:T(1024)}, u32[]{:S(2)}) copy-start(f32[1024]{0:T(1024)} %param.8) | copy-start | bytes 12292

commit v3 on v2

v3 whole, which is shorter than its diff:
```python
import functools
import math

import jax
import jax.numpy as jnp
from jax import lax
from jax.experimental import pallas as pl
from jax.experimental.pallas import tpu as pltpu
from jax.sharding import PartitionSpec as P

NPIX = 1024
LANES = 128

wave_scales = (1.2088, 1.0, 0.8953)
two_pi = 2.0 * math.pi
sin_terms = [(-1.0) ** n / math.factorial(2 * n + 1) * (0.5 * math.pi) ** (2 * n + 1) for n in range(5)]
cos_terms = [(-1.0) ** n / math.factorial(2 * n) * (0.5 * math.pi) ** (2 * n) for n in range(6)]


def horner(square, terms):
    value = terms[-1]
    for term in terms[-2::-1]:
        value = value * square + term
    return value


def circle(turns):
    rest = turns - jnp.floor(turns + 0.5)
    square = rest * rest
    sin = rest * horner(square, sin_terms)
    cos = horner(square, cos_terms)
    sin, cos = 2.0 * sin * cos, 1.0 - 2.0 * sin * sin
    return 1.0 - 2.0 * sin * sin, 2.0 * sin * cos


def times(left, right):
    return (left[0] * right[0] - left[1] * right[1], left[0] * right[1] + left[1] * right[0])


def ladder(first, second, twice, count):
    out = [first, second]
    while len(out) < count:
        out.append(twice * out[-1] - out[-2])
    return out[:count]


def climb(first, second, twice, count):
    re = ladder(first[0], second[0], twice, count)
    im = ladder(first[1], second[1], twice, count)
    return list(zip(re, im))


def psf_kernel(sizes, *refs):
    count = sizes[0]
    ray_refs, grad_ref, psf_ref, sum_refs = refs[:count], refs[count], refs[count + 1], refs[count + 2 : 2 * count + 2]
    (rays_s, dense, row_fine, row_wide, col_base, col_step, grad_s, psf_s, cot_t, sums, ray_sem, grad_sem, psf_sem,
     *tables) = refs[2 * count + 2 :]
    shards, local, plen, clen, wides, norm = sizes
    wide_clen = max(clen, LANES)
    tiles = local // LANES
    row_tab, col_tab, col_half, field, cot = [tables[3 * n : 3 * n + 3] for n in range(5)]

    loads = []

    def load(source, slot):
        loads.append(pltpu.make_async_copy(source, rays_s.at[slot], ray_sem.at[slot]))
        loads[-1].start()

    for slot in range(shards):
        load(ray_refs[slot], slot)
    grad_load = pltpu.make_async_copy(grad_ref, grad_s, grad_sem)
    grad_load.start()

    x_mid = (lax.axis_index("pix") * plen).astype(jnp.float32) + (0.5 * plen - 0.5 * NPIX)
    y_low = (lax.axis_index("ray") * clen).astype(jnp.float32) + (0.5 - 0.5 * NPIX)
    for wave in range(3):
        field[wave][...] = jnp.zeros_like(field[wave])
        if wide_clen > clen:
            col_half[wave][...] = jnp.zeros_like(col_half[wave])
    for slot, copy in enumerate(loads):
        copy.wait()
        for tile in range(tiles):
            for item in range(4):
                dense[item, tile, slot : slot + 1, :] = rays_s[slot, tile, item : item + 1, :]

    @pl.loop(0, tiles)
    def _(tile):
        path, dir_l, dir_m, amp = [dense[item, tile] for item in range(4)]
        phase = path + (dir_l * x_mid + dir_m * y_low)
        amp = amp * norm

        def spread(base, values):
            for sub, value in enumerate(values):
                for part in range(2):
                    base[wave, part, tile, pl.ds(sub, shards, stride=8), :] = value[part]

        for wave in range(3):
            scale = wave_scales[wave]
            first = circle((0.5 * scale) * dir_l)
            step = times(first, first)
            spread(row_fine, climb(first, times(first, step), 2.0 * step[0], 8))
            first = circle((8.0 * scale) * dir_l)
            step = times(first, first)
            spread(row_wide, climb(first, times(first, step), 2.0 * step[0], wides))
            cos, sin = circle(scale * phase)
            first = (amp * cos, amp * sin)
            step = circle(scale * dir_m)
            spread(col_base, climb(first, times(first, step), 2.0 * step[0], 8))
            step = circle((8.0 * scale) * dir_m)
            for index, value in enumerate((step[0], step[1], 2.0 * step[0])):
                col_step[wave, index, tile, :shards, :] = value

    @pl.loop(0, shards)
    def _(shard):
        rows8 = pl.ds(pl.multiple_of(shard * 8, 8), 8)
        for wave in range(3):
            def whole(ref, *index):
                return jnp.concatenate([ref[(wave, index[0], tile) + index[1:]] for tile in range(tiles)], axis=1)

            every = slice(None)
            fine = [whole(row_fine, part, rows8, every) for part in range(2)]
            for pair in range(wides // 2):
                wide = [[whole(row_wide, part, pl.ds(shard * 8 + 2 * pair + n, 8, stride=0), every) for n in range(2)] for part in range(2)]
                for wide_part, fine_part, block in ((0, 0, 0), (1, 1, 1), (1, 0, 2), (0, 1, 3)):
                    both = [wide[wide_part][n] * fine[fine_part] for n in range(2)]
                    rows16 = slice(8 * wides * block + 16 * pair, 8 * wides * block + 16 * pair + 16)
                    row_tab[wave][shard, rows16, :] = jnp.concatenate(both, axis=0).astype(jnp.bfloat16)
            step = [whole(col_step, index, pl.ds(shard, 8, stride=0), every) for index in range(3)]
            first = [whole(col_base, part, rows8, every) for part in range(2)]
            second = times(first, step)
            for part in range(2):
                run = ladder(first[part], second[part], step[2], clen // 8)
                for pair in range(clen // 16):
                    both = jnp.concatenate(run[2 * pair : 2 * pair + 2], axis=0)
                    rows16 = slice(part * clen + 16 * pair, part * clen + 16 * pair + 16)
                    col_tab[wave][shard, rows16, :] = both
                    low = part * wide_clen + 16 * pair
                    col_half[wave][low : low + 16, :] = both.astype(jnp.bfloat16)
            field[wave][...] += lax.dot_general(
                row_tab[wave][shard], col_half[wave][...], (((1,), (1,)), ((), ())), preferred_element_type=jnp.float32
            )

    sub8 = lax.broadcasted_iota(jnp.int32, (8, wide_clen), 0)
    fine_row = sub8.astype(jnp.float32) + 0.5
    mid = plen // 2

    def flip(value):
        return jnp.take_along_axis(value, 7 - sub8, axis=0)

    grad_load.wait()
    for wave in range(3):
        for wide in range(wides):
            parts = []
            for side in (slice(0, wide_clen), slice(wide_clen, 2 * wide_clen)):
                parts.append([field[wave][8 * (wides * block + wide) : 8 * (wides * block + wide) + 8, side] for block in range(4)])
            (cc_r, ss_r, sc_r, cs_r), (cc_i, ss_i, sc_i, cs_i) = parts
            lines = []
            for sign in (1, -1):
                if sign == 1:
                    even_r, even_i, odd_r, odd_i = cc_r - ss_r, cc_i - ss_i, sc_r + cs_r, sc_i + cs_i
                    up_row, dn_row = mid + 16 * wide + 8, mid - 16 * wide - 16
                    offset = (16.0 * wide + 8.0) + fine_row
                else:
                    even_r, even_i, odd_r, odd_i = cc_r + ss_r, cc_i + ss_i, sc_r - cs_r, sc_i - cs_i
                    up_row, dn_row = mid + 16 * wide, mid - 16 * wide - 8
                    offset = (16.0 * wide + 8.0) - fine_row
                up_r, up_i = even_r - odd_i, even_i + odd_r
                dn_r, dn_i = even_r + odd_i, even_i - odd_r
                up_rows, dn_rows = slice(up_row, up_row + 8), slice(dn_row, dn_row + 8)
                up, dn = up_r * up_r + up_i * up_i, dn_r * dn_r + dn_i * dn_i
                g_up, g_dn = grad_s[wave, up_rows, :], grad_s[wave, dn_rows, :]
                if sign == 1:
                    dn, g_dn = flip(dn), flip(g_dn)
                else:
                    up, g_up = flip(up), flip(g_up)
                psf_s[wave, up_rows, :] = up
                psf_s[wave, dn_rows, :] = dn
                dn_r, dn_i, up_r, up_i = g_dn * dn_r, g_dn * dn_i, g_up * up_r, g_up * up_i
                p_r, p_i, m_r, m_i = up_r + dn_r, up_i + dn_i, up_r - dn_r, up_i - dn_i
                lines.append(
                    ((p_r, m_i), (p_i, -m_r), (offset * m_r, offset * p_i), (offset * m_i, -(offset * p_r)))
                )
            for kind in range(4):
                (cos_p, sin_p), (cos_m, sin_m) = lines[0][kind], lines[1][kind]
                for block, value in enumerate((cos_p + cos_m, cos_m - cos_p, sin_p + sin_m, sin_p - sin_m)):
                    cot_t[kind, 8 * (wides * block + wide) : 8 * (wides * block + wide) + 8, :] = value
        flat = [cot_t[kind].T for kind in range(4)]
        for group in range(clen // 8):
            rows = slice(8 * group, 8 * group + 8)
            for pair in range(2):
                both = jnp.concatenate([flat[2 * pair][rows], flat[2 * pair + 1][rows]], axis=0)
                cot[wave][32 * group + 16 * pair : 32 * group + 16 * pair + 16, :] = both.astype(jnp.bfloat16)
    psf_store = pltpu.make_async_copy(psf_s, psf_ref, psf_sem)
    psf_store.start()

    sub = lax.broadcasted_iota(jnp.int32, (8, local), 0).astype(jnp.float32)
    y_sub = sub + (y_low + clen)

    @pl.loop(0, shards)
    def _(shard):
        total = [jnp.zeros((8, local), jnp.float32) for _ in range(4)]
        for wave in range(3):
            scale = 2.0 * wave_scales[wave]
            back = jnp.dot(cot[wave][...], row_tab[wave][shard], preferred_element_type=jnp.float32)
            im_sum = jnp.zeros((8, local), jnp.float32)
            up_sum = jnp.zeros((8, local), jnp.float32)
            re_sum = jnp.zeros((8, local), jnp.float32)
            x_sum = jnp.zeros((8, local), jnp.float32)
            for group in range(clen // 8):
                e_r, e_i, f_r, f_i = [back[32 * group + 8 * n : 32 * group + 8 * n + 8] for n in range(4)]
                b_r = col_tab[wave][shard, 8 * group : 8 * group + 8, :]
                b_i = col_tab[wave][shard, clen + 8 * group : clen + 8 * group + 8, :]
                im_sum = im_sum + (b_r * e_i - b_i * e_r)
                re_sum = re_sum + (b_r * e_r + b_i * e_i)
                x_sum = x_sum + (b_r * f_i - b_i * f_r)
                up_sum = up_sum + im_sum
            total[0] = total[0] + scale * im_sum
            total[1] = total[1] + (scale * two_pi) * (x_mid * im_sum + x_sum)
            total[2] = total[2] + (scale * two_pi) * (y_sub * im_sum - 8.0 * up_sum)
            total[3] = total[3] + 2.0 * re_sum
        rows = [jnp.sum(value, axis=0, keepdims=True) for value in total]
        sums[shard] = jnp.concatenate(rows, axis=0)

    for slot in range(shards):
        sum_refs[slot][...] = sums[slot]
    psf_store.wait()


def split_pairs(shards):
    if shards == 8:
        return ((2, 7), (4, 5), (3, 6)), 1
    pairs = (shards - 2) // 2
    return tuple((1 + n, 1 + pairs + n) for n in range(pairs)), shards - 1


def on_device(positions, directions, path, amplitude, psf_grad):
    x, y, dir_l, dir_m = positions[0], positions[1], directions[0], directions[1]
    local = path.shape[0]
    tiles = local // LANES
    shards = lax.axis_size("ray")
    rows = lax.axis_size("pix")
    plen = NPIX // rows
    clen = NPIX // shards
    wides = plen // 32
    wide_clen = max(clen, LANES)
    norm = 1.0 / math.sqrt(local * shards)
    pairs, last = split_pairs(shards)
    count = len(pairs)

    def swap(value, ray_even, ray_odd, pix=0):
        moves = []
        for r in range(shards):
            for p in range(rows):
                moves.append((r * rows + p, (r ^ (ray_odd if p % 2 else ray_even)) * rows + (p ^ pix)))
        return lax.ppermute(value, ("ray", "pix"), moves)

    fixed = path * (1.0 / two_pi) - (dir_l * x + dir_m * y)
    packed = jnp.stack([fixed, dir_l, dir_m, amplitude]).reshape(4, tiles, LANES).transpose(1, 0, 2)
    near = [swap(packed, even, odd) for even, odd in pairs]
    extra = swap(packed, last, last)
    far = [swap(part, 0, 0, 1) for part in near]

    weight = jnp.pad(psf_grad, ((0, 0), (0, 0), (0, wide_clen - clen))) if wide_clen > clen else psf_grad
    sizes = (shards, local, plen, clen, wides, norm)
    f32, bf16 = jnp.float32, jnp.bfloat16
    vmem = pl.BlockSpec(memory_space=pltpu.VMEM)
    anywhere = pl.BlockSpec(memory_space=pltpu.HBM)
    psf, *parts = pl.pallas_call(
        functools.partial(psf_kernel, sizes),
        out_shape=[jax.ShapeDtypeStruct((3, plen, wide_clen), f32)] + [jax.ShapeDtypeStruct((4, local), f32)] * shards,
        in_specs=[anywhere] * (shards + 1),
        out_specs=[anywhere] + [vmem] * shards,
        scratch_shapes=[
            pltpu.VMEM((shards, tiles, 4, LANES), f32),
            pltpu.VMEM((4, tiles, shards, LANES), f32),
            pltpu.VMEM((3, 2, tiles, 8 * shards, LANES), f32),
            pltpu.VMEM((3, 2, tiles, 8 * shards + 8, LANES), f32),
            pltpu.VMEM((3, 2, tiles, 8 * shards, LANES), f32),
            pltpu.VMEM((3, 3, tiles, shards + 8, LANES), f32),
            pltpu.VMEM((3, plen, wide_clen), f32),
            pltpu.VMEM((3, plen, wide_clen), f32),
            pltpu.VMEM((4, 32 * wides, wide_clen), f32),
            pltpu.VMEM((shards, 4, local), f32),
            pltpu.SemaphoreType.DMA((shards,)),
            pltpu.SemaphoreType.DMA,
            pltpu.SemaphoreType.DMA,
            *[pltpu.VMEM((shards, 32 * wides, local), bf16)] * 3,
            *[pltpu.VMEM((shards, 2 * clen, local), f32)] * 3,
            *[pltpu.VMEM((2 * wide_clen, local), bf16)] * 3,
            *[pltpu.VMEM((32 * wides, 2 * wide_clen), f32)] * 3,
            *[pltpu.VMEM((4 * clen, 32 * wides), bf16)] * 3,
        ],
        compiler_params=pltpu.CompilerParams(vmem_limit_bytes=62 * 1024 * 1024),
    )(packed, *near, *far, extra, weight)

    psf = psf[..., :clen]

    own_sum, near_sum, far_sum, extra_sum = parts[0], parts[1 : 1 + count], parts[1 + count : 1 + 2 * count], parts[-1]
    near_sum = [near + swap(far, 0, 0, 1) for near, far in zip(near_sum, far_sum)]
    total = own_sum + swap(extra_sum, last, last)
    for part, (even, odd) in zip(near_sum, pairs):
        total = total + swap(part, even, odd)
    bit = 1
    while bit < rows:
        total = total + swap(total, 0, 0, bit)
        bit *= 2
    s1, s2, s3, s4 = total
    grads = jnp.stack(
        [
            s1,
            -two_pi * dir_l * s1,
            -two_pi * dir_m * s1,
            (s2 - two_pi * x * s1) / NPIX,
            (s3 - two_pi * y * s1) / NPIX,
            s4 / amplitude,
        ]
    )
    return (psf, grads)


def solution(mesh):
    in_specs = (P(None, "ray"), P(None, "ray"), P("ray"), P("ray"), P(None, "pix", "ray"))
    out_specs = (P(None, "pix", "ray"), P(None, "ray"))
    return jax.shard_map(on_device, mesh=mesh, in_specs=in_specs, out_specs=out_specs, check_vma=False)
```

time: 50.7 us -> 48.2 us (0.951)
  local copies, waits for them, and re-layouts: 6.25 us -> 1.98 us
  waiting for transfers between devices: 6.75 us -> 9.24 us
  other arithmetic: 2.46 us -> 1.63 us
  Pallas kernels: 18.4 us -> 17.7 us
  starting transfers between devices: 15.8 us -> 16.4 us
    unnamed x20 -> x30, local copies, waits for them, and re-layouts: 3.99 us -> 1.32 us
    ppermute x12 -> x16, waiting for transfers between devices: 6.75 us -> 9.24 us  [swap(): return lax.ppermute(value, ('ray', 'pix'), moves)]
    slice x1 -> x0, local copies, waits for them, and re-layouts: 1.05 us -> none  [on_device(): weight[:, 0, ::-1]]
    concatenate x2 -> x0, other arithmetic: 0.8 us -> none  [the longest x1 0.77 us: on_device(): jnp.concatenate([positions, directions, path[None], amplitude[None]], axi...]
    transpose x1, other arithmetic: 0.77 us -> 0.02 us  [on_device(): jnp.stack([fixed, dir_l, dir_m, amplitude]).reshape(4, tiles, LANES)]
    add x4 -> x7, other arithmetic: 0.84 us -> 1.56 us  [the longest x1 0.79 us: on_device(): fixed = path * (1.0 / two_pi) - (dir_l * x + dir_m * y)]
    pallas_call x1, Pallas kernels: 18.4 us -> 17.7 us  [on_device(): pl.pallas_call(functools.partial(psf_kernel, sizes), out_shape=[jax.Shape...]
    ppermute x12 -> x16, starting transfers between devices: 15.8 us -> 16.4 us  [swap(): return lax.ppermute(value, ('ray', 'pix'), moves)]
  transfers between devices with their start and end apart: 12 -> 16, of which waited for: 7 -> 8; matrix products, arithmetic and copies ran while one was open for 11% -> 2% of each run, Pallas kernels for 0% -> 0%
where the time goes in v3:
time: 48.2 us; the launch traced here: 47.7 us
  Pallas kernels  17.7 us (37%)
  starting transfers between devices  16.4 us (34%)
  waiting for transfers between devices  9.24 us (19%)
  local copies, waits for them, and re-layouts  1.98 us (4%)
  other arithmetic  1.63 us (3%)
  between operations  0.8 us (2%)
    pallas_call x1, Pallas kernels, on_device(): pl.pallas_call(functools.partial(psf_kernel, sizes), out_shape=[jax.Shape...  17.7 us
    ppermute x16, starting transfers between devices, swap(): return lax.ppermute(value, ('ray', 'pix'), moves)  16.4 us
    ppermute x16, waiting for transfers between devices, swap(): return lax.ppermute(value, ('ray', 'pix'), moves)  9.24 us
    unnamed x30, local copies, waits for them, and re-layouts  1.32 us
  transfers between devices with their start and end apart: 16, of which 8 were waited for; matrix products, arithmetic and copies ran while one was open for 2% of the time, Pallas kernels for 0%

profile of v3, /device:TPU:0, one launch (start us, length us, event | category | flops | bytes accessed | tf_op | source)
XLA Modules:
  0.0 47.7 jit_solution(3043300861106155031)
XLA Ops:
  0.6 0.0 copy-start.14
  0.6 0.8 %multiply_add_fusion = f32[1,1024]{1,0:T(1,128)S(1)} fusion(f32[2,1024]{1,0:T(2,128)} %param.5, f32[2,1024]{1,0:T(2,128)} %param.6), kind=kLoop, calls=%fused_computation.8 | loop fusion | flops 3072 | bytes 20480 | tf_op jit(solution)/shard_map/add | solution.py:257
  1.4 0.0 copy-done.14
  1.4 0.0 copy-start
  1.5 0.0 copy-start.13
  1.5 0.7 %copy-done = f32[2,1024]{1,0:T(2,128)S(1)} copy-done((f32[2,1024]{1,0:T(2,128)S(1)}, f32[2,1024]{1,0:T(2,128)}, u32[]{:S(2)}) %copy-start) | copy-done | bytes 8216
  2.1 0.0 copy-done.13
  2.2 0.0 copy-start.1
  2.2 4.0 %collective-permute-start.2 = (f32[8,4,128]{2,1,0:T(4,128)S(1)}, f32[8,4,128]{2,1,0:T(4,128)S(1)}, u32[]{:S(2)}, u32[]{:S(2)}) collective-permute-start(f32[8,4,128]{2,1,0:T(4,128)S(1)} %maximum_bitcast_fusion.refs_0_), channel_id=1, source_target_pairs={{0,12},{1,25},{2,14},{3,27},{4,8},{5,29},{6,10},{7,31},{8,4},{9,17... | collective-permute-start | bytes 49160 | tf_op jit(solution)/shard_map/ppermute | solution.py:255
  6.2 2.6 %collective-permute-start.1 = (f32[8,4,128]{2,1,0:T(4,128)S(1)}, f32[8,4,128]{2,1,0:T(4,128)S(1)}, u32[]{:S(2)}, u32[]{:S(2)}) collective-permute-start(f32[8,4,128]{2,1,0:T(4,128)S(1)} %maximum_bitcast_fusion.refs_0_), channel_id=1, source_target_pairs={{0,16},{1,21},{2,18},{3,23},{4,20},{5,17},{6,22},{7,19},{8,24},{9,... | collective-permute-start | bytes 49160 | tf_op jit(solution)/shard_map/ppermute | solution.py:255
  8.8 0.4 collective-permute-start
  9.3 0.5 %collective-permute-start.6 = (f32[8,4,128]{2,1,0:T(4,128)S(1)}, f32[8,4,128]{2,1,0:T(4,128)S(1)}, u32[]{:S(2)}, u32[]{:S(2)}) collective-permute-start(f32[8,4,128]{2,1,0:T(4,128)S(1)} %maximum_bitcast_fusion.refs_0_), channel_id=1, source_target_pairs={{0,4},{1,5},{2,6},{3,7},{4,0},{5,1},{6,2},{7,3},{8,12},{9,13},{10,... | collective-permute-start | bytes 49160 | tf_op jit(solution)/shard_map/ppermute | solution.py:255
  9.8 0.0 collective-permute-done.2.refs_3_
  9.8 0.6 %collective-permute-start.5 = (f32[8,4,128]{2,1,0:T(4,128)S(1)}, f32[8,4,128]{2,1,0:T(4,128)S(1)}, u32[]{:S(2)}, u32[]{:S(2)}) collective-permute-start(f32[8,4,128]{2,1,0:T(4,128)S(1)} %collective-permute-done.2.refs_3_), channel_id=1, source_target_pairs={{0,1},{1,0},{2,3},{3,2},{4,5},{5,4},{6,7},{7,6},{8,9},{9,8},{10,11... | collective-permute-start | bytes 49160 | tf_op jit(solution)/shard_map/ppermute | solution.py:255
  10.4 0.6 %collective-permute-done.1.refs_2_ = f32[8,4,128]{2,1,0:T(4,128)S(1)} collective-permute-done((f32[8,4,128]{2,1,0:T(4,128)S(1)}, f32[8,4,128]{2,1,0:T(4,128)S(1)}, u32[]{:S(2)}, u32[]{:S(2)}) %collective-permute-start.1) | collective-permute-done | bytes 16416 | tf_op jit(solution)/shard_map/ppermute | solution.py:255
  11.0 0.3 collective-permute-start.4
  11.2 1.4 %collective-permute-done.refs_1_ = f32[8,4,128]{2,1,0:T(4,128)S(1)} collective-permute-done((f32[8,4,128]{2,1,0:T(4,128)S(1)}, f32[8,4,128]{2,1,0:T(4,128)S(1)}, u32[]{:S(2)}, u32[]{:S(2)}) %collective-permute-start) | collective-permute-done | bytes 16416 | tf_op jit(solution)/shard_map/ppermute | solution.py:255
  12.7 0.0 collective-permute-start.3
  12.7 0.4 collective-permute-done.6.refs_7_
  13.0 0.0 collective-permute-done.5.refs_6_
  13.0 0.0 collective-permute-done.4.refs_5_
  13.0 0.0 copy-start.10
  13.0 0.8 %collective-permute-done.3.refs_4_ = f32[8,4,128]{2,1,0:T(4,128)S(1)} collective-permute-done((f32[8,4,128]{2,1,0:T(4,128)S(1)}, f32[8,4,128]{2,1,0:T(4,128)S(1)}, u32[]{:S(2)}, u32[]{:S(2)}) %collective-permute-start.3) | collective-permute-done | bytes 16416 | tf_op jit(solution)/shard_map/ppermute | solution.py:255
  13.8 0.0 copy-done.1
  13.8 0.0 copy-done.3
  13.8 0.0 copy-done.5
  13.9 0.6 %copy-done.11 = f32[8,4,128]{2,1,0:T(4,128)} copy-done((f32[8,4,128]{2,1,0:T(4,128)}, f32[8,4,128]{2,1,0:T(4,128)S(1)}, u32[]{:S(2)}) %copy-start.11) | copy-done | bytes 16408
  14.5 17.7 %shard_map.68 = (f32[3,256,128]{2,1,0:T(8,128)}, f32[4,1024]{1,0:T(4,128)}, f32[4,1024]{1,0:T(4,128)}, f32[4,1024]{1,0:T(4,128)}, f32[4,1024]{1,0:T(4,128)}, /*i...) custom-call(f32[8,4,128]{2,1,0:T(4,128)} %copy-done.1, f32[8,4,128]{2,1,0:T(4,128)} %copy-done.6, ...), custom_call_target="tpu_custom_call" | custom-call | tf_op jit(solution)/shard_map/pallas_call | solution.py:268
  32.2 0.2 collective-permute-start.8
  32.4 0.3 collective-permute-start.10
  32.7 0.2 collective-permute-start.12
  32.9 1.1 %collective-permute-start.7 = (f32[4,1024]{1,0:T(4,128)}, f32[4,1024]{1,0:T(4,128)S(1)}, u32[]{:S(2)}, u32[]{:S(2)}) collective-permute-start(f32[4,1024]{1,0:T(4,128)} %get-tuple-element.13), channel_id=1, source_target_pairs={{0,4},{1,5},{2,6},{3,7},{4,0},{5,1},{6,2},{7,3},{8,12},{9,13},{10,... | collective-permute-start | bytes 49160 | tf_op jit(solution)/shard_map/ppermute | solution.py:255
  34.0 0.0 collective-permute-done.8
  34.0 0.7 %add.36 = f32[4,1024]{1,0:T(4,128)S(1)} add(f32[4,1024]{1,0:T(4,128)} %get-tuple-element.14, f32[4,1024]{1,0:T(4,128)S(1)} %collective-permute-done.8) | non-fusion elementwise | flops 4096 | bytes 49152 | tf_op jit(solution)/shard_map/add | solution.py:299
  34.7 1.0 %collective-permute-start.9 = (f32[4,1024]{1,0:T(4,128)S(1)}, f32[4,1024]{1,0:T(4,128)S(1)}, u32[]{:S(2)}, u32[]{:S(2)}) collective-permute-start(f32[4,1024]{1,0:T(4,128)S(1)} %add.36), channel_id=1, source_target_pairs={{0,8},{1,29},{2,10},{3,31},{4,12},{5,25},{6,14},{7,27},{8,0},{9,21... | collective-permute-start | bytes 49160 | tf_op jit(solution)/shard_map/ppermute | solution.py:255
  35.7 0.0 collective-permute-done.10
  35.7 1.1 %collective-permute-start.11 = (f32[4,1024]{1,0:T(4,128)S(1)}, f32[4,1024]{1,0:T(4,128)S(1)}, u32[]{:S(2)}, u32[]{:S(2)}) collective-permute-start(f32[4,1024]{1,0:T(4,128)S(1)} %add.38), channel_id=1, source_target_pairs={{0,16},{1,21},{2,18},{3,23},{4,20},{5,17},{6,22},{7,19},{8,24},{9,... | collective-permute-start | bytes 49160 | tf_op jit(solution)/shard_map/ppermute | solution.py:255
  36.8 0.0 collective-permute-done.12
  36.8 1.9 %collective-permute-start.13 = (f32[4,1024]{1,0:T(4,128)S(1)}, f32[4,1024]{1,0:T(4,128)S(1)}, u32[]{:S(2)}, u32[]{:S(2)}) collective-permute-start(f32[4,1024]{1,0:T(4,128)S(1)} %add.40), channel_id=1, source_target_pairs={{0,12},{1,25},{2,14},{3,27},{4,8},{5,29},{6,10},{7,31},{8,4},{9,17... | collective-permute-start | bytes 49160 | tf_op jit(solution)/shard_map/ppermute | solution.py:255
  38.7 0.0 collective-permute-done.7
  38.7 0.0 collective-permute-done.9
  38.7 1.8 %collective-permute-done.11 = f32[4,1024]{1,0:T(4,128)S(1)} collective-permute-done((f32[4,1024]{1,0:T(4,128)S(1)}, f32[4,1024]{1,0:T(4,128)S(1)}, u32[]{:S(2)}, u32[]{:S(2)}) %collective-permute-start.11) | collective-permute-done | bytes 16416 | tf_op jit(solution)/shard_map/ppermute | solution.py:255
  40.5 1.2 %collective-permute-done.13 = f32[4,1024]{1,0:T(4,128)S(1)} collective-permute-done((f32[4,1024]{1,0:T(4,128)S(1)}, f32[4,1024]{1,0:T(4,128)S(1)}, u32[]{:S(2)}, u32[]{:S(2)}) %collective-permute-start.13) | collective-permute-done | bytes 16416 | tf_op jit(solution)/shard_map/ppermute | solution.py:255
  41.7 0.6 %collective-permute-start.14 = (f32[4,1024]{1,0:T(4,128)S(1)}, f32[4,1024]{1,0:T(4,128)S(1)}, u32[]{:S(2)}, u32[]{:S(2)}) collective-permute-start(f32[4,1024]{1,0:T(4,128)S(1)} %add_add_fusion), channel_id=1, source_target_pairs={{0,1},{1,0},{2,3},{3,2},{4,5},{5,4},{6,7},{7,6},{8,9},{9,8},{10,11... | collective-permute-start | bytes 49160 | tf_op jit(solution)/shard_map/ppermute | solution.py:255
  42.3 0.8 %collective-permute-done.14 = f32[4,1024]{1,0:T(4,128)S(1)} collective-permute-done((f32[4,1024]{1,0:T(4,128)S(1)}, f32[4,1024]{1,0:T(4,128)S(1)}, u32[]{:S(2)}, u32[]{:S(2)}) %collective-permute-start.14) | collective-permute-done | bytes 16416 | tf_op jit(solution)/shard_map/ppermute | solution.py:255
  43.2 1.5 %collective-permute-start.15 = (f32[4,1024]{1,0:T(4,128)S(1)}, f32[4,1024]{1,0:T(4,128)S(1)}, u32[]{:S(2)}, u32[]{:S(2)}) collective-permute-start(f32[4,1024]{1,0:T(4,128)S(1)} %add.42), channel_id=1, source_target_pairs={{0,2},{1,3},{2,0},{3,1},{4,6},{5,7},{6,4},{7,5},{8,10},{9,11},{10,... | collective-permute-start | bytes 49160 | tf_op jit(solution)/shard_map/ppermute | solution.py:255
  44.7 2.3 %collective-permute-done.15 = f32[4,1024]{1,0:T(4,128)S(1)} collective-permute-done((f32[4,1024]{1,0:T(4,128)S(1)}, f32[4,1024]{1,0:T(4,128)S(1)}, u32[]{:S(2)}, u32[]{:S(2)}) %collective-permute-start.15) | collective-permute-done | bytes 16416 | tf_op jit(solution)/shard_map/ppermute | solution.py:255
  47.0 0.7 %stack.27 = f32[6,1024]{1,0:T(8,128)} concatenate(f32[1,1024]{1,0:T(1,128)S(1)} %get-tuple-element.28, f32[1,1024]{1,0:T(1,128)S(1)} %get-tuple-element.26, f32[1,1024]{1,0:T(1,128)S(1)} %get-tuple-element.27, f32[1,1024]{1,0:T(1,128)S(1)} %get-tuple-element.21, f32[1,1024]{1,0:T(1,128)S(1)} %get-tuple-element.20, f32[1,1024]{1,0:T(1,128)S(1)} %bitcast.10), dimensions={0} | concatenate | bytes 49152 | tf_op jit(solution)/shard_map/stack | solution.py:308
  (27 shorter events, 0.1 us)
Async XLA Ops:
  0.6 0.8 %copy-start.14 = (f32[1024]{0:T(1024)S(1)}, f32[1024]{0:T(1024)}, u32[]{:S(2)}) copy-start(f32[1024]{0:T(1024)} %param.7) | copy-start | bytes 12292
  1.4 0.7 %copy-start = (f32[2,1024]{1,0:T(2,128)S(1)}, f32[2,1024]{1,0:T(2,128)}, u32[]{:S(2)}) copy-start(f32[2,1024]{1,0:T(2,128)} %param.6) | copy-start | bytes 24580
  1.5 0.7 %copy-start.13 = (f32[1024]{0:T(1024)S(1)}, f32[1024]{0:T(1024)}, u32[]{:S(2)}) copy-start(f32[1024]{0:T(1024)} %param.8) | copy-start | bytes 12292
  2.2 11.7 %copy-start.1 = (f32[8,4,128]{2,1,0:T(4,128)}, f32[8,4,128]{2,1,0:T(4,128)S(1)}, u32[]{:S(2)}) copy-start(f32[8,4,128]{2,1,0:T(4,128)S(1)} %maximum_bitcast_fusion.refs_0_) | copy-start | bytes 49156
  2.2 7.6 %collective-permute-start.2 = (f32[8,4,128]{2,1,0:T(4,128)S(1)}, f32[8,4,128]{2,1,0:T(4,128)S(1)}, u32[]{:S(2)}, u32[]{:S(2)}) collective-permute-start(f32[8,4,128]{2,1,0:T(4,128)S(1)} %maximum_bitcast_fusion.refs_0_), channel_id=1, source_target_pairs={{0,12},{1,25},{2,14},{3,27},{4,8},{5,29},{6,10},{7,31},{8,4},{9,17... | collective-permute-start | bytes 49160 | tf_op jit(solution)/shard_map/ppermute | solution.py:255
  6.2 4.7 %collective-permute-start.1 = (f32[8,4,128]{2,1,0:T(4,128)S(1)}, f32[8,4,128]{2,1,0:T(4,128)S(1)}, u32[]{:S(2)}, u32[]{:S(2)}) collective-permute-start(f32[8,4,128]{2,1,0:T(4,128)S(1)} %maximum_bitcast_fusion.refs_0_), channel_id=1, source_target_pairs={{0,16},{1,21},{2,18},{3,23},{4,20},{5,17},{6,22},{7,19},{8,24},{9,... | collective-permute-start | bytes 49160 | tf_op jit(solution)/shard_map/ppermute | solution.py:255
  8.8 3.8 %collective-permute-start = (f32[8,4,128]{2,1,0:T(4,128)S(1)}, f32[8,4,128]{2,1,0:T(4,128)S(1)}, u32[]{:S(2)}, u32[]{:S(2)}) collective-permute-start(f32[8,4,128]{2,1,0:T(4,128)S(1)} %maximum_bitcast_fusion.refs_0_), channel_id=1, source_target_pairs={{0,8},{1,29},{2,10},{3,31},{4,12},{5,25},{6,14},{7,27},{8,0},{9,21... | collective-permute-start | bytes 49160 | tf_op jit(solution)/shard_map/ppermute | solution.py:255
  9.3 3.7 %collective-permute-start.6 = (f32[8,4,128]{2,1,0:T(4,128)S(1)}, f32[8,4,128]{2,1,0:T(4,128)S(1)}, u32[]{:S(2)}, u32[]{:S(2)}) collective-permute-start(f32[8,4,128]{2,1,0:T(4,128)S(1)} %maximum_bitcast_fusion.refs_0_), channel_id=1, source_target_pairs={{0,4},{1,5},{2,6},{3,7},{4,0},{5,1},{6,2},{7,3},{8,12},{9,13},{10,... | collective-permute-start | bytes 49160 | tf_op jit(solution)/shard_map/ppermute | solution.py:255
  9.8 4.1 %copy-start.3 = (f32[8,4,128]{2,1,0:T(4,128)}, f32[8,4,128]{2,1,0:T(4,128)S(1)}, u32[]{:S(2)}) copy-start(f32[8,4,128]{2,1,0:T(4,128)S(1)} %collective-permute-done.2.refs_3_) | copy-start | bytes 49156
  9.8 3.2 %collective-permute-start.5 = (f32[8,4,128]{2,1,0:T(4,128)S(1)}, f32[8,4,128]{2,1,0:T(4,128)S(1)}, u32[]{:S(2)}, u32[]{:S(2)}) collective-permute-start(f32[8,4,128]{2,1,0:T(4,128)S(1)} %collective-permute-done.2.refs_3_), channel_id=1, source_target_pairs={{0,1},{1,0},{2,3},{3,2},{4,5},{5,4},{6,7},{7,6},{8,9},{9,8},{10,11... | collective-permute-start | bytes 49160 | tf_op jit(solution)/shard_map/ppermute | solution.py:255
  10.9 2.9 %copy-start.5 = (f32[8,4,128]{2,1,0:T(4,128)}, f32[8,4,128]{2,1,0:T(4,128)S(1)}, u32[]{:S(2)}) copy-start(f32[8,4,128]{2,1,0:T(4,128)S(1)} %collective-permute-done.1.refs_2_) | copy-start | bytes 49156
  11.0 2.1 %collective-permute-start.4 = (f32[8,4,128]{2,1,0:T(4,128)S(1)}, f32[8,4,128]{2,1,0:T(4,128)S(1)}, u32[]{:S(2)}, u32[]{:S(2)}) collective-permute-start(f32[8,4,128]{2,1,0:T(4,128)S(1)} %collective-permute-done.1.refs_2_), channel_id=1, source_target_pairs={{0,1},{1,0},{2,3},{3,2},{4,5},{5,4},{6,7},{7,6},{8,9},{9,8},{10,11... | collective-permute-start | bytes 49160 | tf_op jit(solution)/shard_map/ppermute | solution.py:255
  12.7 1.2 %copy-start.6 = (f32[8,4,128]{2,1,0:T(4,128)}, f32[8,4,128]{2,1,0:T(4,128)S(1)}, u32[]{:S(2)}) copy-start(f32[8,4,128]{2,1,0:T(4,128)S(1)} %collective-permute-done.refs_1_) | copy-start | bytes 49156
  12.7 1.2 %collective-permute-start.3 = (f32[8,4,128]{2,1,0:T(4,128)S(1)}, f32[8,4,128]{2,1,0:T(4,128)S(1)}, u32[]{:S(2)}, u32[]{:S(2)}) collective-permute-start(f32[8,4,128]{2,1,0:T(4,128)S(1)} %collective-permute-done.refs_1_), channel_id=1, source_target_pairs={{0,1},{1,0},{2,3},{3,2},{4,5},{5,4},{6,7},{7,6},{8,9},{9,8},{10,11... | collective-permute-start | bytes 49160 | tf_op jit(solution)/shard_map/ppermute | solution.py:255
  13.0 0.8 %copy-start.7 = (f32[8,4,128]{2,1,0:T(4,128)}, f32[8,4,128]{2,1,0:T(4,128)S(1)}, u32[]{:S(2)}) copy-start(f32[8,4,128]{2,1,0:T(4,128)S(1)} %collective-permute-done.6.refs_7_) | copy-start | bytes 49156
  13.0 0.9 %copy-start.9 = (f32[8,4,128]{2,1,0:T(4,128)}, f32[8,4,128]{2,1,0:T(4,128)S(1)}, u32[]{:S(2)}) copy-start(f32[8,4,128]{2,1,0:T(4,128)S(1)} %collective-permute-done.5.refs_6_) | copy-start | bytes 49156
  13.0 0.9 %copy-start.10 = (f32[8,4,128]{2,1,0:T(4,128)}, f32[8,4,128]{2,1,0:T(4,128)S(1)}, u32[]{:S(2)}) copy-start(f32[8,4,128]{2,1,0:T(4,128)S(1)} %collective-permute-done.4.refs_5_) | copy-start | bytes 49156
  13.9 0.6 %copy-start.11 = (f32[8,4,128]{2,1,0:T(4,128)}, f32[8,4,128]{2,1,0:T(4,128)S(1)}, u32[]{:S(2)}) copy-start(f32[8,4,128]{2,1,0:T(4,128)S(1)} %collective-permute-done.3.refs_4_) | copy-start | bytes 49156
  32.2 1.8 %collective-permute-start.8 = (f32[4,1024]{1,0:T(4,128)}, f32[4,1024]{1,0:T(4,128)S(1)}, u32[]{:S(2)}, u32[]{:S(2)}) collective-permute-start(f32[4,1024]{1,0:T(4,128)} %get-tuple-element.15), channel_id=1, source_target_pairs={{0,1},{1,0},{2,3},{3,2},{4,5},{5,4},{6,7},{7,6},{8,9},{9,8},{10,11... | collective-permute-start | bytes 49160 | tf_op jit(solution)/shard_map/ppermute | solution.py:255
  32.4 3.3 %collective-permute-start.10 = (f32[4,1024]{1,0:T(4,128)}, f32[4,1024]{1,0:T(4,128)S(1)}, u32[]{:S(2)}, u32[]{:S(2)}) collective-permute-start(f32[4,1024]{1,0:T(4,128)} %get-tuple-element.17), channel_id=1, source_target_pairs={{0,1},{1,0},{2,3},{3,2},{4,5},{5,4},{6,7},{7,6},{8,9},{9,8},{10,11... | collective-permute-start | bytes 49160 | tf_op jit(solution)/shard_map/ppermute | solution.py:255
  32.7 4.0 %collective-permute-start.12 = (f32[4,1024]{1,0:T(4,128)}, f32[4,1024]{1,0:T(4,128)S(1)}, u32[]{:S(2)}, u32[]{:S(2)}) collective-permute-start(f32[4,1024]{1,0:T(4,128)} %get-tuple-element.19), channel_id=1, source_target_pairs={{0,1},{1,0},{2,3},{3,2},{4,5},{5,4},{6,7},{7,6},{8,9},{9,8},{10,11... | collective-permute-start | bytes 49160 | tf_op jit(solution)/shard_map/ppermute | solution.py:255
  32.9 5.8 %collective-permute-start.7 = (f32[4,1024]{1,0:T(4,128)}, f32[4,1024]{1,0:T(4,128)S(1)}, u32[]{:S(2)}, u32[]{:S(2)}) collective-permute-start(f32[4,1024]{1,0:T(4,128)} %get-tuple-element.13), channel_id=1, source_target_pairs={{0,4},{1,5},{2,6},{3,7},{4,0},{5,1},{6,2},{7,3},{8,12},{9,13},{10,... | collective-permute-start | bytes 49160 | tf_op jit(solution)/shard_map/ppermute | solution.py:255
  34.0 1.7 %copy-start.8 = (f32[4,1024]{1,0:T(4,128)S(1)}, f32[4,1024]{1,0:T(4,128)}, u32[]{:S(2)}) copy-start(f32[4,1024]{1,0:T(4,128)} %get-tuple-element.16) | copy-start | bytes 49156
  34.7 4.0 %collective-permute-start.9 = (f32[4,1024]{1,0:T(4,128)S(1)}, f32[4,1024]{1,0:T(4,128)S(1)}, u32[]{:S(2)}, u32[]{:S(2)}) collective-permute-start(f32[4,1024]{1,0:T(4,128)S(1)} %add.36), channel_id=1, source_target_pairs={{0,8},{1,29},{2,10},{3,31},{4,12},{5,25},{6,14},{7,27},{8,0},{9,21... | collective-permute-start | bytes 49160 | tf_op jit(solution)/shard_map/ppermute | solution.py:255
  35.7 1.1 %copy-start.4 = (f32[4,1024]{1,0:T(4,128)S(1)}, f32[4,1024]{1,0:T(4,128)}, u32[]{:S(2)}) copy-start(f32[4,1024]{1,0:T(4,128)} %get-tuple-element.18) | copy-start | bytes 49156
  35.7 4.7 %collective-permute-start.11 = (f32[4,1024]{1,0:T(4,128)S(1)}, f32[4,1024]{1,0:T(4,128)S(1)}, u32[]{:S(2)}, u32[]{:S(2)}) collective-permute-start(f32[4,1024]{1,0:T(4,128)S(1)} %add.38), channel_id=1, source_target_pairs={{0,16},{1,21},{2,18},{3,23},{4,20},{5,17},{6,22},{7,19},{8,24},{9,... | collective-permute-start | bytes 49160 | tf_op jit(solution)/shard_map/ppermute | solution.py:255
  36.8 4.9 %copy-start.12 = (f32[4,1024]{1,0:T(4,128)S(1)}, f32[4,1024]{1,0:T(4,128)}, u32[]{:S(2)}) copy-start(f32[4,1024]{1,0:T(4,128)} %get-tuple-element.12) | copy-start | bytes 49156
  36.8 4.8 %collective-permute-start.13 = (f32[4,1024]{1,0:T(4,128)S(1)}, f32[4,1024]{1,0:T(4,128)S(1)}, u32[]{:S(2)}, u32[]{:S(2)}) collective-permute-start(f32[4,1024]{1,0:T(4,128)S(1)} %add.40), channel_id=1, source_target_pairs={{0,12},{1,25},{2,14},{3,27},{4,8},{5,29},{6,10},{7,31},{8,4},{9,17... | collective-permute-start | bytes 49160 | tf_op jit(solution)/shard_map/ppermute | solution.py:255
  41.7 1.5 %collective-permute-start.14 = (f32[4,1024]{1,0:T(4,128)S(1)}, f32[4,1024]{1,0:T(4,128)S(1)}, u32[]{:S(2)}, u32[]{:S(2)}) collective-permute-start(f32[4,1024]{1,0:T(4,128)S(1)} %add_add_fusion), channel_id=1, source_target_pairs={{0,1},{1,0},{2,3},{3,2},{4,5},{5,4},{6,7},{7,6},{8,9},{9,8},{10,11... | collective-permute-start | bytes 49160 | tf_op jit(solution)/shard_map/ppermute | solution.py:255
  43.2 3.8 %copy-start.2 = (f32[2,1024]{1,0:T(2,128)S(1)}, f32[2,1024]{1,0:T(2,128)}, u32[]{:S(2)}) copy-start(f32[2,1024]{1,0:T(2,128)} %param.5) | copy-start | bytes 24580
  43.2 3.8 %collective-permute-start.15 = (f32[4,1024]{1,0:T(4,128)S(1)}, f32[4,1024]{1,0:T(4,128)S(1)}, u32[]{:S(2)}, u32[]{:S(2)}) collective-permute-start(f32[4,1024]{1,0:T(4,128)S(1)} %add.42), channel_id=1, source_target_pairs={{0,2},{1,3},{2,0},{3,1},{4,6},{5,7},{6,4},{7,5},{8,10},{9,11},{10,... | collective-permute-start | bytes 49160 | tf_op jit(solution)/shard_map/ppermute | solution.py:255

commit v4 on v3

--- a/solution.py
+++ b/solution.py
@@ -83,7 +83,7 @@
             for item in range(4):
                 dense[item, tile, slot : slot + 1, :] = rays_s[slot, tile, item : item + 1, :]
 
-    @pl.loop(0, tiles)
+    @pl.loop(0, tiles, unroll=True)
     def _(tile):
         path, dir_l, dir_m, amp = [dense[item, tile] for item in range(4)]
         phase = path + (dir_l * x_mid + dir_m * y_low)
@@ -228,7 +228,7 @@
 
 def split_pairs(shards):
     if shards == 8:
-        return ((2, 7), (4, 5), (3, 6)), 1
+        return ((3, 7), (4, 5), (1, 6)), 2
     pairs = (shards - 2) // 2
     return tuple((1 + n, 1 + pairs + n) for n in range(pairs)), shards - 1
 
@@ -300,10 +300,10 @@
     total = own_sum + swap(extra_sum, last, last)
     for part, (even, odd) in zip(near_sum, pairs):
         total = total + swap(part, even, odd)
-    bit = 1
-    while bit < rows:
+    bit = rows // 2
+    while bit:
         total = total + swap(total, 0, 0, bit)
-        bit *= 2
+        bit //= 2
     s1, s2, s3, s4 = total
     grads = jnp.stack(
         [

time: 48.2 us -> 47.4 us (0.983)
  waiting for transfers between devices: 9.24 us -> 8.42 us
    ppermute x16, waiting for transfers between devices: 9.24 us -> 8.42 us  [swap(): return lax.ppermute(value, ('ray', 'pix'), moves)]
  transfers between devices with their start and end apart: 16 -> 16, of which waited for: 8 -> 7; matrix products, arithmetic and copies ran while one was open for 2% -> 2% of each run, Pallas kernels for 0% -> 0%
where the time goes in v4:
time: 47.4 us; the launch traced here: 46.8 us
  Pallas kernels  17.6 us (37%)
  starting transfers between devices  16.2 us (34%)
  waiting for transfers between devices  8.42 us (18%)
  local copies, waits for them, and re-layouts  2.15 us (5%)
  other arithmetic  1.63 us (3%)
  between operations  0.8 us (2%)
    pallas_call x1, Pallas kernels, on_device(): pl.pallas_call(functools.partial(psf_kernel, sizes), out_shape=[jax.Shape...  17.6 us
    ppermute x16, starting transfers between devices, swap(): return lax.ppermute(value, ('ray', 'pix'), moves)  16.2 us
    ppermute x16, waiting for transfers between devices, swap(): return lax.ppermute(value, ('ray', 'pix'), moves)  8.42 us
    unnamed x30, local copies, waits for them, and re-layouts  1.49 us
  transfers between devices with their start and end apart: 16, of which 7 were waited for; matrix products, arithmetic and copies ran while one was open for 2% of the time, Pallas kernels for 0%

profile of v4, /device:TPU:0, one launch (start us, length us, event | category | flops | bytes accessed | tf_op | source)
XLA Modules:
  0.0 46.8 jit_solution(15638447905054071845)
XLA Ops:
  0.6 0.0 copy-start.14
  0.6 0.8 %multiply_add_fusion = f32[1,1024]{1,0:T(1,128)S(1)} fusion(f32[2,1024]{1,0:T(2,128)} %param.5, f32[2,1024]{1,0:T(2,128)} %param.6), kind=kLoop, calls=%fused_computation.8 | loop fusion | flops 3072 | bytes 20480 | tf_op jit(solution)/shard_map/add | solution.py:257
  1.4 0.0 copy-done.14
  1.4 0.0 copy-start
  1.5 0.0 copy-start.13
  1.5 0.7 %copy-done = f32[2,1024]{1,0:T(2,128)S(1)} copy-done((f32[2,1024]{1,0:T(2,128)S(1)}, f32[2,1024]{1,0:T(2,128)}, u32[]{:S(2)}) %copy-start) | copy-done | bytes 8216
  2.1 0.0 copy-done.13
  2.2 0.0 copy-start.1
  2.2 3.0 %collective-permute-start.2 = (f32[8,4,128]{2,1,0:T(4,128)S(1)}, f32[8,4,128]{2,1,0:T(4,128)S(1)}, u32[]{:S(2)}, u32[]{:S(2)}) collective-permute-start(f32[8,4,128]{2,1,0:T(4,128)S(1)} %maximum_bitcast_fusion.refs_0_), channel_id=1, source_target_pairs={{0,4},{1,25},{2,6},{3,27},{4,0},{5,29},{6,2},{7,31},{8,12},{9,17},... | collective-permute-start | bytes 49160 | tf_op jit(solution)/shard_map/ppermute | solution.py:255
  5.2 2.6 %collective-permute-start.1 = (f32[8,4,128]{2,1,0:T(4,128)S(1)}, f32[8,4,128]{2,1,0:T(4,128)S(1)}, u32[]{:S(2)}, u32[]{:S(2)}) collective-permute-start(f32[8,4,128]{2,1,0:T(4,128)S(1)} %maximum_bitcast_fusion.refs_0_), channel_id=1, source_target_pairs={{0,16},{1,21},{2,18},{3,23},{4,20},{5,17},{6,22},{7,19},{8,24},{9,... | collective-permute-start | bytes 49160 | tf_op jit(solution)/shard_map/ppermute | solution.py:255
  7.8 1.5 %collective-permute-start = (f32[8,4,128]{2,1,0:T(4,128)S(1)}, f32[8,4,128]{2,1,0:T(4,128)S(1)}, u32[]{:S(2)}, u32[]{:S(2)}) collective-permute-start(f32[8,4,128]{2,1,0:T(4,128)S(1)} %maximum_bitcast_fusion.refs_0_), channel_id=1, source_target_pairs={{0,12},{1,29},{2,14},{3,31},{4,8},{5,25},{6,10},{7,27},{8,4},{9,21... | collective-permute-start | bytes 49160 | tf_op jit(solution)/shard_map/ppermute | solution.py:255
  9.3 0.4 collective-permute-start.6
  9.8 0.0 collective-permute-done.2.refs_3_
  9.8 0.6 %collective-permute-start.5 = (f32[8,4,128]{2,1,0:T(4,128)S(1)}, f32[8,4,128]{2,1,0:T(4,128)S(1)}, u32[]{:S(2)}, u32[]{:S(2)}) collective-permute-start(f32[8,4,128]{2,1,0:T(4,128)S(1)} %collective-permute-done.2.refs_3_), channel_id=1, source_target_pairs={{0,1},{1,0},{2,3},{3,2},{4,5},{5,4},{6,7},{7,6},{8,9},{9,8},{10,11... | collective-permute-start | bytes 49160 | tf_op jit(solution)/shard_map/ppermute | solution.py:255
  10.4 0.0 collective-permute-done.1.refs_2_
  10.4 0.8 %collective-permute-start.4 = (f32[8,4,128]{2,1,0:T(4,128)S(1)}, f32[8,4,128]{2,1,0:T(4,128)S(1)}, u32[]{:S(2)}, u32[]{:S(2)}) collective-permute-start(f32[8,4,128]{2,1,0:T(4,128)S(1)} %collective-permute-done.1.refs_2_), channel_id=1, source_target_pairs={{0,1},{1,0},{2,3},{3,2},{4,5},{5,4},{6,7},{7,6},{8,9},{9,8},{10,11... | collective-permute-start | bytes 49160 | tf_op jit(solution)/shard_map/ppermute | solution.py:255
  11.2 1.4 %collective-permute-done.refs_1_ = f32[8,4,128]{2,1,0:T(4,128)S(1)} collective-permute-done((f32[8,4,128]{2,1,0:T(4,128)S(1)}, f32[8,4,128]{2,1,0:T(4,128)S(1)}, u32[]{:S(2)}, u32[]{:S(2)}) %collective-permute-start) | collective-permute-done | bytes 16416 | tf_op jit(solution)/shard_map/ppermute | solution.py:255
  12.6 0.0 collective-permute-start.3
  12.6 0.5 collective-permute-done.6.refs_7_
  13.1 0.0 collective-permute-done.5.refs_6_
  13.1 0.0 collective-permute-done.4.refs_5_
  13.1 0.7 %collective-permute-done.3.refs_4_ = f32[8,4,128]{2,1,0:T(4,128)S(1)} collective-permute-done((f32[8,4,128]{2,1,0:T(4,128)S(1)}, f32[8,4,128]{2,1,0:T(4,128)S(1)}, u32[]{:S(2)}, u32[]{:S(2)}) %collective-permute-start.3) | collective-permute-done | bytes 16416 | tf_op jit(solution)/shard_map/ppermute | solution.py:255
  13.8 0.0 copy-done.3
  13.9 0.6 %copy-done.11 = f32[8,4,128]{2,1,0:T(4,128)} copy-done((f32[8,4,128]{2,1,0:T(4,128)}, f32[8,4,128]{2,1,0:T(4,128)S(1)}, u32[]{:S(2)}) %copy-start.11) | copy-done | bytes 16408
  14.4 17.6 %shard_map.68 = (f32[3,256,128]{2,1,0:T(8,128)}, f32[4,1024]{1,0:T(4,128)}, f32[4,1024]{1,0:T(4,128)}, f32[4,1024]{1,0:T(4,128)}, f32[4,1024]{1,0:T(4,128)}, /*i...) custom-call(f32[8,4,128]{2,1,0:T(4,128)} %copy-done.1, f32[8,4,128]{2,1,0:T(4,128)} %copy-done.6, ...), custom_call_target="tpu_custom_call" | custom-call | tf_op jit(solution)/shard_map/pallas_call | solution.py:268
  32.1 0.2 collective-permute-start.8
  32.3 0.3 collective-permute-start.10
  32.6 0.2 collective-permute-start.12
  32.8 1.4 %collective-permute-start.7 = (f32[4,1024]{1,0:T(4,128)}, f32[4,1024]{1,0:T(4,128)S(1)}, u32[]{:S(2)}, u32[]{:S(2)}) collective-permute-start(f32[4,1024]{1,0:T(4,128)} %get-tuple-element.13), channel_id=1, source_target_pairs={{0,8},{1,9},{2,10},{3,11},{4,12},{5,13},{6,14},{7,15},{8,0},{9,1},... | collective-permute-start | bytes 49160 | tf_op jit(solution)/shard_map/ppermute | solution.py:255
  34.2 0.0 collective-permute-done.8
  34.2 0.7 %add.36 = f32[4,1024]{1,0:T(4,128)S(1)} add(f32[4,1024]{1,0:T(4,128)} %get-tuple-element.14, f32[4,1024]{1,0:T(4,128)S(1)} %collective-permute-done.8) | non-fusion elementwise | flops 4096 | bytes 49152 | tf_op jit(solution)/shard_map/add | solution.py:299
  35.0 1.3 %collective-permute-start.9 = (f32[4,1024]{1,0:T(4,128)S(1)}, f32[4,1024]{1,0:T(4,128)S(1)}, u32[]{:S(2)}, u32[]{:S(2)}) collective-permute-start(f32[4,1024]{1,0:T(4,128)S(1)} %add.36), channel_id=1, source_target_pairs={{0,12},{1,29},{2,14},{3,31},{4,8},{5,25},{6,10},{7,27},{8,4},{9,21... | collective-permute-start | bytes 49160 | tf_op jit(solution)/shard_map/ppermute | solution.py:255
  36.3 0.0 collective-permute-done.10
  36.3 0.0 copy-done.8
  36.3 0.5 %collective-permute-start.11 = (f32[4,1024]{1,0:T(4,128)S(1)}, f32[4,1024]{1,0:T(4,128)S(1)}, u32[]{:S(2)}, u32[]{:S(2)}) collective-permute-start(f32[4,1024]{1,0:T(4,128)S(1)} %add.38), channel_id=1, source_target_pairs={{0,16},{1,21},{2,18},{3,23},{4,20},{5,17},{6,22},{7,19},{8,24},{9,... | collective-permute-start | bytes 49160 | tf_op jit(solution)/shard_map/ppermute | solution.py:255
  36.8 0.0 collective-permute-done.12
  36.8 0.2 copy-done.4
  37.0 1.4 %collective-permute-start.13 = (f32[4,1024]{1,0:T(4,128)S(1)}, f32[4,1024]{1,0:T(4,128)S(1)}, u32[]{:S(2)}, u32[]{:S(2)}) collective-permute-start(f32[4,1024]{1,0:T(4,128)S(1)} %add.40), channel_id=1, source_target_pairs={{0,4},{1,25},{2,6},{3,27},{4,0},{5,29},{6,2},{7,31},{8,12},{9,17},... | collective-permute-start | bytes 49160 | tf_op jit(solution)/shard_map/ppermute | solution.py:255
  38.4 0.0 collective-permute-done.7
  38.5 1.2 %collective-permute-done.9 = f32[4,1024]{1,0:T(4,128)S(1)} collective-permute-done((f32[4,1024]{1,0:T(4,128)S(1)}, f32[4,1024]{1,0:T(4,128)S(1)}, u32[]{:S(2)}, u32[]{:S(2)}) %collective-permute-start.9) | collective-permute-done | bytes 16416 | tf_op jit(solution)/shard_map/ppermute | solution.py:255
  39.6 1.4 %collective-permute-done.11 = f32[4,1024]{1,0:T(4,128)S(1)} collective-permute-done((f32[4,1024]{1,0:T(4,128)S(1)}, f32[4,1024]{1,0:T(4,128)S(1)}, u32[]{:S(2)}, u32[]{:S(2)}) %collective-permute-start.11) | collective-permute-done | bytes 16416 | tf_op jit(solution)/shard_map/ppermute | solution.py:255
  41.0 0.0 collective-permute-done.13
  41.0 1.6 %collective-permute-start.14 = (f32[4,1024]{1,0:T(4,128)S(1)}, f32[4,1024]{1,0:T(4,128)S(1)}, u32[]{:S(2)}, u32[]{:S(2)}) collective-permute-start(f32[4,1024]{1,0:T(4,128)S(1)} %add_add_fusion), channel_id=1, source_target_pairs={{0,2},{1,3},{2,0},{3,1},{4,6},{5,7},{6,4},{7,5},{8,10},{9,11},{10,... | collective-permute-start | bytes 49160 | tf_op jit(solution)/shard_map/ppermute | solution.py:255
  42.6 2.2 %collective-permute-done.14 = f32[4,1024]{1,0:T(4,128)S(1)} collective-permute-done((f32[4,1024]{1,0:T(4,128)S(1)}, f32[4,1024]{1,0:T(4,128)S(1)}, u32[]{:S(2)}, u32[]{:S(2)}) %collective-permute-start.14) | collective-permute-done | bytes 16416 | tf_op jit(solution)/shard_map/ppermute | solution.py:255
  44.9 0.2 collective-permute-start.15
  45.0 1.1 %collective-permute-done.15 = f32[4,1024]{1,0:T(4,128)S(1)} collective-permute-done((f32[4,1024]{1,0:T(4,128)S(1)}, f32[4,1024]{1,0:T(4,128)S(1)}, u32[]{:S(2)}, u32[]{:S(2)}) %collective-permute-start.15) | collective-permute-done | bytes 16416 | tf_op jit(solution)/shard_map/ppermute | solution.py:255
  46.1 0.0 copy-done.2
  46.2 0.7 %stack.27 = f32[6,1024]{1,0:T(8,128)} concatenate(f32[1,1024]{1,0:T(1,128)S(1)} %get-tuple-element.28, f32[1,1024]{1,0:T(1,128)S(1)} %get-tuple-element.26, f32[1,1024]{1,0:T(1,128)S(1)} %get-tuple-element.27, f32[1,1024]{1,0:T(1,128)S(1)} %get-tuple-element.21, f32[1,1024]{1,0:T(1,128)S(1)} %get-tuple-element.20, f32[1,1024]{1,0:T(1,128)S(1)} %bitcast.10), dimensions={0} | concatenate | bytes 49152 | tf_op jit(solution)/shard_map/stack | solution.py:308
  (27 shorter events, 0.1 us)
Async XLA Ops:
  0.6 0.8 %copy-start.14 = (f32[1024]{0:T(1024)S(1)}, f32[1024]{0:T(1024)}, u32[]{:S(2)}) copy-start(f32[1024]{0:T(1024)} %param.7) | copy-start | bytes 12292
  1.4 0.7 %copy-start = (f32[2,1024]{1,0:T(2,128)S(1)}, f32[2,1024]{1,0:T(2,128)}, u32[]{:S(2)}) copy-start(f32[2,1024]{1,0:T(2,128)} %param.6) | copy-start | bytes 24580
  1.5 0.7 %copy-start.13 = (f32[1024]{0:T(1024)S(1)}, f32[1024]{0:T(1024)}, u32[]{:S(2)}) copy-start(f32[1024]{0:T(1024)} %param.8) | copy-start | bytes 12292
  2.2 11.6 %copy-start.1 = (f32[8,4,128]{2,1,0:T(4,128)}, f32[8,4,128]{2,1,0:T(4,128)S(1)}, u32[]{:S(2)}) copy-start(f32[8,4,128]{2,1,0:T(4,128)S(1)} %maximum_bitcast_fusion.refs_0_) | copy-start | bytes 49156
  2.2 7.6 %collective-permute-start.2 = (f32[8,4,128]{2,1,0:T(4,128)S(1)}, f32[8,4,128]{2,1,0:T(4,128)S(1)}, u32[]{:S(2)}, u32[]{:S(2)}) collective-permute-start(f32[8,4,128]{2,1,0:T(4,128)S(1)} %maximum_bitcast_fusion.refs_0_), channel_id=1, source_target_pairs={{0,4},{1,25},{2,6},{3,27},{4,0},{5,29},{6,2},{7,31},{8,12},{9,17},... | collective-permute-start | bytes 49160 | tf_op jit(solution)/shard_map/ppermute | solution.py:255
  5.2 5.2 %collective-permute-start.1 = (f32[8,4,128]{2,1,0:T(4,128)S(1)}, f32[8,4,128]{2,1,0:T(4,128)S(1)}, u32[]{:S(2)}, u32[]{:S(2)}) collective-permute-start(f32[8,4,128]{2,1,0:T(4,128)S(1)} %maximum_bitcast_fusion.refs_0_), channel_id=1, source_target_pairs={{0,16},{1,21},{2,18},{3,23},{4,20},{5,17},{6,22},{7,19},{8,24},{9,... | collective-permute-start | bytes 49160 | tf_op jit(solution)/shard_map/ppermute | solution.py:255
  7.8 4.8 %collective-permute-start = (f32[8,4,128]{2,1,0:T(4,128)S(1)}, f32[8,4,128]{2,1,0:T(4,128)S(1)}, u32[]{:S(2)}, u32[]{:S(2)}) collective-permute-start(f32[8,4,128]{2,1,0:T(4,128)S(1)} %maximum_bitcast_fusion.refs_0_), channel_id=1, source_target_pairs={{0,12},{1,29},{2,14},{3,31},{4,8},{5,25},{6,10},{7,27},{8,4},{9,21... | collective-permute-start | bytes 49160 | tf_op jit(solution)/shard_map/ppermute | solution.py:255
  9.3 3.7 %collective-permute-start.6 = (f32[8,4,128]{2,1,0:T(4,128)S(1)}, f32[8,4,128]{2,1,0:T(4,128)S(1)}, u32[]{:S(2)}, u32[]{:S(2)}) collective-permute-start(f32[8,4,128]{2,1,0:T(4,128)S(1)} %maximum_bitcast_fusion.refs_0_), channel_id=1, source_target_pairs={{0,8},{1,9},{2,10},{3,11},{4,12},{5,13},{6,14},{7,15},{8,0},{9,1},... | collective-permute-start | bytes 49160 | tf_op jit(solution)/shard_map/ppermute | solution.py:255
  9.8 4.0 %copy-start.3 = (f32[8,4,128]{2,1,0:T(4,128)}, f32[8,4,128]{2,1,0:T(4,128)S(1)}, u32[]{:S(2)}) copy-start(f32[8,4,128]{2,1,0:T(4,128)S(1)} %collective-permute-done.2.refs_3_) | copy-start | bytes 49156
  9.8 3.3 %collective-permute-start.5 = (f32[8,4,128]{2,1,0:T(4,128)S(1)}, f32[8,4,128]{2,1,0:T(4,128)S(1)}, u32[]{:S(2)}, u32[]{:S(2)}) collective-permute-start(f32[8,4,128]{2,1,0:T(4,128)S(1)} %collective-permute-done.2.refs_3_), channel_id=1, source_target_pairs={{0,1},{1,0},{2,3},{3,2},{4,5},{5,4},{6,7},{7,6},{8,9},{9,8},{10,11... | collective-permute-start | bytes 49160 | tf_op jit(solution)/shard_map/ppermute | solution.py:255
  10.4 3.4 %copy-start.5 = (f32[8,4,128]{2,1,0:T(4,128)}, f32[8,4,128]{2,1,0:T(4,128)S(1)}, u32[]{:S(2)}) copy-start(f32[8,4,128]{2,1,0:T(4,128)S(1)} %collective-permute-done.1.refs_2_) | copy-start | bytes 49156
  10.4 2.7 %collective-permute-start.4 = (f32[8,4,128]{2,1,0:T(4,128)S(1)}, f32[8,4,128]{2,1,0:T(4,128)S(1)}, u32[]{:S(2)}, u32[]{:S(2)}) collective-permute-start(f32[8,4,128]{2,1,0:T(4,128)S(1)} %collective-permute-done.1.refs_2_), channel_id=1, source_target_pairs={{0,1},{1,0},{2,3},{3,2},{4,5},{5,4},{6,7},{7,6},{8,9},{9,8},{10,11... | collective-permute-start | bytes 49160 | tf_op jit(solution)/shard_map/ppermute | solution.py:255
  12.6 1.2 %copy-start.6 = (f32[8,4,128]{2,1,0:T(4,128)}, f32[8,4,128]{2,1,0:T(4,128)S(1)}, u32[]{:S(2)}) copy-start(f32[8,4,128]{2,1,0:T(4,128)S(1)} %collective-permute-done.refs_1_) | copy-start | bytes 49156
  12.6 1.2 %collective-permute-start.3 = (f32[8,4,128]{2,1,0:T(4,128)S(1)}, f32[8,4,128]{2,1,0:T(4,128)S(1)}, u32[]{:S(2)}, u32[]{:S(2)}) collective-permute-start(f32[8,4,128]{2,1,0:T(4,128)S(1)} %collective-permute-done.refs_1_), channel_id=1, source_target_pairs={{0,1},{1,0},{2,3},{3,2},{4,5},{5,4},{6,7},{7,6},{8,9},{9,8},{10,11... | collective-permute-start | bytes 49160 | tf_op jit(solution)/shard_map/ppermute | solution.py:255
  13.1 0.8 %copy-start.7 = (f32[8,4,128]{2,1,0:T(4,128)}, f32[8,4,128]{2,1,0:T(4,128)S(1)}, u32[]{:S(2)}) copy-start(f32[8,4,128]{2,1,0:T(4,128)S(1)} %collective-permute-done.6.refs_7_) | copy-start | bytes 49156
  13.1 0.8 %copy-start.9 = (f32[8,4,128]{2,1,0:T(4,128)}, f32[8,4,128]{2,1,0:T(4,128)S(1)}, u32[]{:S(2)}) copy-start(f32[8,4,128]{2,1,0:T(4,128)S(1)} %collective-permute-done.5.refs_6_) | copy-start | bytes 49156
  13.1 0.8 %copy-start.10 = (f32[8,4,128]{2,1,0:T(4,128)}, f32[8,4,128]{2,1,0:T(4,128)S(1)}, u32[]{:S(2)}) copy-start(f32[8,4,128]{2,1,0:T(4,128)S(1)} %collective-permute-done.4.refs_5_) | copy-start | bytes 49156
  13.9 0.6 %copy-start.11 = (f32[8,4,128]{2,1,0:T(4,128)}, f32[8,4,128]{2,1,0:T(4,128)S(1)}, u32[]{:S(2)}) copy-start(f32[8,4,128]{2,1,0:T(4,128)S(1)} %collective-permute-done.3.refs_4_) | copy-start | bytes 49156
  32.1 2.2 %collective-permute-start.8 = (f32[4,1024]{1,0:T(4,128)}, f32[4,1024]{1,0:T(4,128)S(1)}, u32[]{:S(2)}, u32[]{:S(2)}) collective-permute-start(f32[4,1024]{1,0:T(4,128)} %get-tuple-element.15), channel_id=1, source_target_pairs={{0,1},{1,0},{2,3},{3,2},{4,5},{5,4},{6,7},{7,6},{8,9},{9,8},{10,11... | collective-permute-start | bytes 49160 | tf_op jit(solution)/shard_map/ppermute | solution.py:255
  32.3 4.0 %collective-permute-start.10 = (f32[4,1024]{1,0:T(4,128)}, f32[4,1024]{1,0:T(4,128)S(1)}, u32[]{:S(2)}, u32[]{:S(2)}) collective-permute-start(f32[4,1024]{1,0:T(4,128)} %get-tuple-element.17), channel_id=1, source_target_pairs={{0,1},{1,0},{2,3},{3,2},{4,5},{5,4},{6,7},{7,6},{8,9},{9,8},{10,11... | collective-permute-start | bytes 49160 | tf_op jit(solution)/shard_map/ppermute | solution.py:255
  32.6 4.2 %collective-permute-start.12 = (f32[4,1024]{1,0:T(4,128)}, f32[4,1024]{1,0:T(4,128)S(1)}, u32[]{:S(2)}, u32[]{:S(2)}) collective-permute-start(f32[4,1024]{1,0:T(4,128)} %get-tuple-element.19), channel_id=1, source_target_pairs={{0,1},{1,0},{2,3},{3,2},{4,5},{5,4},{6,7},{7,6},{8,9},{9,8},{10,11... | collective-permute-start | bytes 49160 | tf_op jit(solution)/shard_map/ppermute | solution.py:255
  32.8 5.6 %collective-permute-start.7 = (f32[4,1024]{1,0:T(4,128)}, f32[4,1024]{1,0:T(4,128)S(1)}, u32[]{:S(2)}, u32[]{:S(2)}) collective-permute-start(f32[4,1024]{1,0:T(4,128)} %get-tuple-element.13), channel_id=1, source_target_pairs={{0,8},{1,9},{2,10},{3,11},{4,12},{5,13},{6,14},{7,15},{8,0},{9,1},... | collective-permute-start | bytes 49160 | tf_op jit(solution)/shard_map/ppermute | solution.py:255
  34.2 2.1 %copy-start.8 = (f32[4,1024]{1,0:T(4,128)S(1)}, f32[4,1024]{1,0:T(4,128)}, u32[]{:S(2)}) copy-start(f32[4,1024]{1,0:T(4,128)} %get-tuple-element.16) | copy-start | bytes 49156
  35.0 4.6 %collective-permute-start.9 = (f32[4,1024]{1,0:T(4,128)S(1)}, f32[4,1024]{1,0:T(4,128)S(1)}, u32[]{:S(2)}, u32[]{:S(2)}) collective-permute-start(f32[4,1024]{1,0:T(4,128)S(1)} %add.36), channel_id=1, source_target_pairs={{0,12},{1,29},{2,14},{3,31},{4,8},{5,25},{6,10},{7,27},{8,4},{9,21... | collective-permute-start | bytes 49160 | tf_op jit(solution)/shard_map/ppermute | solution.py:255
  36.3 0.7 %copy-start.4 = (f32[4,1024]{1,0:T(4,128)S(1)}, f32[4,1024]{1,0:T(4,128)}, u32[]{:S(2)}) copy-start(f32[4,1024]{1,0:T(4,128)} %get-tuple-element.18) | copy-start | bytes 49156
  36.3 4.7 %collective-permute-start.11 = (f32[4,1024]{1,0:T(4,128)S(1)}, f32[4,1024]{1,0:T(4,128)S(1)}, u32[]{:S(2)}, u32[]{:S(2)}) collective-permute-start(f32[4,1024]{1,0:T(4,128)S(1)} %add.38), channel_id=1, source_target_pairs={{0,16},{1,21},{2,18},{3,23},{4,20},{5,17},{6,22},{7,19},{8,24},{9,... | collective-permute-start | bytes 49160 | tf_op jit(solution)/shard_map/ppermute | solution.py:255
  37.0 4.0 %copy-start.12 = (f32[4,1024]{1,0:T(4,128)S(1)}, f32[4,1024]{1,0:T(4,128)}, u32[]{:S(2)}) copy-start(f32[4,1024]{1,0:T(4,128)} %get-tuple-element.12) | copy-start | bytes 49156
  37.0 4.0 %collective-permute-start.13 = (f32[4,1024]{1,0:T(4,128)S(1)}, f32[4,1024]{1,0:T(4,128)S(1)}, u32[]{:S(2)}, u32[]{:S(2)}) collective-permute-start(f32[4,1024]{1,0:T(4,128)S(1)} %add.40), channel_id=1, source_target_pairs={{0,4},{1,25},{2,6},{3,27},{4,0},{5,29},{6,2},{7,31},{8,12},{9,17},... | collective-permute-start | bytes 49160 | tf_op jit(solution)/shard_map/ppermute | solution.py:255
  41.0 3.8 %collective-permute-start.14 = (f32[4,1024]{1,0:T(4,128)S(1)}, f32[4,1024]{1,0:T(4,128)S(1)}, u32[]{:S(2)}, u32[]{:S(2)}) collective-permute-start(f32[4,1024]{1,0:T(4,128)S(1)} %add_add_fusion), channel_id=1, source_target_pairs={{0,2},{1,3},{2,0},{3,1},{4,6},{5,7},{6,4},{7,5},{8,10},{9,11},{10,... | collective-permute-start | bytes 49160 | tf_op jit(solution)/shard_map/ppermute | solution.py:255
  44.8 1.3 %copy-start.2 = (f32[2,1024]{1,0:T(2,128)S(1)}, f32[2,1024]{1,0:T(2,128)}, u32[]{:S(2)}) copy-start(f32[2,1024]{1,0:T(2,128)} %param.5) | copy-start | bytes 24580
  44.9 1.2 %collective-permute-start.15 = (f32[4,1024]{1,0:T(4,128)S(1)}, f32[4,1024]{1,0:T(4,128)S(1)}, u32[]{:S(2)}, u32[]{:S(2)}) collective-permute-start(f32[4,1024]{1,0:T(4,128)S(1)} %add.42), channel_id=1, source_target_pairs={{0,1},{1,0},{2,3},{3,2},{4,5},{5,4},{6,7},{7,6},{8,9},{9,8},{10,11... | collective-permute-start | bytes 49160 | tf_op jit(solution)/shard_map/ppermute | solution.py:255

commit v5 on v4

--- a/solution.py
+++ b/solution.py
@@ -193,23 +193,31 @@
     psf_store = pltpu.make_async_copy(psf_s, psf_ref, psf_sem)
     psf_store.start()
 
-    sub = lax.broadcasted_iota(jnp.int32, (8, local), 0).astype(jnp.float32)
+    sub = lax.broadcasted_iota(jnp.int32, (8, 512), 0).astype(jnp.float32)
     y_sub = sub + (y_low + clen)
 
     @pl.loop(0, shards)
     def _(shard):
-        total = [jnp.zeros((8, local), jnp.float32) for _ in range(4)]
-        for wave in range(3):
+        jobs = [(piece, wave) for piece in range(local // 512) for wave in range(3)]
+
+        def dot(piece, wave):
+            return jnp.dot(cot[wave][...], row_tab[wave][shard, :, piece * 512 : (piece + 1) * 512], preferred_element_type=jnp.float32)
+
+        ready = [dot(*job) for job in jobs[:1]]
+        for number, (piece, wave) in enumerate(jobs):
+            span = slice(piece * 512, (piece + 1) * 512)
+            if wave == 0:
+                total = [jnp.zeros((8, 512), jnp.float32) for _ in range(4)]
             scale = 2.0 * wave_scales[wave]
-            back = jnp.dot(cot[wave][...], row_tab[wave][shard], preferred_element_type=jnp.float32)
-            im_sum = jnp.zeros((8, local), jnp.float32)
-            up_sum = jnp.zeros((8, local), jnp.float32)
-            re_sum = jnp.zeros((8, local), jnp.float32)
-            x_sum = jnp.zeros((8, local), jnp.float32)
+            if number + 1 < len(jobs):
+                ready.append(dot(*jobs[number + 1]))
+            back = ready[number]
+            ready[number] = None
+            im_sum = up_sum = re_sum = x_sum = jnp.zeros((8, 512), jnp.float32)
             for group in range(clen // 8):
                 e_r, e_i, f_r, f_i = [back[32 * group + 8 * n : 32 * group + 8 * n + 8] for n in range(4)]
-                b_r = col_tab[wave][shard, 8 * group : 8 * group + 8, :]
-                b_i = col_tab[wave][shard, clen + 8 * group : clen + 8 * group + 8, :]
+                b_r = col_tab[wave][shard, 8 * group : 8 * group + 8, span]
+                b_i = col_tab[wave][shard, clen + 8 * group : clen + 8 * group + 8, span]
                 im_sum = im_sum + (b_r * e_i - b_i * e_r)
                 re_sum = re_sum + (b_r * e_r + b_i * e_i)
                 x_sum = x_sum + (b_r * f_i - b_i * f_r)
@@ -218,8 +226,9 @@
             total[1] = total[1] + (scale * two_pi) * (x_mid * im_sum + x_sum)
             total[2] = total[2] + (scale * two_pi) * (y_sub * im_sum - 8.0 * up_sum)
             total[3] = total[3] + 2.0 * re_sum
-        rows = [jnp.sum(value, axis=0, keepdims=True) for value in total]
-        sums[shard] = jnp.concatenate(rows, axis=0)
+            if wave == 2:
+                rows = [jnp.sum(value, axis=0, keepdims=True) for value in total]
+                sums[shard, :, span] = jnp.concatenate(rows, axis=0)
 
     for slot in range(shards):
         sum_refs[slot][...] = sums[slot]

time: 47.4 us -> 47.4 us (level)
  no operation moved by 1% of the time
where the time goes in v5:
time: 47.4 us; the launch traced here: 46.8 us
  Pallas kernels  17.6 us (37%)
  starting transfers between devices  16.2 us (34%)
  waiting for transfers between devices  8.42 us (18%)
  local copies, waits for them, and re-layouts  2.15 us (5%)
  other arithmetic  1.63 us (3%)
  between operations  0.8 us (2%)
    pallas_call x1, Pallas kernels, on_device(): pl.pallas_call(functools.partial(psf_kernel, sizes), out_shape=[jax.Shape...  17.6 us
    ppermute x16, starting transfers between devices, swap(): return lax.ppermute(value, ('ray', 'pix'), moves)  16.2 us
    ppermute x16, waiting for transfers between devices, swap(): return lax.ppermute(value, ('ray', 'pix'), moves)  8.42 us
    unnamed x30, local copies, waits for them, and re-layouts  1.49 us
  transfers between devices with their start and end apart: 16, of which 7 were waited for; matrix products, arithmetic and copies ran while one was open for 2% of the time, Pallas kernels for 0%

profile of v5, /device:TPU:0, one launch (start us, length us, event | category | flops | bytes accessed | tf_op | source)
XLA Modules:
  0.0 46.8 jit_solution(2793153322230436703)
XLA Ops:
  0.6 0.0 copy-start.14
  0.6 0.8 %multiply_add_fusion = f32[1,1024]{1,0:T(1,128)S(1)} fusion(f32[2,1024]{1,0:T(2,128)} %param.5, f32[2,1024]{1,0:T(2,128)} %param.6), kind=kLoop, calls=%fused_computation.8 | loop fusion | flops 3072 | bytes 20480 | tf_op jit(solution)/shard_map/add | solution.py:266
  1.4 0.0 copy-done.14
  1.4 0.0 copy-start
  1.5 0.0 copy-start.13
  1.5 0.7 %copy-done = f32[2,1024]{1,0:T(2,128)S(1)} copy-done((f32[2,1024]{1,0:T(2,128)S(1)}, f32[2,1024]{1,0:T(2,128)}, u32[]{:S(2)}) %copy-start) | copy-done | bytes 8216
  2.1 0.0 copy-done.13
  2.2 0.0 copy-start.1
  2.2 3.0 %collective-permute-start.2 = (f32[8,4,128]{2,1,0:T(4,128)S(1)}, f32[8,4,128]{2,1,0:T(4,128)S(1)}, u32[]{:S(2)}, u32[]{:S(2)}) collective-permute-start(f32[8,4,128]{2,1,0:T(4,128)S(1)} %maximum_bitcast_fusion.refs_0_), channel_id=1, source_target_pairs={{0,4},{1,25},{2,6},{3,27},{4,0},{5,29},{6,2},{7,31},{8,12},{9,17},... | collective-permute-start | bytes 49160 | tf_op jit(solution)/shard_map/ppermute | solution.py:264
  5.2 2.6 %collective-permute-start.1 = (f32[8,4,128]{2,1,0:T(4,128)S(1)}, f32[8,4,128]{2,1,0:T(4,128)S(1)}, u32[]{:S(2)}, u32[]{:S(2)}) collective-permute-start(f32[8,4,128]{2,1,0:T(4,128)S(1)} %maximum_bitcast_fusion.refs_0_), channel_id=1, source_target_pairs={{0,16},{1,21},{2,18},{3,23},{4,20},{5,17},{6,22},{7,19},{8,24},{9,... | collective-permute-start | bytes 49160 | tf_op jit(solution)/shard_map/ppermute | solution.py:264
  7.8 1.5 %collective-permute-start = (f32[8,4,128]{2,1,0:T(4,128)S(1)}, f32[8,4,128]{2,1,0:T(4,128)S(1)}, u32[]{:S(2)}, u32[]{:S(2)}) collective-permute-start(f32[8,4,128]{2,1,0:T(4,128)S(1)} %maximum_bitcast_fusion.refs_0_), channel_id=1, source_target_pairs={{0,12},{1,29},{2,14},{3,31},{4,8},{5,25},{6,10},{7,27},{8,4},{9,21... | collective-permute-start | bytes 49160 | tf_op jit(solution)/shard_map/ppermute | solution.py:264
  9.3 0.4 collective-permute-start.6
  9.8 0.0 collective-permute-done.2.refs_3_
  9.8 0.6 %collective-permute-start.5 = (f32[8,4,128]{2,1,0:T(4,128)S(1)}, f32[8,4,128]{2,1,0:T(4,128)S(1)}, u32[]{:S(2)}, u32[]{:S(2)}) collective-permute-start(f32[8,4,128]{2,1,0:T(4,128)S(1)} %collective-permute-done.2.refs_3_), channel_id=1, source_target_pairs={{0,1},{1,0},{2,3},{3,2},{4,5},{5,4},{6,7},{7,6},{8,9},{9,8},{10,11... | collective-permute-start | bytes 49160 | tf_op jit(solution)/shard_map/ppermute | solution.py:264
  10.4 0.0 collective-permute-done.1.refs_2_
  10.4 0.8 %collective-permute-start.4 = (f32[8,4,128]{2,1,0:T(4,128)S(1)}, f32[8,4,128]{2,1,0:T(4,128)S(1)}, u32[]{:S(2)}, u32[]{:S(2)}) collective-permute-start(f32[8,4,128]{2,1,0:T(4,128)S(1)} %collective-permute-done.1.refs_2_), channel_id=1, source_target_pairs={{0,1},{1,0},{2,3},{3,2},{4,5},{5,4},{6,7},{7,6},{8,9},{9,8},{10,11... | collective-permute-start | bytes 49160 | tf_op jit(solution)/shard_map/ppermute | solution.py:264
  11.2 1.4 %collective-permute-done.refs_1_ = f32[8,4,128]{2,1,0:T(4,128)S(1)} collective-permute-done((f32[8,4,128]{2,1,0:T(4,128)S(1)}, f32[8,4,128]{2,1,0:T(4,128)S(1)}, u32[]{:S(2)}, u32[]{:S(2)}) %collective-permute-start) | collective-permute-done | bytes 16416 | tf_op jit(solution)/shard_map/ppermute | solution.py:264
  12.6 0.0 collective-permute-start.3
  12.6 0.5 collective-permute-done.6.refs_7_
  13.1 0.0 collective-permute-done.5.refs_6_
  13.1 0.0 collective-permute-done.4.refs_5_
  13.1 0.0 copy-start.10
  13.1 0.7 %collective-permute-done.3.refs_4_ = f32[8,4,128]{2,1,0:T(4,128)S(1)} collective-permute-done((f32[8,4,128]{2,1,0:T(4,128)S(1)}, f32[8,4,128]{2,1,0:T(4,128)S(1)}, u32[]{:S(2)}, u32[]{:S(2)}) %collective-permute-start.3) | collective-permute-done | bytes 16416 | tf_op jit(solution)/shard_map/ppermute | solution.py:264
  13.8 0.0 copy-done.3
  13.9 0.6 %copy-done.11 = f32[8,4,128]{2,1,0:T(4,128)} copy-done((f32[8,4,128]{2,1,0:T(4,128)}, f32[8,4,128]{2,1,0:T(4,128)S(1)}, u32[]{:S(2)}) %copy-start.11) | copy-done | bytes 16408
  14.4 17.6 %shard_map.68 = (f32[3,256,128]{2,1,0:T(8,128)}, f32[4,1024]{1,0:T(4,128)}, f32[4,1024]{1,0:T(4,128)}, f32[4,1024]{1,0:T(4,128)}, f32[4,1024]{1,0:T(4,128)}, /*i...) custom-call(f32[8,4,128]{2,1,0:T(4,128)} %copy-done.1, f32[8,4,128]{2,1,0:T(4,128)} %copy-done.6, ...), custom_call_target="tpu_custom_call" | custom-call | tf_op jit(solution)/shard_map/pallas_call | solution.py:277
  32.1 0.2 collective-permute-start.8
  32.3 0.3 collective-permute-start.10
  32.6 0.2 collective-permute-start.12
  32.8 1.4 %collective-permute-start.7 = (f32[4,1024]{1,0:T(4,128)}, f32[4,1024]{1,0:T(4,128)S(1)}, u32[]{:S(2)}, u32[]{:S(2)}) collective-permute-start(f32[4,1024]{1,0:T(4,128)} %get-tuple-element.13), channel_id=1, source_target_pairs={{0,8},{1,9},{2,10},{3,11},{4,12},{5,13},{6,14},{7,15},{8,0},{9,1},... | collective-permute-start | bytes 49160 | tf_op jit(solution)/shard_map/ppermute | solution.py:264
  34.2 0.0 collective-permute-done.8
  34.2 0.7 %add.36 = f32[4,1024]{1,0:T(4,128)S(1)} add(f32[4,1024]{1,0:T(4,128)} %get-tuple-element.14, f32[4,1024]{1,0:T(4,128)S(1)} %collective-permute-done.8) | non-fusion elementwise | flops 4096 | bytes 49152 | tf_op jit(solution)/shard_map/add | solution.py:308
  35.0 1.3 %collective-permute-start.9 = (f32[4,1024]{1,0:T(4,128)S(1)}, f32[4,1024]{1,0:T(4,128)S(1)}, u32[]{:S(2)}, u32[]{:S(2)}) collective-permute-start(f32[4,1024]{1,0:T(4,128)S(1)} %add.36), channel_id=1, source_target_pairs={{0,12},{1,29},{2,14},{3,31},{4,8},{5,25},{6,10},{7,27},{8,4},{9,21... | collective-permute-start | bytes 49160 | tf_op jit(solution)/shard_map/ppermute | solution.py:264
  36.3 0.0 collective-permute-done.10
  36.3 0.5 %collective-permute-start.11 = (f32[4,1024]{1,0:T(4,128)S(1)}, f32[4,1024]{1,0:T(4,128)S(1)}, u32[]{:S(2)}, u32[]{:S(2)}) collective-permute-start(f32[4,1024]{1,0:T(4,128)S(1)} %add.38), channel_id=1, source_target_pairs={{0,16},{1,21},{2,18},{3,23},{4,20},{5,17},{6,22},{7,19},{8,24},{9,... | collective-permute-start | bytes 49160 | tf_op jit(solution)/shard_map/ppermute | solution.py:264
  36.8 0.0 collective-permute-done.12
  36.8 0.2 copy-done.4
  37.0 1.4 %collective-permute-start.13 = (f32[4,1024]{1,0:T(4,128)S(1)}, f32[4,1024]{1,0:T(4,128)S(1)}, u32[]{:S(2)}, u32[]{:S(2)}) collective-permute-start(f32[4,1024]{1,0:T(4,128)S(1)} %add.40), channel_id=1, source_target_pairs={{0,4},{1,25},{2,6},{3,27},{4,0},{5,29},{6,2},{7,31},{8,12},{9,17},... | collective-permute-start | bytes 49160 | tf_op jit(solution)/shard_map/ppermute | solution.py:264
  38.4 0.0 collective-permute-done.7
  38.4 1.2 %collective-permute-done.9 = f32[4,1024]{1,0:T(4,128)S(1)} collective-permute-done((f32[4,1024]{1,0:T(4,128)S(1)}, f32[4,1024]{1,0:T(4,128)S(1)}, u32[]{:S(2)}, u32[]{:S(2)}) %collective-permute-start.9) | collective-permute-done | bytes 16416 | tf_op jit(solution)/shard_map/ppermute | solution.py:264
  39.6 1.4 %collective-permute-done.11 = f32[4,1024]{1,0:T(4,128)S(1)} collective-permute-done((f32[4,1024]{1,0:T(4,128)S(1)}, f32[4,1024]{1,0:T(4,128)S(1)}, u32[]{:S(2)}, u32[]{:S(2)}) %collective-permute-start.11) | collective-permute-done | bytes 16416 | tf_op jit(solution)/shard_map/ppermute | solution.py:264
  41.0 0.0 collective-permute-done.13
  41.0 0.0 copy-done.12
  41.0 1.6 %collective-permute-start.14 = (f32[4,1024]{1,0:T(4,128)S(1)}, f32[4,1024]{1,0:T(4,128)S(1)}, u32[]{:S(2)}, u32[]{:S(2)}) collective-permute-start(f32[4,1024]{1,0:T(4,128)S(1)} %add_add_fusion), channel_id=1, source_target_pairs={{0,2},{1,3},{2,0},{3,1},{4,6},{5,7},{6,4},{7,5},{8,10},{9,11},{10,... | collective-permute-start | bytes 49160 | tf_op jit(solution)/shard_map/ppermute | solution.py:264
  42.6 2.2 %collective-permute-done.14 = f32[4,1024]{1,0:T(4,128)S(1)} collective-permute-done((f32[4,1024]{1,0:T(4,128)S(1)}, f32[4,1024]{1,0:T(4,128)S(1)}, u32[]{:S(2)}, u32[]{:S(2)}) %collective-permute-start.14) | collective-permute-done | bytes 16416 | tf_op jit(solution)/shard_map/ppermute | solution.py:264
  44.8 0.2 collective-permute-start.15
  45.0 1.1 %collective-permute-done.15 = f32[4,1024]{1,0:T(4,128)S(1)} collective-permute-done((f32[4,1024]{1,0:T(4,128)S(1)}, f32[4,1024]{1,0:T(4,128)S(1)}, u32[]{:S(2)}, u32[]{:S(2)}) %collective-permute-start.15) | collective-permute-done | bytes 16416 | tf_op jit(solution)/shard_map/ppermute | solution.py:264
  46.2 0.7 %stack.27 = f32[6,1024]{1,0:T(8,128)} concatenate(f32[1,1024]{1,0:T(1,128)S(1)} %get-tuple-element.28, f32[1,1024]{1,0:T(1,128)S(1)} %get-tuple-element.26, f32[1,1024]{1,0:T(1,128)S(1)} %get-tuple-element.27, f32[1,1024]{1,0:T(1,128)S(1)} %get-tuple-element.21, f32[1,1024]{1,0:T(1,128)S(1)} %get-tuple-element.20, f32[1,1024]{1,0:T(1,128)S(1)} %bitcast.10), dimensions={0} | concatenate | bytes 49152 | tf_op jit(solution)/shard_map/stack | solution.py:317
  (27 shorter events, 0.1 us)
Async XLA Ops:
  0.6 0.8 %copy-start.14 = (f32[1024]{0:T(1024)S(1)}, f32[1024]{0:T(1024)}, u32[]{:S(2)}) copy-start(f32[1024]{0:T(1024)} %param.7) | copy-start | bytes 12292
  1.4 0.7 %copy-start = (f32[2,1024]{1,0:T(2,128)S(1)}, f32[2,1024]{1,0:T(2,128)}, u32[]{:S(2)}) copy-start(f32[2,1024]{1,0:T(2,128)} %param.6) | copy-start | bytes 24580
  1.5 0.7 %copy-start.13 = (f32[1024]{0:T(1024)S(1)}, f32[1024]{0:T(1024)}, u32[]{:S(2)}) copy-start(f32[1024]{0:T(1024)} %param.8) | copy-start | bytes 12292
  2.2 11.6 %copy-start.1 = (f32[8,4,128]{2,1,0:T(4,128)}, f32[8,4,128]{2,1,0:T(4,128)S(1)}, u32[]{:S(2)}) copy-start(f32[8,4,128]{2,1,0:T(4,128)S(1)} %maximum_bitcast_fusion.refs_0_) | copy-start | bytes 49156
  2.2 7.6 %collective-permute-start.2 = (f32[8,4,128]{2,1,0:T(4,128)S(1)}, f32[8,4,128]{2,1,0:T(4,128)S(1)}, u32[]{:S(2)}, u32[]{:S(2)}) collective-permute-start(f32[8,4,128]{2,1,0:T(4,128)S(1)} %maximum_bitcast_fusion.refs_0_), channel_id=1, source_target_pairs={{0,4},{1,25},{2,6},{3,27},{4,0},{5,29},{6,2},{7,31},{8,12},{9,17},... | collective-permute-start | bytes 49160 | tf_op jit(solution)/shard_map/ppermute | solution.py:264
  5.2 5.2 %collective-permute-start.1 = (f32[8,4,128]{2,1,0:T(4,128)S(1)}, f32[8,4,128]{2,1,0:T(4,128)S(1)}, u32[]{:S(2)}, u32[]{:S(2)}) collective-permute-start(f32[8,4,128]{2,1,0:T(4,128)S(1)} %maximum_bitcast_fusion.refs_0_), channel_id=1, source_target_pairs={{0,16},{1,21},{2,18},{3,23},{4,20},{5,17},{6,22},{7,19},{8,24},{9,... | collective-permute-start | bytes 49160 | tf_op jit(solution)/shard_map/ppermute | solution.py:264
  7.8 4.8 %collective-permute-start = (f32[8,4,128]{2,1,0:T(4,128)S(1)}, f32[8,4,128]{2,1,0:T(4,128)S(1)}, u32[]{:S(2)}, u32[]{:S(2)}) collective-permute-start(f32[8,4,128]{2,1,0:T(4,128)S(1)} %maximum_bitcast_fusion.refs_0_), channel_id=1, source_target_pairs={{0,12},{1,29},{2,14},{3,31},{4,8},{5,25},{6,10},{7,27},{8,4},{9,21... | collective-permute-start | bytes 49160 | tf_op jit(solution)/shard_map/ppermute | solution.py:264
  9.3 3.7 %collective-permute-start.6 = (f32[8,4,128]{2,1,0:T(4,128)S(1)}, f32[8,4,128]{2,1,0:T(4,128)S(1)}, u32[]{:S(2)}, u32[]{:S(2)}) collective-permute-start(f32[8,4,128]{2,1,0:T(4,128)S(1)} %maximum_bitcast_fusion.refs_0_), channel_id=1, source_target_pairs={{0,8},{1,9},{2,10},{3,11},{4,12},{5,13},{6,14},{7,15},{8,0},{9,1},... | collective-permute-start | bytes 49160 | tf_op jit(solution)/shard_map/ppermute | solution.py:264
  9.8 4.0 %copy-start.3 = (f32[8,4,128]{2,1,0:T(4,128)}, f32[8,4,128]{2,1,0:T(4,128)S(1)}, u32[]{:S(2)}) copy-start(f32[8,4,128]{2,1,0:T(4,128)S(1)} %collective-permute-done.2.refs_3_) | copy-start | bytes 49156
  9.8 3.3 %collective-permute-start.5 = (f32[8,4,128]{2,1,0:T(4,128)S(1)}, f32[8,4,128]{2,1,0:T(4,128)S(1)}, u32[]{:S(2)}, u32[]{:S(2)}) collective-permute-start(f32[8,4,128]{2,1,0:T(4,128)S(1)} %collective-permute-done.2.refs_3_), channel_id=1, source_target_pairs={{0,1},{1,0},{2,3},{3,2},{4,5},{5,4},{6,7},{7,6},{8,9},{9,8},{10,11... | collective-permute-start | bytes 49160 | tf_op jit(solution)/shard_map/ppermute | solution.py:264
  10.4 3.4 %copy-start.5 = (f32[8,4,128]{2,1,0:T(4,128)}, f32[8,4,128]{2,1,0:T(4,128)S(1)}, u32[]{:S(2)}) copy-start(f32[8,4,128]{2,1,0:T(4,128)S(1)} %collective-permute-done.1.refs_2_) | copy-start | bytes 49156
  10.4 2.7 %collective-permute-start.4 = (f32[8,4,128]{2,1,0:T(4,128)S(1)}, f32[8,4,128]{2,1,0:T(4,128)S(1)}, u32[]{:S(2)}, u32[]{:S(2)}) collective-permute-start(f32[8,4,128]{2,1,0:T(4,128)S(1)} %collective-permute-done.1.refs_2_), channel_id=1, source_target_pairs={{0,1},{1,0},{2,3},{3,2},{4,5},{5,4},{6,7},{7,6},{8,9},{9,8},{10,11... | collective-permute-start | bytes 49160 | tf_op jit(solution)/shard_map/ppermute | solution.py:264
  12.6 1.2 %copy-start.6 = (f32[8,4,128]{2,1,0:T(4,128)}, f32[8,4,128]{2,1,0:T(4,128)S(1)}, u32[]{:S(2)}) copy-start(f32[8,4,128]{2,1,0:T(4,128)S(1)} %collective-permute-done.refs_1_) | copy-start | bytes 49156
  12.6 1.2 %collective-permute-start.3 = (f32[8,4,128]{2,1,0:T(4,128)S(1)}, f32[8,4,128]{2,1,0:T(4,128)S(1)}, u32[]{:S(2)}, u32[]{:S(2)}) collective-permute-start(f32[8,4,128]{2,1,0:T(4,128)S(1)} %collective-permute-done.refs_1_), channel_id=1, source_target_pairs={{0,1},{1,0},{2,3},{3,2},{4,5},{5,4},{6,7},{7,6},{8,9},{9,8},{10,11... | collective-permute-start | bytes 49160 | tf_op jit(solution)/shard_map/ppermute | solution.py:264
  13.1 0.8 %copy-start.7 = (f32[8,4,128]{2,1,0:T(4,128)}, f32[8,4,128]{2,1,0:T(4,128)S(1)}, u32[]{:S(2)}) copy-start(f32[8,4,128]{2,1,0:T(4,128)S(1)} %collective-permute-done.6.refs_7_) | copy-start | bytes 49156
  13.1 0.8 %copy-start.9 = (f32[8,4,128]{2,1,0:T(4,128)}, f32[8,4,128]{2,1,0:T(4,128)S(1)}, u32[]{:S(2)}) copy-start(f32[8,4,128]{2,1,0:T(4,128)S(1)} %collective-permute-done.5.refs_6_) | copy-start | bytes 49156
  13.1 0.8 %copy-start.10 = (f32[8,4,128]{2,1,0:T(4,128)}, f32[8,4,128]{2,1,0:T(4,128)S(1)}, u32[]{:S(2)}) copy-start(f32[8,4,128]{2,1,0:T(4,128)S(1)} %collective-permute-done.4.refs_5_) | copy-start | bytes 49156
  13.9 0.6 %copy-start.11 = (f32[8,4,128]{2,1,0:T(4,128)}, f32[8,4,128]{2,1,0:T(4,128)S(1)}, u32[]{:S(2)}) copy-start(f32[8,4,128]{2,1,0:T(4,128)S(1)} %collective-permute-done.3.refs_4_) | copy-start | bytes 49156
  32.1 2.2 %collective-permute-start.8 = (f32[4,1024]{1,0:T(4,128)}, f32[4,1024]{1,0:T(4,128)S(1)}, u32[]{:S(2)}, u32[]{:S(2)}) collective-permute-start(f32[4,1024]{1,0:T(4,128)} %get-tuple-element.15), channel_id=1, source_target_pairs={{0,1},{1,0},{2,3},{3,2},{4,5},{5,4},{6,7},{7,6},{8,9},{9,8},{10,11... | collective-permute-start | bytes 49160 | tf_op jit(solution)/shard_map/ppermute | solution.py:264
  32.3 4.0 %collective-permute-start.10 = (f32[4,1024]{1,0:T(4,128)}, f32[4,1024]{1,0:T(4,128)S(1)}, u32[]{:S(2)}, u32[]{:S(2)}) collective-permute-start(f32[4,1024]{1,0:T(4,128)} %get-tuple-element.17), channel_id=1, source_target_pairs={{0,1},{1,0},{2,3},{3,2},{4,5},{5,4},{6,7},{7,6},{8,9},{9,8},{10,11... | collective-permute-start | bytes 49160 | tf_op jit(solution)/shard_map/ppermute | solution.py:264
  32.6 4.2 %collective-permute-start.12 = (f32[4,1024]{1,0:T(4,128)}, f32[4,1024]{1,0:T(4,128)S(1)}, u32[]{:S(2)}, u32[]{:S(2)}) collective-permute-start(f32[4,1024]{1,0:T(4,128)} %get-tuple-element.19), channel_id=1, source_target_pairs={{0,1},{1,0},{2,3},{3,2},{4,5},{5,4},{6,7},{7,6},{8,9},{9,8},{10,11... | collective-permute-start | bytes 49160 | tf_op jit(solution)/shard_map/ppermute | solution.py:264
  32.8 5.6 %collective-permute-start.7 = (f32[4,1024]{1,0:T(4,128)}, f32[4,1024]{1,0:T(4,128)S(1)}, u32[]{:S(2)}, u32[]{:S(2)}) collective-permute-start(f32[4,1024]{1,0:T(4,128)} %get-tuple-element.13), channel_id=1, source_target_pairs={{0,8},{1,9},{2,10},{3,11},{4,12},{5,13},{6,14},{7,15},{8,0},{9,1},... | collective-permute-start | bytes 49160 | tf_op jit(solution)/shard_map/ppermute | solution.py:264
  34.2 2.1 %copy-start.8 = (f32[4,1024]{1,0:T(4,128)S(1)}, f32[4,1024]{1,0:T(4,128)}, u32[]{:S(2)}) copy-start(f32[4,1024]{1,0:T(4,128)} %get-tuple-element.16) | copy-start | bytes 49156
  35.0 4.6 %collective-permute-start.9 = (f32[4,1024]{1,0:T(4,128)S(1)}, f32[4,1024]{1,0:T(4,128)S(1)}, u32[]{:S(2)}, u32[]{:S(2)}) collective-permute-start(f32[4,1024]{1,0:T(4,128)S(1)} %add.36), channel_id=1, source_target_pairs={{0,12},{1,29},{2,14},{3,31},{4,8},{5,25},{6,10},{7,27},{8,4},{9,21... | collective-permute-start | bytes 49160 | tf_op jit(solution)/shard_map/ppermute | solution.py:264
  36.3 0.7 %copy-start.4 = (f32[4,1024]{1,0:T(4,128)S(1)}, f32[4,1024]{1,0:T(4,128)}, u32[]{:S(2)}) copy-start(f32[4,1024]{1,0:T(4,128)} %get-tuple-element.18) | copy-start | bytes 49156
  36.3 4.7 %collective-permute-start.11 = (f32[4,1024]{1,0:T(4,128)S(1)}, f32[4,1024]{1,0:T(4,128)S(1)}, u32[]{:S(2)}, u32[]{:S(2)}) collective-permute-start(f32[4,1024]{1,0:T(4,128)S(1)} %add.38), channel_id=1, source_target_pairs={{0,16},{1,21},{2,18},{3,23},{4,20},{5,17},{6,22},{7,19},{8,24},{9,... | collective-permute-start | bytes 49160 | tf_op jit(solution)/shard_map/ppermute | solution.py:264
  37.0 4.0 %copy-start.12 = (f32[4,1024]{1,0:T(4,128)S(1)}, f32[4,1024]{1,0:T(4,128)}, u32[]{:S(2)}) copy-start(f32[4,1024]{1,0:T(4,128)} %get-tuple-element.12) | copy-start | bytes 49156
  37.0 4.0 %collective-permute-start.13 = (f32[4,1024]{1,0:T(4,128)S(1)}, f32[4,1024]{1,0:T(4,128)S(1)}, u32[]{:S(2)}, u32[]{:S(2)}) collective-permute-start(f32[4,1024]{1,0:T(4,128)S(1)} %add.40), channel_id=1, source_target_pairs={{0,4},{1,25},{2,6},{3,27},{4,0},{5,29},{6,2},{7,31},{8,12},{9,17},... | collective-permute-start | bytes 49160 | tf_op jit(solution)/shard_map/ppermute | solution.py:264
  41.0 3.8 %collective-permute-start.14 = (f32[4,1024]{1,0:T(4,128)S(1)}, f32[4,1024]{1,0:T(4,128)S(1)}, u32[]{:S(2)}, u32[]{:S(2)}) collective-permute-start(f32[4,1024]{1,0:T(4,128)S(1)} %add_add_fusion), channel_id=1, source_target_pairs={{0,2},{1,3},{2,0},{3,1},{4,6},{5,7},{6,4},{7,5},{8,10},{9,11},{10,... | collective-permute-start | bytes 49160 | tf_op jit(solution)/shard_map/ppermute | solution.py:264
  44.8 1.3 %copy-start.2 = (f32[2,1024]{1,0:T(2,128)S(1)}, f32[2,1024]{1,0:T(2,128)}, u32[]{:S(2)}) copy-start(f32[2,1024]{1,0:T(2,128)} %param.5) | copy-start | bytes 24580
  44.8 1.2 %collective-permute-start.15 = (f32[4,1024]{1,0:T(4,128)S(1)}, f32[4,1024]{1,0:T(4,128)S(1)}, u32[]{:S(2)}, u32[]{:S(2)}) collective-permute-start(f32[4,1024]{1,0:T(4,128)S(1)} %add.42), channel_id=1, source_target_pairs={{0,1},{1,0},{2,3},{3,2},{4,5},{5,4},{6,7},{7,6},{8,9},{9,8},{10,11... | collective-permute-start | bytes 49160 | tf_op jit(solution)/shard_map/ppermute | solution.py:264
